TPU v7x, 512 devices: a whole 4x8x8 slice. The times are simulated.
512 devices in a mesh: group: 16 (over y, core), dev: 32 (over z, x).
Axes of the slice: x: 4, y: 8, z: 8, core: 2. Of those that a mesh axis runs over, the one named last changes fastest.
Arguments:
- direction: float32 [524288], P(('group', 'dev')), may hold values from -6 to 6
- krylov: float32 [8, 524288], P(None, ('group', 'dev')), may hold values from -0.0078125 to 0.0078125
- bases: bfloat16 [2048, 32, 256], P(('group', 'dev')), may hold values from -0.375 to 0.375
- near_tiles: bfloat16 [6144, 256, 256], P(('group', 'dev')), may hold values from -0.15625 to 0.15625
- near_pairs: int32 [6144, 2], P(('group', 'dev')), may hold values from 0 to 127
- near_mask: int32 [6144], P(('group', 'dev')), may hold values 0 or 1
- far_blocks: bfloat16 [32768, 1024], P(('group', 'dev')), may hold values from -0.1875 to 0.1875
- far_pairs: int32 [32768, 2], P(('group', 'dev')), may hold values from 0 to 2047, as said below
- far_mask: int32 [32768], P(('group', 'dev')), may hold values 0 or 1
Outputs:
- next_vector: float32 [524288], P(('group', 'dev'))
- projections: float32 [8], replicated
Inputs may be any that keep to these rules, and one draw needn't show every extreme that they name: `far_pairs`: the first cluster of far slot s lies in the group of the device that owns the slot; the second lies in that group or in one of the two groups next to it along the group axis, counted cyclically.
All inputs are finite; a program needn't handle non-finite values. No bound on the sum of `near_mask` or of `far_mask` on one device may be relied on, other than what follows from the above.
Results may differ from a plain program's by a relative error of at most 0.0047.
Values may be sent and summed in bfloat16 or wider, within the bound.
No kernel may reach another device: no remote copies, remote signals or barrier semaphores. Data moves between devices by JAX's collectives and lax.ppermute only.
A program may use at most 64 MiB of HBM per device.

v0:
```python
import jax
import jax.numpy as jnp
from jax import lax
from jax.sharding import PartitionSpec as P


def extended(block, sides, width):
    for axis, dim in sides:
        count = lax.axis_size(axis)
        forward = [(i, i + 1) for i in range(count - 1)]
        forward.append((count - 1, 0))
        backward = [(target, source) for source, target in forward]
        low = lax.ppermute(
            lax.slice_in_dim(block, block.shape[dim] - width, None, axis=dim), axis, forward
        )
        high = lax.ppermute(lax.slice_in_dim(block, 0, width, axis=dim), axis, backward)
        block = jnp.concatenate([low, block, high], axis=dim)
    return block


def passed_along(value, axis, steps):
    count = lax.axis_size(axis)
    pairs = [(source, (source + steps) % count) for source in range(count)]
    return lax.ppermute(value, axis, pairs)


def spread_rows(left_ids, right_ids, forward, backward, width):
    targets = jnp.arange(width, dtype=jnp.int32)
    pick_left = (left_ids[:, None] == targets[None, :]).astype(jnp.float32)
    pick_right = (right_ids[:, None] == targets[None, :]).astype(jnp.float32)
    summed = jnp.dot(pick_left.T, forward, precision=lax.Precision.HIGHEST)
    return summed + jnp.dot(pick_right.T, backward, precision=lax.Precision.HIGHEST)


def local(
    direction, krylov, bases, near_tiles, near_pairs, near_mask, far_blocks, far_pairs, far_mask
):
    leaves = bases.shape[0]
    rank_size = bases.shape[1]
    leaf_size = bases.shape[2]
    panels_bf = direction.astype(jnp.bfloat16).reshape(leaves, leaf_size)
    group_panels = lax.all_gather(panels_bf, "dev", axis=0, tiled=True)
    left_ids = near_pairs[:, 0]
    right_ids = near_pairs[:, 1]
    forward = jnp.einsum(
        "spq,sq->sp", near_tiles, group_panels[right_ids], preferred_element_type=jnp.float32
    )
    backward = jnp.einsum(
        "spq,sp->sq", near_tiles, group_panels[left_ids], preferred_element_type=jnp.float32
    )
    live_slots = near_mask.astype(jnp.float32)
    forward = forward * live_slots[:, None]
    backward = backward * (live_slots * (left_ids != right_ids).astype(jnp.float32))[:, None]
    near_partial = spread_rows(left_ids, right_ids, forward, backward, group_panels.shape[0])
    near_part = lax.psum_scatter(near_partial, "dev", scatter_dimension=0, tiled=True)
    coeffs = jnp.einsum("crp,cp->cr", bases, panels_bf, preferred_element_type=jnp.float32).astype(
        jnp.bfloat16
    )
    group_coeffs = lax.all_gather(coeffs, "dev", axis=0, tiled=True)
    group_width = group_coeffs.shape[0]
    widened = extended(group_coeffs, (("group", 0),), group_width)
    group_here = lax.axis_index("group")
    group_count = lax.axis_size("group")

    def local_number(global_ids):
        step_over = (global_ids // group_width - group_here + group_count) % group_count
        block = jnp.where(step_over == 0, 1, jnp.where(step_over == 1, 2, 0)).astype(jnp.int32)
        return block * group_width + global_ids % group_width

    blocks = far_blocks.reshape(-1, rank_size, rank_size)
    far_left = local_number(far_pairs[:, 0])
    far_right = local_number(far_pairs[:, 1])
    far_forward = jnp.einsum(
        "srq,sq->sr", blocks, widened[far_right], preferred_element_type=jnp.float32
    )
    far_backward = jnp.einsum(
        "srq,sr->sq", blocks, widened[far_left], preferred_element_type=jnp.float32
    )
    far_live = far_mask.astype(jnp.float32)
    far_forward = far_forward * far_live[:, None]
    far_backward = far_backward * (far_live * (far_left != far_right).astype(jnp.float32))[:, None]
    far_partial = spread_rows(far_left, far_right, far_forward, far_backward, 3 * group_width)
    three_blocks = far_partial.reshape(3, group_width, rank_size)
    from_before = passed_along(three_blocks[2], "group", 1)
    from_after = passed_along(three_blocks[0], "group", -1)
    group_total = three_blocks[1] + from_before + from_after
    far_coef = lax.psum_scatter(group_total, "dev", scatter_dimension=0, tiled=True)
    far_part = jnp.einsum(
        "crp,cr->cp", bases, far_coef.astype(jnp.bfloat16), preferred_element_type=jnp.float32
    )
    product = (near_part + far_part).reshape(-1)
    local_proj = jnp.dot(krylov, product, precision=lax.Precision.HIGHEST)
    projections = lax.psum(local_proj, ("group", "dev"))
    remainder = product - jnp.dot(projections, krylov, precision=lax.Precision.HIGHEST)
    length_sq = lax.psum(jnp.sum(remainder * remainder), ("group", "dev"))
    panel_count = lax.axis_size(("group", "dev")) * product.shape[0]
    root_mean = jnp.sqrt(length_sq / panel_count)
    return (remainder / root_mean, projections)


def solution(mesh):
    in_specs = (
        P(("group", "dev")),
        P(None, ("group", "dev")),
        P(("group", "dev"), None, None),
        P(("group", "dev"), None, None),
        P(("group", "dev"), None),
        P(("group", "dev")),
        P(("group", "dev"), None),
        P(("group", "dev"), None),
        P(("group", "dev")),
    )
    out_specs = (P(("group", "dev")), P())
    return jax.shard_map(local, mesh=mesh, in_specs=in_specs, out_specs=out_specs, check_vma=False)
```

profile of v0, /device:TPU:1, one launch (start us, length us, event | category | flops | bytes accessed | tf_op | source)
XLA Modules:
  0.0 466.6 jit_solution(766201390838690261)
XLA Ops:
  7.2 0.0 copy-start
  7.2 0.0 all-reduce.4.cloned.1.call-start
  7.2 0.8 convert_element_type.10
  8.0 1.0 fusion.47
  9.0 39.7 %all-gather.1 = bf16[32,4,32]{2,1,0:T(4,128)(2,1)S(1)} all-gather(bf16[1,4,32]{2,1,0:T(4,128)(2,1)S(1)} %convert_bitcast_fusion), channel_id=1, replica_groups=mesh['group'=16,'dev'=32] {'dev'}, dimensions={0}, use_global_device_ids=true | all-gather | bytes 8448 | tf_op jit(solution)/shard_map/all_gather | solution.py:59
  48.7 10.8 %collective-permute-start.1 = (bf16[128,32]{1,0:T(8,128)(2,1)S(1)}, bf16[128,32]{1,0:T(8,128)(2,1)S(1)}, u32[]{:S(2)}, u32[]{:S(2)}) collective-permute-start(bf16[128,32]{1,0:T(8,128)(2,1)S(1)} %bitcast.101), channel_id=1, source_target_pairs={{32,0},{64,32},{96,64},{128,96},{160,128},{192,160},{224,192},{256... | collective-permute-start | bytes 24584 | tf_op jit(solution)/shard_map/ppermute | solution.py:16
  59.5 1.2 collective-permute-start
  60.7 0.8 slice_bitcast_fusion
  61.4 0.7 convert_element_type.22
  62.1 0.8 compare_select_fusion.21
  62.9 0.8 fusion.38
  63.6 0.8 compare_select_fusion.12
  64.4 35.6 %all-gather = bf16[32,4,256]{2,1,0:T(4,128)(2,1)S(1)} all-gather(bf16[1,4,256]{2,1,0:T(4,128)(2,1)S(1)} %reshape.59), channel_id=1, replica_groups=mesh['group'=16,'dev'=32] {'dev'}, dimensions={0}, use_global_device_ids=true | all-gather | bytes 67584 | tf_op jit(solution)/shard_map/all_gather | solution.py:42
  100.1 0.6 gather_fusion
  100.7 0.6 gather_fusion.1
  101.3 0.0 copy-start.5
  101.3 0.0 copy-start.1
  101.3 0.5 fusion.17
  101.8 0.3 fusion.15
  102.1 0.3 fusion.10
  102.5 0.2 copy.18
  102.7 0.8 copy.29
  103.5 0.0 copy-start.3
  103.5 0.0 copy-start.2
  103.5 0.0 collective-permute-done.1
  103.6 0.6 gather_fusion.2
  104.2 0.6 gather_fusion.3
  104.8 0.4 fusion.5
  105.2 0.3 fusion.3
  105.5 0.3 fusion
  105.8 0.3 convolution_add_fusion.1
  106.1 11.6 %collective-permute-start.3 = (f32[128,32]{0,1:T(8,128)S(1)}, f32[128,32]{0,1:T(8,128)S(1)}, u32[]{:S(2)}, u32[]{:S(2)}) collective-permute-start(f32[128,32]{0,1:T(8,128)S(1)} %get-tuple-element.11), channel_id=1, source_target_pairs={{0,480},{32,0},{64,32},{96,64},{128,96},{160,128},{192,160},{224,1... | collective-permute-start | bytes 49160 | tf_op jit(solution)/shard_map/ppermute | solution.py:24
  117.7 1.2 collective-permute-start.2
  118.9 1.0 convolution_add_fusion
  119.9 0.0 all-reduce.4.cloned.1.call-update
  119.9 1.3 dynamic-slice
  121.8 112.6 %all-reduce.1 = bf16[128,32]{0,1:T(8,128)(2,1)S(1)} all-reduce(f32[128,32]{0,1:T(8,128)S(1)} %fusion.9), channel_id=3, replica_groups=mesh['group'=16,'dev'=32] {'dev'}, use_global_device_ids=true, to_apply=%region_1.2.clone | all-reduce | flops 4096 | bytes 24576
  234.5 0.1 fusion.19
  234.5 0.1 copy.31
  234.6 0.1 fusion.48
  234.8 28.0 %all-reduce.4.cloned.1.call-done = f32[128,256]{1,0:T(8,128)} async-done(((f32[128,256]{1,0:T(8,128)}), f32[128,256]{1,0:T(8,128)}) %all-reduce.4.cloned.1.call-update) | async-done | bytes 131088
  262.7 0.7 fusion.42
  263.5 0.2 convolution_bitcast_fusion
  263.6 99.7 %psum.14 = f32[8]{0:T(128)S(1)} all-reduce(f32[8]{0:T(128)S(1)} %convolution_bitcast_fusion), channel_id=1, replica_groups=mesh['group'=16,'dev'=32] {'group','dev'}, use_global_device_ids=true, to_apply=%region_2.3 | all-reduce | flops 8 | bytes 64 | tf_op jit(solution)/shard_map/psum | solution.py:93
  363.3 0.2 fusion.40
  363.5 0.6 multiply_reduce_fusion
  364.1 94.3 %psum.15 = f32[]{:T(128)} all-reduce(f32[]{:T(128)} %get-tuple-element.2), channel_id=1, replica_groups=mesh['group'=16,'dev'=32] {'group','dev'}, use_global_device_ids=true, to_apply=%region_4.5 | all-reduce | flops 1 | bytes 8 | tf_op jit(solution)/shard_map/psum | solution.py:95
  459.1 0.6 broadcast_divide_fusion
  (22 shorter events, 0.1 us)
Async XLA Ops:
  7.2 94.1 %copy-start = (bf16[12,256,256]{2,1,0:T(8,128)(2,1)S(1)}, bf16[12,256,256]{2,1,0:T(8,128)(2,1)}, u32[]{:S(2)}) copy-start(bf16[12,256,256]{2,1,0:T(8,128)(2,1)} %param.12) | copy-start | bytes 4718596
  7.2 255.6 %all-reduce.4.cloned.1.call-start = ((), (), s32[]{:S(2)}) async-start(), calls=%async_computation | async-start | bytes 262144
  48.7 54.8 %collective-permute-start.1 = (bf16[128,32]{1,0:T(8,128)(2,1)S(1)}, bf16[128,32]{1,0:T(8,128)(2,1)S(1)}, u32[]{:S(2)}, u32[]{:S(2)}) collective-permute-start(bf16[128,32]{1,0:T(8,128)(2,1)S(1)} %bitcast.101), channel_id=1, source_target_pairs={{32,0},{64,32},{96,64},{128,96},{160,128},{192,160},{224,192},{256... | collective-permute-start | bytes 24584 | tf_op jit(solution)/shard_map/ppermute | solution.py:16
  59.5 44.0 %collective-permute-start = (bf16[128,32]{1,0:T(8,128)(2,1)S(1)}, bf16[128,32]{1,0:T(8,128)(2,1)S(1)}, u32[]{:S(2)}, u32[]{:S(2)}) collective-permute-start(bf16[128,32]{1,0:T(8,128)(2,1)S(1)} %bitcast.102), channel_id=1, source_target_pairs={{0,32},{32,64},{64,96},{96,128},{128,160},{160,192},{192,224},{224... | collective-permute-start | bytes 24584 | tf_op jit(solution)/shard_map/ppermute | solution.py:13
  101.3 1.2 copy-start.5
  101.3 1.2 copy-start.1
  103.5 131.2 %copy-start.3 = (bf16[4,32,256]{2,1,0:T(8,128)(2,1)S(1)}, bf16[4,32,256]{2,1,0:T(8,128)(2,1)}, u32[]{:S(2)}) copy-start(bf16[4,32,256]{2,1,0:T(8,128)(2,1)} %param.11) | copy-start | bytes 196612
  103.5 159.9 %copy-start.2 = (f32[8,1024]{1,0:T(8,128)S(1)}, f32[8,1024]{1,0:T(8,128)}, u32[]{:S(2)}) copy-start(f32[8,1024]{1,0:T(8,128)} %param.10) | copy-start | bytes 98308
  106.1 15.7 %collective-permute-start.3 = (f32[128,32]{0,1:T(8,128)S(1)}, f32[128,32]{0,1:T(8,128)S(1)}, u32[]{:S(2)}, u32[]{:S(2)}) collective-permute-start(f32[128,32]{0,1:T(8,128)S(1)} %get-tuple-element.11), channel_id=1, source_target_pairs={{0,480},{32,0},{64,32},{96,64},{128,96},{160,128},{192,160},{224,1... | collective-permute-start | bytes 49160 | tf_op jit(solution)/shard_map/ppermute | solution.py:24
  117.7 4.2 collective-permute-start.2
  363.3 96.4 %copy-start.4 = (f32[8]{0:T(128)}, f32[8]{0:T(128)S(1)}, u32[]{:S(2)}) copy-start(f32[8]{0:T(128)S(1)} %psum.14) | copy-start | bytes 100
Sparse Core Ops, SparseCore 0:
  120.0 142.6 all-reduce.3
where the time goes:
time: 468 us; the launch traced here: 467 us
  blocking collectives  382 us (82%)
  waiting for transfers between devices  28 us (6%)
  starting transfers between devices  24.8 us (5%)
  between operations  15.6 us (3%)
  other arithmetic  6.5 us (1%)
  local copies, waits for them, and re-layouts  4.92 us (1%)
  matrix products  4.76 us (1%)
    unnamed x1, blocking collectives  113 us
    psum x1, blocking collectives, local(): projections = lax.psum(local_proj, ('group', 'dev'))  99.7 us
    psum x1, blocking collectives, local(): length_sq = lax.psum(jnp.sum(remainder * remainder), ('group', 'dev'))  94.3 us
    all_gather x1, blocking collectives, local(): group_coeffs = lax.all_gather(coeffs, 'dev', axis=0, tiled=True)  39.7 us
    all_gather x1, blocking collectives, local(): group_panels = lax.all_gather(panels_bf, 'dev', axis=0, tiled=True)  35.6 us
    unnamed x2, waiting for transfers between devices  28 us
    ppermute x2, starting transfers between devices, passed_along(): return lax.ppermute(value, axis, pairs)  12.8 us
    ppermute x1, starting transfers between devices, extended(): lax.ppermute(lax.slice_in_dim(block, 0, width, axis=dim), axis, backward)  10.8 us
  transfers between devices with their start and end apart: 5, of which 1 were waited for; matrix products, arithmetic and copies ran while one was open for 2% of the time, Pallas kernels for 0%

commit v1 on v0

v1 whole, which is shorter than its diff:
```python
import jax
import jax.numpy as jnp
from jax import lax
from jax.experimental import pallas as pl
from jax.experimental.pallas import tpu as pltpu
from jax.sharding import PartitionSpec as P

F32 = jnp.float32
BF16 = jnp.bfloat16
NX, NZ, NY = 4, 8, 8
VMEM = pl.BlockSpec(memory_space=pltpu.VMEM)
HBM = pl.BlockSpec(memory_space=pltpu.HBM)
SMEM = pl.BlockSpec(memory_space=pltpu.SMEM)


def call(body, outs, specs, scratch=()):
    kernel = pl.pallas_call(
        body,
        out_shape=outs,
        in_specs=specs,
        out_specs=jax.tree.map(lambda _: VMEM, outs),
        scratch_shapes=list(scratch),
        compiler_params=pltpu.CompilerParams(vmem_limit_bytes=24 * 1024 * 1024),
    )

    def run(*args):
        return kernel(
            *(
                pltpu.with_memory_space_constraint(arg, pltpu.HBM) if spec is HBM else arg
                for arg, spec in zip(args, specs, strict=True)
            )
        )

    return run


def iota(shape, dim):
    return lax.broadcasted_iota(jnp.int32, shape, dim)


def mm(a, b):
    return lax.dot_general(a, b, (((1,), (0,)), ((), ())), preferred_element_type=F32)


def mm_t(a, b):
    return lax.dot_general(a, b, (((1,), (1,)), ((), ())), preferred_element_type=F32)


def mm_exact(a, b, dims):
    return lax.dot_general(
        a, b, (dims, ((), ())), precision=lax.Precision.HIGHEST, preferred_element_type=F32
    )


def halves(value):
    high = value.astype(BF16)
    return high, (value - high.astype(F32)).astype(BF16)


def one_hot(mask):
    return mask.astype(F32).astype(BF16)


def columns(rows):
    width = rows.shape[1]
    same = one_hot(iota((width, width), 0) == iota((width, width), 1))
    return mm_t(same, rows.astype(F32).astype(BF16)).astype(jnp.int32)


def to_all(value, axis):
    return lax.all_to_all(value, axis, split_axis=0, concat_axis=0, tiled=True)


def group_shift(value, step):
    return lax.ppermute(value, "group", [(g, (g + step) % (2 * NY)) for g in range(2 * NY)])


def pack_body(direction_hbm, bases_hbm, out_ref, own_ref, direction_ref, bases_ref, sems):
    copies = [
        pltpu.make_async_copy(direction_hbm, direction_ref, sems.at[0]),
        pltpu.make_async_copy(bases_hbm, bases_ref, sems.at[1]),
    ]
    for copy in copies:
        copy.start()
    for copy in copies:
        copy.wait()
    xb = direction_ref[...].astype(BF16)
    rank_rows = bases_ref[...]
    low = mm_t(xb, rank_rows[:, :128])
    high = mm_t(xb, rank_rows[:, 128:])
    row = iota((8, 128), 0)
    twice = (iota((8, 128), 1) >> 5) * 2
    kept = jnp.where(row == twice, low, 0.0) + jnp.where(row == twice + 1, high, 0.0)
    coeffs = jnp.sum(kept, axis=0, keepdims=True)
    own_ref[...] = coeffs.astype(BF16)
    out_ref[...] = jnp.concatenate([xb, jnp.where(row == 0, coeffs, 0.0).astype(BF16)], axis=0)


def copies_body(packed_ref, before_ref, after_ref, out_ref):
    row = iota((16, 128), 0)
    packed = packed_ref[...].astype(F32)
    packed = jnp.where(row == 9, before_ref[...].astype(F32), packed)
    packed = jnp.where(row == 10, after_ref[...].astype(F32), packed).astype(BF16)
    for d in range(out_ref.shape[0]):
        out_ref[d] = packed


def prep_body(blocks_hbm, pairs_hbm, mask_hbm, near_pairs_hbm, near_mask_hbm, krylov_hbm,
              out_ref, near_ref, gram_ref, pairs_ref, mask_ref, krylov_ref, sems):
    slots = blocks_hbm.shape[0]
    ends = (
        (blocks_hbm, out_ref.at[0:slots]),
        (pairs_hbm, pairs_ref),
        (mask_hbm, mask_ref),
        (near_pairs_hbm, near_ref.at[0:2]),
        (near_mask_hbm, near_ref.at[2:3]),
        (krylov_hbm, krylov_ref),
    )
    copies = [pltpu.make_async_copy(*end, sems.at[k]) for k, end in enumerate(ends)]
    for copy in copies:
        copy.start()
    for copy in copies:
        copy.wait()
    i_row, j_row = pairs_ref[0:1, :], pairs_ref[1:2, :]
    row = iota((16, slots), 0)
    digits = jnp.zeros((16, slots), jnp.int32)
    for k, value in enumerate((i_row >> 7, i_row & 127, j_row >> 7, j_row & 127, mask_ref[...])):
        digits = jnp.where(row == k, value, digits)
    out_ref[slots : slots + 16, :] = jnp.zeros((16, out_ref.shape[1]), BF16)
    out_ref[slots : slots + 16, 0:slots] = digits.astype(F32).astype(BF16)
    rows = krylov_ref[...]
    gram = mm_exact(rows, rows, ((1,), (1,)))
    lane, row = iota((8, 128), 1) - 8, iota((8, 128), 0)
    inside = (lane >= 0) & (lane < 64)
    wide = mm_exact(gram, jnp.where(inside & ((lane & 7) == row), 1.0, 0.0), ((1,), (0,)))
    gram_ref[...] = jnp.sum(
        jnp.where(inside & ((lane >> 3) == row), wide, 0.0), axis=0, keepdims=True
    )


def near_field(gathered, tiles, pairs):
    slots = len(tiles)
    i_row, j_row, mask = pairs[0:1, :], pairs[1:2, :], pairs[2:3, :]
    cols = columns(pairs)
    lanes = iota((slots, gathered.shape[0]), 1)

    def gather(c):
        row = (c >> 2) * 16 + (c & 3) * 2
        first = mm(one_hot(lanes == row), gathered)
        second = mm(one_hot(lanes == row + 1), gathered)
        return jnp.concatenate([first, second], axis=1).astype(BF16)

    right = gather(cols[:, 1:2])
    left = gather(cols[:, 0:1])
    slot = iota((slots, 256), 0)
    forward = jnp.zeros((slots, 256), F32)
    backward = jnp.zeros((slots, 256), F32)
    for s in range(slots):
        tile = tiles[s]()
        forward = jnp.where(slot == s, mm_t(right, tile), forward)
        backward = jnp.where(slot == s, mm(left, tile), backward)
    rows = iota((256, slots), 0)
    i_target = jnp.where(mask == 1, i_row * 2, -8)
    j_target = jnp.where((mask == 1) & (i_row != j_row), j_row * 2, -8)
    total = jnp.zeros((256, 128), F32)
    for target, value in ((i_target, forward), (j_target, backward)):
        for half in range(2):
            pick = one_hot(rows == target + half)
            for part in halves(value[:, half * 128 : half * 128 + 128]):
                total = total + mm(pick, part)
    return total


def far_field(gathered, bundles, group):
    slots = bundles[0].shape[0] - 16
    digits = [bundle[slots : slots + 16, 0:slots] for bundle in bundles]
    rows = [d.astype(F32).astype(jnp.int32) for d in digits]
    cols = jnp.concatenate([columns(r) for r in rows], axis=0)
    blocks = jnp.concatenate([bundle[0:slots, :] for bundle in bundles], axis=0).astype(F32)
    total_slots = blocks.shape[0]
    i_group, i_low, j_group, j_low, live = (cols[:, k : k + 1] for k in range(5))

    def gather(c_group, c_low):
        step = (c_group - group) & (2 * NY - 1)
        which = jnp.where(step == 0, 0, jnp.where(step == 1, 2, 1))
        place = (c_low >> 2) * 16 + 8 + which
        n = c_low.shape[0]
        taken = mm(one_hot(iota((n, gathered.shape[0]), 1) == place), gathered)
        return jnp.where((iota((n, 128), 1) >> 5) == (c_low & 3), taken, 0.0).astype(BF16)

    right = gather(j_group[0:slots], j_low[0:slots])
    left = gather(i_group, i_low)
    rank = iota((128, 1024), 0) & 31
    column = iota((128, 1024), 1)
    by_column = one_hot(rank == (column & 31))
    by_row = one_hot(rank == (column >> 5))
    forward = jnp.zeros((slots, 128), F32)
    for part in halves(blocks[0:slots] * mm(right, by_column)):
        forward = forward + mm_t(part, by_row)
    backward = jnp.zeros((total_slots, 128), F32)
    for part in halves(blocks * mm(left, by_row)):
        backward = backward + mm_t(part, by_column)
    lane_block = iota((total_slots, 128), 1) >> 5
    forward = jnp.where(
        (live[0:slots] == 1) & (lane_block[0:slots] == (i_low[0:slots] & 3)), forward, 0.0
    )
    different = (i_group != j_group) | (i_low != j_low)
    mine = (live == 1) & (j_group == group) & different
    backward = jnp.where(mine & (lane_block == (j_low & 3)), backward, 0.0)
    owner = iota((NZ * NX, slots), 0)
    total = jnp.zeros((NZ * NX, 128), F32)
    pick = one_hot(owner == (rows[0][1:2, :] >> 2))
    for part in halves(forward):
        total = total + mm(pick, part)
    for k in range(len(bundles)):
        pick = one_hot(owner == (rows[k][3:4, :] >> 2))
        for part in halves(backward[k * slots : k * slots + slots]):
            total = total + mm(pick, part)
    return total


def main_body(place_ref, near_ref, own_ref, before_ref, after_ref, gathered_ref,
              tiles_hbm, out_ref, tiles_ref, sems):
    slots = tiles_ref.shape[0]
    copies = [
        pltpu.make_async_copy(tiles_hbm.at[s], tiles_ref.at[s], sems.at[s]) for s in range(slots)
    ]
    for copy in copies:
        copy.start()
    gathered = gathered_ref[...]
    bundles = [ref[...] for ref in (own_ref, before_ref, after_ref)]
    far = far_field(gathered, bundles, place_ref[0])
    for d in range(NZ * NX):
        out_ref[d, :, 1024:1152] = far[d : d + 1, :]

    def tile(s):
        def load():
            copies[s].wait()
            return tiles_ref[s]
        return load

    near = near_field(gathered, [tile(s) for s in range(slots)], near_ref[...])
    for d in range(NZ * NX):
        for r in range(8):
            out_ref[d, :, r * 128 : r * 128 + 128] = near[d * 8 + r : d * 8 + r + 1, :]


def product_body(pieces_ref, bases_ref, krylov_ref, gram_ref, product_ref, copies_ref):
    total = jnp.sum(pieces_ref[...], axis=0)
    near = jnp.concatenate([total[:, r * 128 : r * 128 + 128] for r in range(8)], axis=0)
    coef = total[:, 1024:1152].astype(BF16).astype(F32)
    row, lane = iota((8, 128), 0), iota((8, 128), 1)
    spread = jnp.where((lane >> 5) == (row >> 1), coef, 0.0).astype(BF16)
    low = mm(spread, bases_ref[:, :128])
    high = mm(spread, bases_ref[:, 128:])
    product = near + jnp.where((row & 1) == 0, low, high)
    product_ref[...] = product
    acc = jnp.zeros((8, 128), F32)
    for r in range(8):
        acc = acc + krylov_ref[:, r * 128 : r * 128 + 128] * product[r : r + 1, :]
    proj = jnp.sum(acc, axis=1, keepdims=True)
    square = jnp.sum(product * product, axis=1, keepdims=True)
    values = jnp.where(lane == row, proj, 0.0) + jnp.where(lane == 72, square, 0.0)
    payload = jnp.sum(values, axis=0, keepdims=True) + gram_ref[...]
    for d in range(copies_ref.shape[0]):
        copies_ref[d] = payload


def last_body(count, pieces_ref, product_ref, krylov_ref, next_ref, proj_ref):
    total = jnp.sum(pieces_ref[...], axis=0)
    row, lane = iota((8, 128), 0), iota((8, 128), 1)
    proj = jnp.sum(jnp.where(lane == row, total, 0.0), axis=1, keepdims=True)
    inside = (lane >= 8) & (lane < 72)
    first = jnp.sum(jnp.where(inside & (((lane - 8) >> 3) == row), proj, 0.0), axis=0, keepdims=True)
    second = jnp.sum(jnp.where(inside & ((lane & 7) == row), proj, 0.0), axis=0, keepdims=True)
    lane = iota((1, 128), 1)
    terms = total * jnp.where(lane < 8, -2.0 * total, first * second)
    terms = jnp.where(lane == 72, total, jnp.where(lane < 72, terms, 0.0))
    length_sq = jnp.sum(terms, axis=1, keepdims=True)
    scale = 1.0 / jnp.sqrt(jnp.maximum(length_sq, 0.0) / count)
    for r in range(8):
        taken = jnp.sum(proj * krylov_ref[:, r * 128 : r * 128 + 128], axis=0, keepdims=True)
        next_ref[r : r + 1, :] = (product_ref[r : r + 1, :] - taken) * scale
    proj_ref[...] = total[:, 0:8]


def local(
    direction, krylov, bases, near_tiles, near_pairs, near_mask, far_blocks, far_pairs, far_mask
):
    panels = direction.shape[0]
    devs, groups = NZ * NX, 2 * NY
    rank_rows = bases.reshape(-1, bases.shape[2])
    place = lax.axis_index("group").astype(jnp.int32)[None]
    sds = jax.ShapeDtypeStruct
    slots, far_slots = near_tiles.shape[0], far_blocks.shape[0]

    packed, own = call(
        pack_body,
        [sds((16, 128), BF16), sds((1, 128), BF16)],
        [HBM, HBM],
        [pltpu.VMEM((8, 128), F32), pltpu.VMEM(rank_rows.shape, BF16), pltpu.SemaphoreType.DMA((2,))],
    )(direction.reshape(8, 128), rank_rows)
    copies = call(copies_body, sds((devs, 16, 128), BF16), [VMEM] * 3)(
        packed, group_shift(own, 1), group_shift(own, -1)
    )
    gathered = to_all(copies, "dev")
    bundle, near_rows, gram = call(
        prep_body,
        [
            sds((far_slots + 16, far_blocks.shape[1]), BF16),
            sds((3, slots), jnp.int32),
            sds((1, 128), F32),
        ],
        [HBM] * 6,
        [
            pltpu.VMEM((2, far_slots), jnp.int32),
            pltpu.VMEM((1, far_slots), jnp.int32),
            pltpu.VMEM(krylov.shape, F32),
            pltpu.SemaphoreType.DMA((6,)),
        ],
    )(far_blocks, far_pairs.T, far_mask[None], near_pairs.T, near_mask[None], krylov)
    before, after = group_shift(bundle, 1), group_shift(bundle, -1)

    parts = call(
        main_body,
        sds((devs, 1, 1152), F32),
        [SMEM] + [VMEM] * 5 + [HBM],
        [pltpu.VMEM(near_tiles.shape, BF16), pltpu.SemaphoreType.DMA((slots,))],
    )(
        place, near_rows, bundle, before, after,
        gathered.reshape(-1, 128), near_tiles,
    )
    product, copies = call(
        product_body, [sds((8, 128), F32), sds((groups * devs, 1, 128), F32)], [VMEM] * 4
    )(to_all(parts, "dev"), rank_rows, krylov, gram)
    count = float(panels * devs * groups)

    def finish(*refs):
        last_body(count, *refs)

    next_vector, projections = call(finish, [sds((8, 128), F32), sds((1, 8), F32)], [VMEM] * 3)(
        to_all(copies, ("group", "dev")), product, krylov
    )
    return (next_vector.reshape(-1), projections.reshape(-1))


def solution(mesh):
    in_specs = (
        P(("group", "dev")),
        P(None, ("group", "dev")),
        P(("group", "dev"), None, None),
        P(("group", "dev"), None, None),
        P(("group", "dev"), None),
        P(("group", "dev")),
        P(("group", "dev"), None),
        P(("group", "dev"), None),
        P(("group", "dev")),
    )
    out_specs = (P(("group", "dev")), P())
    return jax.shard_map(local, mesh=mesh, in_specs=in_specs, out_specs=out_specs, check_vma=False)
```

time: 468 us -> 84.9 us (0.18)
  blocking collectives: 382 us -> 48 us
  waiting for transfers between devices: 28 us -> 5.29 us
  between operations: 15.6 us -> 0.68 us
  Pallas kernels: 0 us -> 9.78 us
  other arithmetic: 6.5 us -> 0 us
  local copies, waits for them, and re-layouts: 4.92 us -> 0.01 us
  matrix products: 4.76 us -> 0 us
    psum x2 -> x0, blocking collectives: 194 us -> none  [the longest x1 99.7 us: local(): projections = lax.psum(local_proj, ('group', 'dev'))]
    unnamed x1 -> x0, blocking collectives: 113 us -> none
    all_gather x2 -> x0, blocking collectives: 75.3 us -> none  [the longest x1 39.7 us: local(): group_coeffs = lax.all_gather(coeffs, 'dev', axis=0, tiled=True)]
    all_to_all x0 -> x2, blocking collectives: none -> 48 us  [to_all(): return lax.all_to_all(value, axis, split_axis=0, concat_axis=0, tiled=True)]
    unnamed x2 -> x0, waiting for transfers between devices: 28 us -> none
    ppermute x4, starting transfers between devices: 24.7 us -> 10.8 us  [group_shift(): lax.ppermute(value, 'group', [(g, (g + step) % (2 * NY)) for g in range(2...]
    all_to_all x0 -> x1, starting transfers between devices: none -> 10 us  [to_all(): return lax.all_to_all(value, axis, split_axis=0, concat_axis=0, tiled=True)]
    pallas_call x0 -> x6, Pallas kernels: none -> 9.78 us  [run(): kernel(*(pltpu.with_memory_space_constraint(arg, pltpu.HBM) if spec is HB...]
  transfers between devices with their start and end apart: 5 -> 5, of which waited for: 1 -> 5; matrix products, arithmetic and copies ran while one was open for 2% -> 0% of each run, Pallas kernels for 0% -> 2%
where the time goes in v1:
time: 84.9 us; the launch traced here: 84.6 us
  blocking collectives  48 us (57%)
  starting transfers between devices  20.8 us (24%)
  Pallas kernels  9.78 us (12%)
  waiting for transfers between devices  5.29 us (6%)
    all_to_all x2, blocking collectives, to_all(): return lax.all_to_all(value, axis, split_axis=0, concat_axis=0, tiled=True)  48 us
    ppermute x4, starting transfers between devices, group_shift(): lax.ppermute(value, 'group', [(g, (g + step) % (2 * NY)) for g in range(2...  10.8 us
    all_to_all x1, starting transfers between devices, to_all(): return lax.all_to_all(value, axis, split_axis=0, concat_axis=0, tiled=True)  10 us
    pallas_call x6, Pallas kernels, run(): kernel(*(pltpu.with_memory_space_constraint(arg, pltpu.HBM) if spec is HB...  9.78 us
    ppermute x4, waiting for transfers between devices, group_shift(): lax.ppermute(value, 'group', [(g, (g + step) % (2 * NY)) for g in range(2...  3.38 us
    all_to_all x1, waiting for transfers between devices, to_all(): return lax.all_to_all(value, axis, split_axis=0, concat_axis=0, tiled=True)  1.9 us
  transfers between devices with their start and end apart: 5, of which 5 were waited for; matrix products, arithmetic and copies ran while one was open for 0% of the time, Pallas kernels for 2%

profile of v1, /device:TPU:1, one launch (start us, length us, event | category | flops | bytes accessed | tf_op | source)
XLA Modules:
  0.0 84.6 jit_solution(13332617646003683356)
XLA Ops:
  0.6 1.0 %shard_map.105 = (bf16[16,128]{1,0:T(8,128)(2,1)S(1)}, bf16[1,128]{1,0:T(2,128)(2,1)S(1)}) custom-call(f32[8,128]{1,0:T(8,128)} %bitcast.13, bf16[128,256]{1,0:T(8,128)(2,1)} %bitcast.11), custom_call_target="tpu_custom_call" | custom-call | tf_op jit(solution)/shard_map/pallas_call | solution.py:27
  1.7 6.9 %collective-permute-start.3 = (bf16[1,128]{1,0:T(2,128)(2,1)S(1)}, bf16[1,128]{1,0:T(2,128)(2,1)S(1)}, u32[]{:S(2)}, u32[]{:S(2)}) collective-permute-start(bf16[1,128]{1,0:T(2,128)(2,1)S(1)} %get-tuple-element.14), channel_id=1, source_target_pairs={{0,480},{32,0},{64,32},{96,64},{128,96},{160,128},{192,160},{224,1... | collective-permute-start | bytes 776 | tf_op jit(solution)/shard_map/ppermute | solution.py:75
  8.6 0.0 collective-permute-start.2
  8.6 0.8 collective-permute-done.3.after_ref
  9.4 0.3 collective-permute-done.2.before_ref
  9.7 0.7 shard_map.106
  10.3 0.0 copy-start
  10.3 0.0 copy-start.1
  10.3 10.0 %all-to-all-start = ((bf16[32,16,128]{2,1,0:T(8,128)(2,1)}), bf16[32,16,128]{2,1,0:T(8,128)(2,1)S(1)}, u32[]{:S(2)}, u32[]{:S(2)}) async-start(bf16[32,16,128]{2,1,0:T(8,128)(2,1)} %shard_map.106), calls=%async_computation | async-start | bytes 262144 | tf_op jit(solution)/shard_map/all_to_all | solution.py:71
  20.4 1.3 %shard_map.104 = (bf16[80,1024]{1,0:T(8,128)(2,1)S(1)}, s32[3,12]{1,0:T(4,128)S(1)}, f32[1,128]{1,0:T(1,128)S(1)}) custom-call(bf16[64,1024]{1,0:T(8,128)(2,1)} %blocks_hbm.1, s32[2,64]{1,0:T(2,128)} %bitcast.14, s32[1,64]{1,0:T(1,128)} %bitcast.16, s32[2,12]{1,0:T(2,128)} %bitcast.15, s32[1,12]{1,0:T(1,128)} %bitcast.17, f32[8,1024]{1,0:T(8,128)} %refs_2_.1), custom_call_target="tpu_custom_call" | custom-call | tf_op jit(solution)/shard_map/pallas_call | solution.py:27
  21.7 3.9 %collective-permute-start.1 = (bf16[80,1024]{1,0:T(8,128)(2,1)S(1)}, bf16[80,1024]{1,0:T(8,128)(2,1)S(1)}, u32[]{:S(2)}, u32[]{:S(2)}) collective-permute-start(bf16[80,1024]{1,0:T(8,128)(2,1)S(1)} %get-tuple-element.12.own_ref), channel_id=1, source_target_pairs={{0,480},{32,0},{64,32},{96,64},{128,96},{160,128},{192,160},{224,1... | collective-permute-start | bytes 491528 | tf_op jit(solution)/shard_map/ppermute | solution.py:75
  25.6 0.0 collective-permute-start
  25.6 1.0 %collective-permute-done.1.after_ref = bf16[80,1024]{1,0:T(8,128)(2,1)S(1)} collective-permute-done((bf16[80,1024]{1,0:T(8,128)(2,1)S(1)}, bf16[80,1024]{1,0:T(8,128)(2,1)S(1)}, u32[]{:S(2)}, u32[]{:S(2)}) %collective-permute-start.1) | collective-permute-done | bytes 163872 | tf_op jit(solution)/shard_map/ppermute | solution.py:75
  26.6 1.2 %collective-permute-done.before_ref = bf16[80,1024]{1,0:T(8,128)(2,1)S(1)} collective-permute-done((bf16[80,1024]{1,0:T(8,128)(2,1)S(1)}, bf16[80,1024]{1,0:T(8,128)(2,1)S(1)}, u32[]{:S(2)}, u32[]{:S(2)}) %collective-permute-start) | collective-permute-done | bytes 163872 | tf_op jit(solution)/shard_map/ppermute | solution.py:75
  27.8 1.9 %all-to-all-done = bf16[32,16,128]{2,1,0:T(8,128)(2,1)S(1)} async-done(((bf16[32,16,128]{2,1,0:T(8,128)(2,1)}), bf16[32,16,128]{2,1,0:T(8,128)(2,1)S(1)}, u32[]{:S(2)}, u32[]{:S(2)}) %all-to-all-start) | async-done | bytes 131104 | tf_op jit(solution)/shard_map/all_to_all | solution.py:71
  29.7 5.1 %shard_map.107 = f32[32,1,1152]{2,1,0:T(1,128)S(1)} custom-call(s32[1]{0:T(128)} %bitcast.place_ref, s32[3,12]{1,0:T(4,128)S(1)} %get-tuple-element.11.near_ref, bf16[80,1024]{1,0:T(8,128)(2,1)S(1)} %get-tuple-element.12.own_ref, bf16[80,1024]{1,0:T(8,128)(2,1)S(1)} %collective-permute-done.before_ref, ...), custom_call_target="tpu_custom_call" | custom-call | tf_op jit(solution)/shard_map/pallas_call | solution.py:27
  34.8 16.9 %all_to_all.15.pieces_ref = f32[32,1,1152]{2,1,0:T(1,128)S(1)} all-to-all(f32[32,1,1152]{2,1,0:T(1,128)S(1)} %shard_map.107), channel_id=1, replica_groups=mesh['group'=16,'dev'=32] {'dev'}, dimensions={0} | all-to-all | bytes 294912 | tf_op jit(solution)/shard_map/all_to_all | solution.py:71
  51.7 0.0 copy-done
  51.7 0.0 copy-done.1
  51.7 0.4 shard_map.108
  52.1 31.1 %all_to_all.16.refs_0_ = f32[512,1,128]{2,1,0:T(1,128)S(1)} all-to-all(f32[512,1,128]{2,1,0:T(1,128)S(1)} %get-tuple-element.16), channel_id=1, replica_groups=mesh['group'=16,'dev'=32] {'group','dev'}, dimensions={0} | all-to-all | bytes 524288 | tf_op jit(solution)/shard_map/all_to_all | solution.py:71
  83.3 1.3 %shard_map.109 = (f32[8,128]{1,0:T(8,128)}, f32[1,8]{1,0:T(1,128)}) custom-call(f32[512,1,128]{2,1,0:T(1,128)S(1)} %all_to_all.16.refs_0_, f32[8,128]{1,0:T(8,128)S(1)} %get-tuple-element.17.refs_1_, f32[8,1024]{1,0:T(8,128)S(1)} %copy-done), custom_call_target="tpu_custom_call" | custom-call | tf_op jit(solution)/shard_map/pallas_call | solution.py:27
Async XLA Ops:
  1.7 7.7 %collective-permute-start.3 = (bf16[1,128]{1,0:T(2,128)(2,1)S(1)}, bf16[1,128]{1,0:T(2,128)(2,1)S(1)}, u32[]{:S(2)}, u32[]{:S(2)}) collective-permute-start(bf16[1,128]{1,0:T(2,128)(2,1)S(1)} %get-tuple-element.14), channel_id=1, source_target_pairs={{0,480},{32,0},{64,32},{96,64},{128,96},{160,128},{192,160},{224,1... | collective-permute-start | bytes 776 | tf_op jit(solution)/shard_map/ppermute | solution.py:75
  8.6 1.1 %collective-permute-start.2 = (bf16[1,128]{1,0:T(2,128)(2,1)S(1)}, bf16[1,128]{1,0:T(2,128)(2,1)S(1)}, u32[]{:S(2)}, u32[]{:S(2)}) collective-permute-start(bf16[1,128]{1,0:T(2,128)(2,1)S(1)} %get-tuple-element.14), channel_id=1, source_target_pairs={{0,32},{32,64},{64,96},{96,128},{128,160},{160,192},{192,224},{224... | collective-permute-start | bytes 776 | tf_op jit(solution)/shard_map/ppermute | solution.py:75
  10.3 41.3 %copy-start = (f32[8,1024]{1,0:T(8,128)S(1)}, f32[8,1024]{1,0:T(8,128)}, u32[]{:S(2)}) copy-start(f32[8,1024]{1,0:T(8,128)} %refs_2_.1) | copy-start | bytes 98308
  10.3 41.3 %copy-start.1 = (bf16[4,32,256]{2,1,0:T(8,128)(2,1)S(1)}, bf16[4,32,256]{2,1,0:T(8,128)(2,1)}, u32[]{:S(2)}) copy-start(bf16[4,32,256]{2,1,0:T(8,128)(2,1)} %param.11) | copy-start | bytes 196612
  10.3 19.4 %all-to-all-start = ((bf16[32,16,128]{2,1,0:T(8,128)(2,1)}), bf16[32,16,128]{2,1,0:T(8,128)(2,1)S(1)}, u32[]{:S(2)}, u32[]{:S(2)}) async-start(bf16[32,16,128]{2,1,0:T(8,128)(2,1)} %shard_map.106), calls=%async_computation | async-start | bytes 262144 | tf_op jit(solution)/shard_map/all_to_all | solution.py:71
  21.7 4.9 %collective-permute-start.1 = (bf16[80,1024]{1,0:T(8,128)(2,1)S(1)}, bf16[80,1024]{1,0:T(8,128)(2,1)S(1)}, u32[]{:S(2)}, u32[]{:S(2)}) collective-permute-start(bf16[80,1024]{1,0:T(8,128)(2,1)S(1)} %get-tuple-element.12.own_ref), channel_id=1, source_target_pairs={{0,480},{32,0},{64,32},{96,64},{128,96},{160,128},{192,160},{224,1... | collective-permute-start | bytes 491528 | tf_op jit(solution)/shard_map/ppermute | solution.py:75
  25.6 2.3 %collective-permute-start = (bf16[80,1024]{1,0:T(8,128)(2,1)S(1)}, bf16[80,1024]{1,0:T(8,128)(2,1)S(1)}, u32[]{:S(2)}, u32[]{:S(2)}) collective-permute-start(bf16[80,1024]{1,0:T(8,128)(2,1)S(1)} %get-tuple-element.12.own_ref), channel_id=1, source_target_pairs={{0,32},{32,64},{64,96},{96,128},{128,160},{160,192},{192,224},{224... | collective-permute-start | bytes 491528 | tf_op jit(solution)/shard_map/ppermute | solution.py:75

commit v2 on v1

v2 whole, which is shorter than its diff:
```python
import jax
import jax.numpy as jnp
from jax import lax
from jax.experimental import pallas as pl
from jax.experimental.pallas import tpu as pltpu
from jax.sharding import PartitionSpec as P

F32 = jnp.float32
BF16 = jnp.bfloat16
I32 = jnp.int32
NX, NZ, NY = 4, 8, 8
DEVS, GROUPS = NZ * NX, 2 * NY
VMEM = pl.BlockSpec(memory_space=pltpu.VMEM)
HBM = pl.BlockSpec(memory_space=pltpu.HBM)
SMEM = pl.BlockSpec(memory_space=pltpu.SMEM)
sds = jax.ShapeDtypeStruct


def call(body, outs, specs, scratch=()):
    kernel = pl.pallas_call(
        body,
        out_shape=outs,
        in_specs=specs,
        out_specs=jax.tree.map(lambda _: VMEM, outs),
        scratch_shapes=list(scratch),
        compiler_params=pltpu.CompilerParams(vmem_limit_bytes=24 * 1024 * 1024),
    )

    def run(*args):
        return kernel(
            *(
                pltpu.with_memory_space_constraint(arg, pltpu.HBM) if spec is HBM else arg
                for arg, spec in zip(args, specs, strict=True)
            )
        )

    return run


def iota(shape, dim):
    return lax.broadcasted_iota(I32, shape, dim)


def mm(a, b):
    return lax.dot_general(a, b, (((1,), (0,)), ((), ())), preferred_element_type=F32)


def mm_t(a, b):
    return lax.dot_general(a, b, (((1,), (1,)), ((), ())), preferred_element_type=F32)


def mm_exact(a, b, dims):
    return lax.dot_general(
        a, b, (dims, ((), ())), precision=lax.Precision.HIGHEST, preferred_element_type=F32
    )


def halves(value):
    high = value.astype(BF16)
    return high, (value - high.astype(F32)).astype(BF16)


def one_hot(mask):
    return mask.astype(F32).astype(BF16)


def small(rows):
    return rows.astype(F32).astype(BF16)


def columns(rows):
    width = rows.shape[1]
    same = one_hot(iota((width, width), 0) == iota((width, width), 1))
    return mm_t(same, small(rows)).astype(I32)


def to_all(value, axis):
    return lax.all_to_all(value, axis, split_axis=0, concat_axis=0, tiled=True)


def group_shift(value, step):
    return lax.ppermute(value, "group", [(g, (g + step) % GROUPS) for g in range(GROUPS)])


def started(ends, sems):
    copies = [pltpu.make_async_copy(*end, sems.at[k]) for k, end in enumerate(ends)]
    for copy in copies:
        copy.start()
    return copies


def pack_body(direction_hbm, bases_hbm, out_ref, direction_ref, bases_ref, sems):
    for copy in started(((direction_hbm, direction_ref), (bases_hbm, bases_ref)), sems):
        copy.wait()
    xb = direction_ref[...].astype(BF16)
    rank_rows = bases_ref[...]
    low = mm_t(xb, rank_rows[:, :128])
    high = mm_t(xb, rank_rows[:, 128:])
    row = iota((8, 128), 0)
    twice = (iota((8, 128), 1) >> 5) * 2
    kept = jnp.where(row == twice, low, 0.0) + jnp.where(row == twice + 1, high, 0.0)
    coeffs = jnp.sum(kept, axis=0, keepdims=True)
    packed = jnp.concatenate([xb, jnp.where(row == 0, coeffs, 0.0).astype(BF16)], axis=0)
    for d in range(DEVS):
        out_ref[d] = packed


def prep_body(tiles_hbm, blocks_hbm, pairs_hbm, mask_hbm, near_pairs_hbm, near_mask_hbm, krylov_hbm,
              out_ref, tiles_ref, gather_ref, scatter_ref, gram_ref,
              pairs_ref, mask_ref, near_pairs_ref, near_mask_ref, krylov_ref, sems, tile_sem):
    fetched = pltpu.make_async_copy(tiles_hbm, tiles_ref, tile_sem)
    slots = blocks_hbm.shape[0]
    ends = (
        (blocks_hbm, out_ref.at[0:slots]),
        (pairs_hbm, pairs_ref),
        (mask_hbm, mask_ref),
        (near_pairs_hbm, near_pairs_ref),
        (near_mask_hbm, near_mask_ref),
        (krylov_hbm, krylov_ref),
    )
    copies = started(ends, sems)
    fetched.start()
    for copy in copies:
        copy.wait()
    i_row, j_row = pairs_ref[0:1, :], pairs_ref[1:2, :]
    row = iota((16, slots), 0)
    digits = jnp.zeros((16, slots), I32)
    for k, value in enumerate((i_row >> 7, i_row & 127, j_row >> 7, j_row & 127, mask_ref[...])):
        digits = jnp.where(row == k, value, digits)
    out_ref[slots : slots + 16, :] = jnp.zeros((16, out_ref.shape[1]), BF16)
    out_ref[slots : slots + 16, 0:slots] = small(digits)
    near = near_pairs_ref[...]
    live = near_mask_ref[...]
    near_slots = near.shape[1]
    row = iota((8, near_slots), 0)
    info = jnp.where(row == 0, near[0:1, :], jnp.where(row == 1, near[1:2, :], live))
    m = iota((64, near_slots), 0)
    pick = one_hot((m & 15) == iota((64, near_slots), 1))
    info_cols = mm_t(pick, small(info)).astype(I32)
    i_col, j_col = info_cols[:, 0:1], info_cols[:, 1:2]
    m = iota((64, 1), 0) >> 4
    c = jnp.where(m < 2, j_col, i_col)
    place = (c >> 2) * 16 + (c & 3) * 2 + (m & 1)
    gather_ref[...] = one_hot(iota((64, DEVS * 16), 1) == place)
    lane = iota((near_slots, 128), 1)
    pick = one_hot((lane & 15) == iota((near_slots, 128), 0))
    info_lanes = mm(small(info), pick).astype(I32)
    i_lane, j_lane, live_lane = (info_lanes[k : k + 1, :] for k in range(3))
    kind = (iota((1, 128), 1) >> 4) & 3
    used = (live_lane == 1) & ((kind < 2) | (i_lane != j_lane))
    target = jnp.where(kind < 2, i_lane, j_lane) * 2 + (kind & 1)
    target = jnp.where(used, target, -1)
    scatter_ref[...] = one_hot(iota((DEVS * 8, 128), 0) == target)
    rows = krylov_ref[...]
    gram = mm_exact(rows, rows, ((1,), (1,)))
    lane, row = iota((8, 128), 1) - 8, iota((8, 128), 0)
    inside = (lane >= 0) & (lane < 64)
    wide = mm_exact(gram, jnp.where(inside & ((lane & 7) == row), 1.0, 0.0), ((1,), (0,)))
    gram_ref[...] = jnp.sum(
        jnp.where(inside & ((lane >> 3) == row), wide, 0.0), axis=0, keepdims=True
    )
    fetched.wait()


def coeffs_body(gathered_ref, out_ref):
    rows = iota((DEVS, DEVS * 16), 0) * 16 + 8
    pick = one_hot(iota((DEVS, DEVS * 16), 1) == rows)
    out_ref[...] = mm(pick, gathered_ref[...]).astype(BF16)


def near_body(gathered_ref, gather_ref, scatter_ref, tiles_ref, out_ref):
    taken = mm(gather_ref[...], gathered_ref[...])
    right = jnp.concatenate([taken[0:16], taken[16:32]], axis=1).astype(BF16)
    left = jnp.concatenate([taken[32:48], taken[48:64]], axis=1).astype(BF16)
    slot = iota((16, 256), 0)
    forward = jnp.zeros((16, 256), F32)
    backward = jnp.zeros((16, 256), F32)
    for s in range(tiles_ref.shape[0]):
        tile = tiles_ref[s]
        forward = jnp.where(slot == s, mm_t(right, tile), forward)
        backward = jnp.where(slot == s, mm(left, tile), backward)
    values = jnp.concatenate(
        [forward[:, :128], forward[:, 128:], backward[:, :128], backward[:, 128:]], axis=0
    )
    out_ref[...] = mm(scatter_ref[...], jnp.concatenate(halves(values), axis=0))


def far_body(place_ref, near_ref, own_ref, before_ref, after_ref, own_coef_ref, before_coef_ref,
             after_coef_ref, out_ref):
    group = place_ref[0]
    bundles = (own_ref, before_ref, after_ref)
    slots = own_ref.shape[0] - 16
    total_slots = 3 * slots
    rows = [b[slots : slots + 16, 0:slots].astype(F32).astype(I32) for b in bundles]
    cols = jnp.concatenate([columns(r) for r in rows], axis=0)
    i_group, i_low, j_group, j_low, live = (cols[:, k : k + 1] for k in range(5))
    coeffs = jnp.concatenate([own_coef_ref[...], before_coef_ref[...], after_coef_ref[...]], axis=0)

    def gather(c_group, c_low):
        step = (c_group - group) & (GROUPS - 1)
        which = jnp.where(step == 0, 0, jnp.where(step == 1, 2, 1))
        n = c_low.shape[0]
        taken = mm(one_hot(iota((n, 3 * DEVS), 1) == which * DEVS + (c_low >> 2)), coeffs)
        return jnp.where((iota((n, 128), 1) >> 5) == (c_low & 3), taken, 0.0).astype(BF16)

    right = gather(j_group[0:slots], j_low[0:slots])
    left = gather(i_group, i_low)
    sub, lane = iota((128, 128), 0), iota((128, 128), 1)
    tiled = mm(right, one_hot((sub & 31) == (lane & 31)))
    forward = jnp.zeros((slots, 128), F32)
    backward = jnp.zeros((total_slots, 128), F32)
    for k in range(8):
        parts = [b[0:slots, k * 128 : k * 128 + 128] for b in bundles]
        part = jnp.concatenate(parts, axis=0).astype(F32)
        backward = backward + part * mm(left, one_hot((sub & 31) == 4 * k + (lane >> 5)))
        give = one_hot((lane & 31) == 4 * k + (sub >> 5))
        for piece in halves(part[0:slots] * tiled):
            forward = forward + mm(piece, give)
    backward = backward + pltpu.roll(backward, 64, 1)
    backward = backward + pltpu.roll(backward, 32, 1)
    lane_block = iota((total_slots, 128), 1) >> 5
    forward = jnp.where(
        (live[0:slots] == 1) & (lane_block[0:slots] == (i_low[0:slots] & 3)), forward, 0.0
    )
    different = (i_group != j_group) | (i_low != j_low)
    mine = (live == 1) & (j_group == group) & different
    backward = jnp.where(mine & (lane_block == (j_low & 3)), backward, 0.0)
    owner = iota((DEVS, slots), 0)
    total = jnp.zeros((DEVS, 128), F32)
    pick = one_hot(owner == (rows[0][1:2, :] >> 2))
    for part in halves(forward):
        total = total + mm(pick, part)
    for k in range(3):
        pick = one_hot(owner == (rows[k][3:4, :] >> 2))
        for part in halves(backward[k * slots : k * slots + slots]):
            total = total + mm(pick, part)
    row = iota((8, 128), 0)
    for d in range(DEVS):
        near = near_ref[d * 8 : d * 8 + 8, :]
        near_high = near.astype(BF16).astype(F32)
        far = total[d : d + 1, :]
        far_high = far.astype(BF16).astype(F32)
        tail = jnp.where(row == 0, far_high, jnp.where(row == 1, far - far_high, 0.0))
        out_ref[d] = jnp.concatenate([near_high, near - near_high, tail], axis=0).astype(BF16)


def product_body(pieces_ref, bases_ref, krylov_ref, gram_ref, product_ref, copies_ref):
    total = jnp.sum(pieces_ref[...].astype(F32), axis=0)
    near = total[0:8, :] + total[8:16, :]
    coef = (total[16:17, :] + total[17:18, :]).astype(BF16).astype(F32)
    row, lane = iota((8, 128), 0), iota((8, 128), 1)
    spread = jnp.where((lane >> 5) == (row >> 1), coef, 0.0).astype(BF16)
    low = mm(spread, bases_ref[:, :128])
    high = mm(spread, bases_ref[:, 128:])
    product = near + jnp.where((row & 1) == 0, low, high)
    product_ref[...] = product
    acc = jnp.zeros((8, 128), F32)
    for r in range(8):
        acc = acc + krylov_ref[:, r * 128 : r * 128 + 128] * product[r : r + 1, :]
    proj = jnp.sum(acc, axis=1, keepdims=True)
    square = jnp.sum(product * product, axis=1, keepdims=True)
    values = jnp.where(lane == row, proj, 0.0) + jnp.where(lane == 72, square, 0.0)
    payload = jnp.sum(values, axis=0, keepdims=True) + gram_ref[...]
    for d in range(copies_ref.shape[0]):
        copies_ref[d] = payload


def spread_body(pieces_ref, out_ref):
    total = jnp.sum(pieces_ref[...], axis=0)
    for d in range(out_ref.shape[0]):
        out_ref[d] = total


def last_body(count, pieces_ref, product_ref, krylov_ref, next_ref, proj_ref):
    total = jnp.sum(pieces_ref[...], axis=0)
    row, lane = iota((8, 128), 0), iota((8, 128), 1)
    proj = jnp.sum(jnp.where(lane == row, total, 0.0), axis=1, keepdims=True)
    inside = (lane >= 8) & (lane < 72)
    first = jnp.sum(jnp.where(inside & (((lane - 8) >> 3) == row), proj, 0.0), axis=0, keepdims=True)
    second = jnp.sum(jnp.where(inside & ((lane & 7) == row), proj, 0.0), axis=0, keepdims=True)
    lane = iota((1, 128), 1)
    terms = total * jnp.where(lane < 8, -2.0 * total, first * second)
    terms = jnp.where(lane == 72, total, jnp.where(lane < 72, terms, 0.0))
    length_sq = jnp.sum(terms, axis=1, keepdims=True)
    scale = 1.0 / jnp.sqrt(jnp.maximum(length_sq, 0.0) / count)
    for r in range(8):
        taken = jnp.sum(proj * krylov_ref[:, r * 128 : r * 128 + 128], axis=0, keepdims=True)
        next_ref[r : r + 1, :] = (product_ref[r : r + 1, :] - taken) * scale
    proj_ref[...] = total[:, 0:8]


def local(
    direction, krylov, bases, near_tiles, near_pairs, near_mask, far_blocks, far_pairs, far_mask
):
    panels = direction.shape[0]
    rank_rows = bases.reshape(-1, bases.shape[2])
    place = lax.axis_index("group").astype(I32)[None]
    slots, far_slots = near_tiles.shape[0], far_blocks.shape[0]

    copies = call(
        pack_body,
        sds((DEVS, 16, 128), BF16),
        [HBM, HBM],
        [pltpu.VMEM((8, 128), F32), pltpu.VMEM(rank_rows.shape, BF16), pltpu.SemaphoreType.DMA((2,))],
    )(direction.reshape(8, 128), rank_rows)
    gathered = to_all(copies, "dev").reshape(-1, 128)
    bundle, tiles, gather, scatter, gram = call(
        prep_body,
        [
            sds((far_slots + 16, far_blocks.shape[1]), BF16),
            pltpu.VMEM(near_tiles.shape, BF16),
            sds((64, DEVS * 16), BF16),
            sds((DEVS * 8, 128), BF16),
            sds((1, 128), F32),
        ],
        [HBM] * 7,
        [
            pltpu.VMEM((2, far_slots), I32),
            pltpu.VMEM((1, far_slots), I32),
            pltpu.VMEM((2, slots), I32),
            pltpu.VMEM((1, slots), I32),
            pltpu.VMEM(krylov.shape, F32),
            pltpu.SemaphoreType.DMA((6,)),
            pltpu.SemaphoreType.DMA,
        ],
    )(near_tiles, far_blocks, far_pairs.T, far_mask[None], near_pairs.T, near_mask[None], krylov)
    before, after = group_shift(bundle, 1), group_shift(bundle, -1)

    coeffs = call(coeffs_body, sds((DEVS, 128), BF16), [VMEM])(gathered)
    coeffs_before, coeffs_after = group_shift(coeffs, 1), group_shift(coeffs, -1)
    near = call(near_body, sds((DEVS * 8, 128), F32), [VMEM] * 4)(gathered, gather, scatter, tiles)
    parts = call(far_body, sds((DEVS, 24, 128), BF16), [SMEM] + [VMEM] * 7)(
        place, near, bundle, before, after, coeffs, coeffs_before, coeffs_after
    )
    product, copies = call(
        product_body, [sds((8, 128), F32), sds((GROUPS, 1, 128), F32)], [VMEM] * 4
    )(to_all(parts, "dev"), rank_rows, krylov, gram)
    copies = call(spread_body, sds((DEVS, 1, 128), F32), [VMEM])(to_all(copies, "group"))
    pieces = to_all(copies, "dev")
    count = float(panels * DEVS * GROUPS)

    def finish(*refs):
        last_body(count, *refs)

    next_vector, projections = call(finish, [sds((8, 128), F32), sds((1, 8), F32)], [VMEM] * 3)(
        pieces, product, krylov
    )
    return (next_vector.reshape(-1), projections.reshape(-1))


def solution(mesh):
    in_specs = (
        P(("group", "dev")),
        P(None, ("group", "dev")),
        P(("group", "dev"), None, None),
        P(("group", "dev"), None, None),
        P(("group", "dev"), None),
        P(("group", "dev")),
        P(("group", "dev"), None),
        P(("group", "dev"), None),
        P(("group", "dev")),
    )
    out_specs = (P(("group", "dev")), P())
    return jax.shard_map(local, mesh=mesh, in_specs=in_specs, out_specs=out_specs, check_vma=False)
```

time: 84.9 us -> 75.2 us (0.89)
  blocking collectives: 48 us -> 40.7 us
  Pallas kernels: 9.78 us -> 6.72 us
  waiting for transfers between devices: 5.29 us -> 7.56 us
  starting transfers between devices: 20.8 us -> 19.1 us
    all_to_all x2 -> x3, blocking collectives: 48 us -> 40.7 us  [to_all(): return lax.all_to_all(value, axis, split_axis=0, concat_axis=0, tiled=True)]
    ppermute x4, starting transfers between devices: 10.8 us -> 5.4 us  [group_shift(): lax.ppermute(value, 'group', [(g, (g + step) % GROUPS) for g in range(GRO...]
    all_to_all x1, starting transfers between devices: 10 us -> 13.7 us  [to_all(): return lax.all_to_all(value, axis, split_axis=0, concat_axis=0, tiled=True)]
    all_to_all x1, waiting for transfers between devices: 1.9 us -> 5.55 us  [to_all(): return lax.all_to_all(value, axis, split_axis=0, concat_axis=0, tiled=True)]
    pallas_call x6 -> x8, Pallas kernels: 9.78 us -> 6.72 us  [run(): kernel(*(pltpu.with_memory_space_constraint(arg, pltpu.HBM) if spec is HB...]
    ppermute x4, waiting for transfers between devices: 3.38 us -> 2.01 us  [group_shift(): lax.ppermute(value, 'group', [(g, (g + step) % GROUPS) for g in range(GRO...]
  transfers between devices with their start and end apart: 5 -> 5, of which waited for: 5 -> 2; matrix products, arithmetic and copies ran while one was open for 0% -> 0% of each run, Pallas kernels for 2% -> 4%
where the time goes in v2:
time: 75.2 us; the launch traced here: 74.8 us
  blocking collectives  40.7 us (54%)
  starting transfers between devices  19.1 us (25%)
  waiting for transfers between devices  7.56 us (10%)
  Pallas kernels  6.72 us (9%)
    all_to_all x3, blocking collectives, to_all(): return lax.all_to_all(value, axis, split_axis=0, concat_axis=0, tiled=True)  40.7 us
    all_to_all x1, starting transfers between devices, to_all(): return lax.all_to_all(value, axis, split_axis=0, concat_axis=0, tiled=True)  13.7 us
    pallas_call x8, Pallas kernels, run(): kernel(*(pltpu.with_memory_space_constraint(arg, pltpu.HBM) if spec is HB...  6.72 us
    all_to_all x1, waiting for transfers between devices, to_all(): return lax.all_to_all(value, axis, split_axis=0, concat_axis=0, tiled=True)  5.55 us
    ppermute x4, starting transfers between devices, group_shift(): lax.ppermute(value, 'group', [(g, (g + step) % GROUPS) for g in range(GRO...  5.4 us
    ppermute x4, waiting for transfers between devices, group_shift(): lax.ppermute(value, 'group', [(g, (g + step) % GROUPS) for g in range(GRO...  2.01 us
  transfers between devices with their start and end apart: 5, of which 2 were waited for; matrix products, arithmetic and copies ran while one was open for 0% of the time, Pallas kernels for 4%

profile of v2, /device:TPU:1, one launch (start us, length us, event | category | flops | bytes accessed | tf_op | source)
XLA Modules:
  0.0 74.8 jit_solution(9287376927963889107)
XLA Ops:
  0.6 1.7 %shard_map.104 = bf16[32,16,128]{2,1,0:T(8,128)(2,1)} custom-call(f32[8,128]{1,0:T(8,128)} %bitcast.14, bf16[128,256]{1,0:T(8,128)(2,1)} %bitcast.12), custom_call_target="tpu_custom_call" | custom-call | tf_op jit(solution)/shard_map/pallas_call | solution.py:30
  2.3 13.7 %all-to-all-start = ((bf16[32,16,128]{2,1,0:T(8,128)(2,1)}), bf16[32,16,128]{2,1,0:T(8,128)(2,1)S(1)}, u32[]{:S(2)}, u32[]{:S(2)}) async-start(bf16[32,16,128]{2,1,0:T(8,128)(2,1)} %shard_map.104), calls=%async_computation | async-start | bytes 262144 | tf_op jit(solution)/shard_map/all_to_all | solution.py:78
  16.1 1.6 %shard_map.105 = (bf16[80,1024]{1,0:T(8,128)(2,1)S(1)}, bf16[12,256,256]{2,1,0:T(8,128)(2,1)S(1)}, bf16[64,512]{1,0:T(8,128)(2,1)S(1)}, bf16[256,128]{1,0:T(8,128)(2,1)S(1)}, f32[1,128]{1,0:T(1,128)S(1)}) custom-call(bf16[12,256,256]{2,1,0:T(8,128)(2,1)} %tiles_hbm.1, bf16[64,1024]{1,0:T(8,128)(2,1)} %blocks_hbm.1, s32[2,64]{1,0:T(2,128)} %bitcast.15, ...), custom_call_target="tpu_custom_call" | custom-call | tf_op jit(solution)/shard_map/pallas_call | solution.py:30
  17.7 2.1 %collective-permute-start = (bf16[80,1024]{1,0:T(8,128)(2,1)S(1)}, bf16[80,1024]{1,0:T(8,128)(2,1)S(1)}, u32[]{:S(2)}, u32[]{:S(2)}) collective-permute-start(bf16[80,1024]{1,0:T(8,128)(2,1)S(1)} %get-tuple-element.14.own_ref), channel_id=1, source_target_pairs={{0,32},{32,64},{64,96},{96,128},{128,160},{160,192},{192,224},{224... | collective-permute-start | bytes 491528 | tf_op jit(solution)/shard_map/ppermute | solution.py:82
  19.9 0.0 collective-permute-start.1
  19.9 5.5 %all-to-all-done = bf16[32,16,128]{2,1,0:T(8,128)(2,1)S(1)} async-done(((bf16[32,16,128]{2,1,0:T(8,128)(2,1)}), bf16[32,16,128]{2,1,0:T(8,128)(2,1)S(1)}, u32[]{:S(2)}, u32[]{:S(2)}) %all-to-all-start) | async-done | bytes 131104 | tf_op jit(solution)/shard_map/all_to_all | solution.py:78
  25.4 0.1 shard_map.107.own_coef_ref
  25.5 3.2 %collective-permute-start.2 = (bf16[32,128]{1,0:T(8,128)(2,1)S(1)}, bf16[32,128]{1,0:T(8,128)(2,1)S(1)}, u32[]{:S(2)}, u32[]{:S(2)}) collective-permute-start(bf16[32,128]{1,0:T(8,128)(2,1)S(1)} %shard_map.107.own_coef_ref), channel_id=1, source_target_pairs={{0,32},{32,64},{64,96},{96,128},{128,160},{160,192},{192,224},{224... | collective-permute-start | bytes 24584 | tf_op jit(solution)/shard_map/ppermute | solution.py:82
  28.8 0.0 collective-permute-start.3
  28.8 0.0 copy-start
  28.8 0.0 copy-start.1
  28.8 1.0 %shard_map.106.near_ref = f32[256,128]{1,0:T(8,128)S(1)} custom-call(bf16[512,128]{1,0:T(8,128)(2,1)S(1)} %bitcast.11, bf16[64,512]{1,0:T(8,128)(2,1)S(1)} %get-tuple-element.11.gather_ref, bf16[256,128]{1,0:T(8,128)(2,1)S(1)} %get-tuple-element.12.scatter_ref, bf16[12,256,256]{2,1,0:T(8,128)(2,1)S(1)} %get-tuple-element.13.tiles_ref), custom_call_target="tpu_custom_call" | custom-call | tf_op jit(solution)/shard_map/pallas_call | solution.py:30
  29.8 0.0 collective-permute-done.before_ref
  29.8 0.0 collective-permute-done.1.after_ref
  29.9 0.0 collective-permute-done.2.before_coef_ref
  29.9 2.0 %collective-permute-done.3.after_coef_ref = bf16[32,128]{1,0:T(8,128)(2,1)S(1)} collective-permute-done((bf16[32,128]{1,0:T(8,128)(2,1)S(1)}, bf16[32,128]{1,0:T(8,128)(2,1)S(1)}, u32[]{:S(2)}, u32[]{:S(2)}) %collective-permute-start.3) | collective-permute-done | bytes 8224 | tf_op jit(solution)/shard_map/ppermute | solution.py:82
  31.9 1.1 %shard_map.108 = bf16[32,24,128]{2,1,0:T(8,128)(2,1)S(1)} custom-call(s32[1]{0:T(128)} %bitcast.place_ref, f32[256,128]{1,0:T(8,128)S(1)} %shard_map.106.near_ref, bf16[80,1024]{1,0:T(8,128)(2,1)S(1)} %get-tuple-element.14.own_ref, bf16[80,1024]{1,0:T(8,128)(2,1)S(1)} %collective-permute-done.before_ref, ...), custom_call_target="tpu_custom_call" | custom-call | tf_op jit(solution)/shard_map/pallas_call | solution.py:30
  33.0 13.6 %all_to_all.20.pieces_ref = bf16[32,24,128]{2,1,0:T(8,128)(2,1)S(1)} all-to-all(bf16[32,24,128]{2,1,0:T(8,128)(2,1)S(1)} %shard_map.108), channel_id=1, replica_groups=mesh['group'=16,'dev'=32] {'dev'}, dimensions={0} | all-to-all | bytes 393216 | tf_op jit(solution)/shard_map/all_to_all | solution.py:78
  46.6 0.0 copy-done
  46.6 0.0 copy-done.1
  46.6 0.3 shard_map.109
  46.9 15.5 %all_to_all.21.pieces_ref = f32[16,1,128]{2,1,0:T(1,128)S(1)} all-to-all(f32[16,1,128]{2,1,0:T(1,128)S(1)} %get-tuple-element.16), channel_id=1, replica_groups=mesh['group'=16,'dev'=32] {'group'}, dimensions={0} | all-to-all | bytes 16384 | tf_op jit(solution)/shard_map/all_to_all | solution.py:78
  62.4 11.6 %all_to_all.22.refs_0_ = f32[32,1,128]{2,1,0:T(1,128)S(1)} all-to-all(f32[32,1,128]{2,1,0:T(1,128)S(1)} %shard_map.110), channel_id=1, replica_groups=mesh['group'=16,'dev'=32] {'dev'}, dimensions={0} | all-to-all | bytes 32768 | tf_op jit(solution)/shard_map/all_to_all | solution.py:78
  74.0 0.8 %shard_map.111 = (f32[8,128]{1,0:T(8,128)}, f32[1,8]{1,0:T(1,128)}) custom-call(f32[32,1,128]{2,1,0:T(1,128)S(1)} %all_to_all.22.refs_0_, f32[8,128]{1,0:T(8,128)S(1)} %get-tuple-element.17.refs_1_, f32[8,1024]{1,0:T(8,128)S(1)} %copy-done), custom_call_target="tpu_custom_call" | custom-call | tf_op jit(solution)/shard_map/pallas_call | solution.py:30
  (1 shorter events, 0.0 us)
Async XLA Ops:
  2.3 23.1 %all-to-all-start = ((bf16[32,16,128]{2,1,0:T(8,128)(2,1)}), bf16[32,16,128]{2,1,0:T(8,128)(2,1)S(1)}, u32[]{:S(2)}, u32[]{:S(2)}) async-start(bf16[32,16,128]{2,1,0:T(8,128)(2,1)} %shard_map.104), calls=%async_computation | async-start | bytes 262144 | tf_op jit(solution)/shard_map/all_to_all | solution.py:78
  17.7 12.1 %collective-permute-start = (bf16[80,1024]{1,0:T(8,128)(2,1)S(1)}, bf16[80,1024]{1,0:T(8,128)(2,1)S(1)}, u32[]{:S(2)}, u32[]{:S(2)}) collective-permute-start(bf16[80,1024]{1,0:T(8,128)(2,1)S(1)} %get-tuple-element.14.own_ref), channel_id=1, source_target_pairs={{0,32},{32,64},{64,96},{96,128},{128,160},{160,192},{192,224},{224... | collective-permute-start | bytes 491528 | tf_op jit(solution)/shard_map/ppermute | solution.py:82
  19.9 10.0 %collective-permute-start.1 = (bf16[80,1024]{1,0:T(8,128)(2,1)S(1)}, bf16[80,1024]{1,0:T(8,128)(2,1)S(1)}, u32[]{:S(2)}, u32[]{:S(2)}) collective-permute-start(bf16[80,1024]{1,0:T(8,128)(2,1)S(1)} %get-tuple-element.14.own_ref), channel_id=1, source_target_pairs={{0,480},{32,0},{64,32},{96,64},{128,96},{160,128},{192,160},{224,1... | collective-permute-start | bytes 491528 | tf_op jit(solution)/shard_map/ppermute | solution.py:82
  25.5 4.3 %collective-permute-start.2 = (bf16[32,128]{1,0:T(8,128)(2,1)S(1)}, bf16[32,128]{1,0:T(8,128)(2,1)S(1)}, u32[]{:S(2)}, u32[]{:S(2)}) collective-permute-start(bf16[32,128]{1,0:T(8,128)(2,1)S(1)} %shard_map.107.own_coef_ref), channel_id=1, source_target_pairs={{0,32},{32,64},{64,96},{96,128},{128,160},{160,192},{192,224},{224... | collective-permute-start | bytes 24584 | tf_op jit(solution)/shard_map/ppermute | solution.py:82
  28.8 3.1 %collective-permute-start.3 = (bf16[32,128]{1,0:T(8,128)(2,1)S(1)}, bf16[32,128]{1,0:T(8,128)(2,1)S(1)}, u32[]{:S(2)}, u32[]{:S(2)}) collective-permute-start(bf16[32,128]{1,0:T(8,128)(2,1)S(1)} %shard_map.107.own_coef_ref), channel_id=1, source_target_pairs={{0,480},{32,0},{64,32},{96,64},{128,96},{160,128},{192,160},{224,1... | collective-permute-start | bytes 24584 | tf_op jit(solution)/shard_map/ppermute | solution.py:82
  28.8 17.8 %copy-start = (f32[8,1024]{1,0:T(8,128)S(1)}, f32[8,1024]{1,0:T(8,128)}, u32[]{:S(2)}) copy-start(f32[8,1024]{1,0:T(8,128)} %refs_2_.1) | copy-start | bytes 98308
  28.8 17.8 %copy-start.1 = (bf16[4,32,256]{2,1,0:T(8,128)(2,1)S(1)}, bf16[4,32,256]{2,1,0:T(8,128)(2,1)}, u32[]{:S(2)}) copy-start(bf16[4,32,256]{2,1,0:T(8,128)(2,1)} %param.11) | copy-start | bytes 196612

commit v3 on v2

--- a/solution.py
+++ b/solution.py
@@ -74,8 +74,10 @@
     return mm_t(same, small(rows)).astype(I32)
 
 
-def to_all(value, axis):
-    return lax.all_to_all(value, axis, split_axis=0, concat_axis=0, tiled=True)
+def to_all(value, axis, index_groups=None):
+    return lax.all_to_all(
+        value, axis, split_axis=0, concat_axis=0, tiled=True, axis_index_groups=index_groups
+    )
 
 
 def group_shift(value, step):
@@ -106,7 +108,7 @@
 
 
 def prep_body(tiles_hbm, blocks_hbm, pairs_hbm, mask_hbm, near_pairs_hbm, near_mask_hbm, krylov_hbm,
-              out_ref, tiles_ref, gather_ref, scatter_ref, gram_ref,
+              out_ref, tiles_ref, gather_ref, scatter_ref, take_ref, give_ref, gram_ref,
               pairs_ref, mask_ref, near_pairs_ref, near_mask_ref, krylov_ref, sems, tile_sem):
     fetched = pltpu.make_async_copy(tiles_hbm, tiles_ref, tile_sem)
     slots = blocks_hbm.shape[0]
@@ -151,6 +153,8 @@
     target = jnp.where(kind < 2, i_lane, j_lane) * 2 + (kind & 1)
     target = jnp.where(used, target, -1)
     scatter_ref[...] = one_hot(iota((DEVS * 8, 128), 0) == target)
+    take_ref[...] = one_hot((iota((128, 1024), 0) & 31) == (iota((128, 1024), 1) >> 5))
+    give_ref[...] = one_hot((iota((1024, 128), 0) >> 5) == (iota((1024, 128), 1) & 31))
     rows = krylov_ref[...]
     gram = mm_exact(rows, rows, ((1,), (1,)))
     lane, row = iota((8, 128), 1) - 8, iota((8, 128), 0)
@@ -185,55 +189,93 @@
     out_ref[...] = mm(scatter_ref[...], jnp.concatenate(halves(values), axis=0))
 
 
-def far_body(place_ref, near_ref, own_ref, before_ref, after_ref, own_coef_ref, before_coef_ref,
-             after_coef_ref, out_ref):
-    group = place_ref[0]
-    bundles = (own_ref, before_ref, after_ref)
-    slots = own_ref.shape[0] - 16
-    total_slots = 3 * slots
-    rows = [b[slots : slots + 16, 0:slots].astype(F32).astype(I32) for b in bundles]
-    cols = jnp.concatenate([columns(r) for r in rows], axis=0)
-    i_group, i_low, j_group, j_low, live = (cols[:, k : k + 1] for k in range(5))
-    coeffs = jnp.concatenate([own_coef_ref[...], before_coef_ref[...], after_coef_ref[...]], axis=0)
-
-    def gather(c_group, c_low):
-        step = (c_group - group) & (GROUPS - 1)
-        which = jnp.where(step == 0, 0, jnp.where(step == 1, 2, 1))
-        n = c_low.shape[0]
-        taken = mm(one_hot(iota((n, 3 * DEVS), 1) == which * DEVS + (c_low >> 2)), coeffs)
-        return jnp.where((iota((n, 128), 1) >> 5) == (c_low & 3), taken, 0.0).astype(BF16)
-
-    right = gather(j_group[0:slots], j_low[0:slots])
-    left = gather(i_group, i_low)
+def slot_info(bundle_ref):
+    slots = bundle_ref.shape[0] - 16
+    rows = bundle_ref[slots : slots + 16, 0:slots].astype(F32).astype(I32)
+    return rows, columns(rows)
+
+
+def picked(index, low, coeffs):
+    n = index.shape[0]
+    taken = mm(one_hot(iota((n, coeffs.shape[0]), 1) == index), coeffs)
+    return jnp.where((iota((n, 128), 1) >> 5) == (low & 3), taken, 0.0).astype(BF16)
+
+
+def block_columns(bundle_ref, k):
+    return bundle_ref[0 : bundle_ref.shape[0] - 16, k * 128 : k * 128 + 128].astype(F32)
+
+
+def forward_sums(bundle_ref, right, give_ref):
     sub, lane = iota((128, 128), 0), iota((128, 128), 1)
     tiled = mm(right, one_hot((sub & 31) == (lane & 31)))
-    forward = jnp.zeros((slots, 128), F32)
-    backward = jnp.zeros((total_slots, 128), F32)
+    total = jnp.zeros(tiled.shape, F32)
     for k in range(8):
-        parts = [b[0:slots, k * 128 : k * 128 + 128] for b in bundles]
-        part = jnp.concatenate(parts, axis=0).astype(F32)
-        backward = backward + part * mm(left, one_hot((sub & 31) == 4 * k + (lane >> 5)))
-        give = one_hot((lane & 31) == 4 * k + (sub >> 5))
-        for piece in halves(part[0:slots] * tiled):
-            forward = forward + mm(piece, give)
-    backward = backward + pltpu.roll(backward, 64, 1)
-    backward = backward + pltpu.roll(backward, 32, 1)
-    lane_block = iota((total_slots, 128), 1) >> 5
-    forward = jnp.where(
-        (live[0:slots] == 1) & (lane_block[0:slots] == (i_low[0:slots] & 3)), forward, 0.0
-    )
-    different = (i_group != j_group) | (i_low != j_low)
-    mine = (live == 1) & (j_group == group) & different
-    backward = jnp.where(mine & (lane_block == (j_low & 3)), backward, 0.0)
-    owner = iota((DEVS, slots), 0)
-    total = jnp.zeros((DEVS, 128), F32)
-    pick = one_hot(owner == (rows[0][1:2, :] >> 2))
-    for part in halves(forward):
-        total = total + mm(pick, part)
-    for k in range(3):
-        pick = one_hot(owner == (rows[k][3:4, :] >> 2))
-        for part in halves(backward[k * slots : k * slots + slots]):
-            total = total + mm(pick, part)
+        for piece in halves(block_columns(bundle_ref, k) * tiled):
+            total = total + mm(piece, give_ref[k * 128 : k * 128 + 128, :])
+    return total
+
+
+def backward_sums(bundle_refs, left, take_ref):
+    total = jnp.zeros(left.shape, F32)
+    for k in range(8):
+        blocks = jnp.concatenate([block_columns(ref, k) for ref in bundle_refs], axis=0)
+        total = total + blocks * mm(left, take_ref[:, k * 128 : k * 128 + 128])
+    total = total + pltpu.roll(total, 64, 1)
+    return total + pltpu.roll(total, 32, 1)
+
+
+def in_lanes(value, keep, low):
+    lane_block = iota(value.shape, 1) >> 5
+    return jnp.where(keep & (lane_block == (low & 3)), value, 0.0)
+
+
+def owners_sum(low_row, value):
+    pick = one_hot(iota((DEVS, low_row.shape[1]), 0) == (low_row >> 2))
+    high, low = halves(value)
+    return mm(pick, high) + mm(pick, low)
+
+
+def far_own_body(place_ref, bundle_ref, coef_ref, take_ref, give_ref, out_ref):
+    group = place_ref[0]
+    coeffs = coef_ref[...]
+    rows, cols = slot_info(bundle_ref)
+    i_low, j_group, j_low, live = (cols[:, k : k + 1] for k in (1, 2, 3, 4))
+    here = j_group == group
+    right = picked(jnp.where(here, j_low >> 2, -1), j_low, coeffs)
+    left = picked(i_low >> 2, i_low, coeffs)
+    forward = in_lanes(forward_sums(bundle_ref, right, give_ref), live == 1, i_low)
+    backward = in_lanes(
+        backward_sums((bundle_ref,), left, take_ref),
+        (live == 1) & here & (i_low != j_low),
+        j_low,
+    )
+    out_ref[...] = owners_sum(rows[1:2, :], forward) + owners_sum(rows[3:4, :], backward)
+
+
+def far_body(place_ref, near_ref, far_ref, own_ref, before_ref, after_ref, before_coef_ref,
+             after_coef_ref, take_ref, give_ref, out_ref):
+    group = place_ref[0]
+    both = jnp.concatenate([before_coef_ref[...], after_coef_ref[...]], axis=0)
+    rows, cols = slot_info(own_ref)
+    i_low, j_group, j_low, live = (cols[:, k : k + 1] for k in (1, 2, 3, 4))
+    step = (j_group - group) & (GROUPS - 1)
+    index = jnp.where(step == 0, -1, jnp.where(step == 1, DEVS, 0) + (j_low >> 2))
+    right = picked(index, j_low, both)
+    forward = in_lanes(forward_sums(own_ref, right, give_ref), live == 1, i_low)
+    total = far_ref[...] + owners_sum(rows[1:2, :], forward)
+    infos = [slot_info(ref) for ref in (before_ref, after_ref)]
+    cols = jnp.concatenate([cols for _, cols in infos], axis=0)
+    i_low, j_group, j_low, live = (cols[:, k : k + 1] for k in (1, 2, 3, 4))
+    slots = rows.shape[1]
+    side = jnp.where(iota((2 * slots, 1), 0) < slots, 0, DEVS)
+    left = picked(side + (i_low >> 2), i_low, both)
+    backward = in_lanes(
+        backward_sums((before_ref, after_ref), left, take_ref),
+        (live == 1) & (j_group == group),
+        j_low,
+    )
+    for k in range(2):
+        total = total + owners_sum(infos[k][0][3:4, :], backward[k * slots : k * slots + slots])
     row = iota((8, 128), 0)
     for d in range(DEVS):
         near = near_ref[d * 8 : d * 8 + 8, :]
@@ -289,6 +331,16 @@
     proj_ref[...] = total[:, 0:8]
 
 
+def all_reduce_sets():
+    def number(y, core, z, x_high, x_low):
+        return (y * 2 + core) * DEVS + z * NX + x_high * 2 + x_low
+
+    ys, zs, bits = range(NY), range(NZ), range(2)
+    first = [[number(y, c, z, h, l) for y in ys for h in bits] for c in bits for z in zs for l in bits]
+    second = [[number(y, c, z, h, l) for c in bits for z in zs for l in bits] for y in ys for h in bits]
+    return first, second
+
+
 def local(
     direction, krylov, bases, near_tiles, near_pairs, near_mask, far_blocks, far_pairs, far_mask
 ):
@@ -304,13 +356,15 @@
         [pltpu.VMEM((8, 128), F32), pltpu.VMEM(rank_rows.shape, BF16), pltpu.SemaphoreType.DMA((2,))],
     )(direction.reshape(8, 128), rank_rows)
     gathered = to_all(copies, "dev").reshape(-1, 128)
-    bundle, tiles, gather, scatter, gram = call(
+    bundle, tiles, gather, scatter, take, give, gram = call(
         prep_body,
         [
             sds((far_slots + 16, far_blocks.shape[1]), BF16),
             pltpu.VMEM(near_tiles.shape, BF16),
             sds((64, DEVS * 16), BF16),
             sds((DEVS * 8, 128), BF16),
+            pltpu.VMEM((128, 1024), BF16),
+            pltpu.VMEM((1024, 128), BF16),
             sds((1, 128), F32),
         ],
         [HBM] * 7,
@@ -329,14 +383,20 @@
     coeffs = call(coeffs_body, sds((DEVS, 128), BF16), [VMEM])(gathered)
     coeffs_before, coeffs_after = group_shift(coeffs, 1), group_shift(coeffs, -1)
     near = call(near_body, sds((DEVS * 8, 128), F32), [VMEM] * 4)(gathered, gather, scatter, tiles)
-    parts = call(far_body, sds((DEVS, 24, 128), BF16), [SMEM] + [VMEM] * 7)(
-        place, near, bundle, before, after, coeffs, coeffs_before, coeffs_after
+    far = call(far_own_body, sds((DEVS, 128), F32), [SMEM] + [VMEM] * 4)(
+        place, bundle, coeffs, take, give
+    )
+    parts = call(far_body, sds((DEVS, 24, 128), BF16), [SMEM] + [VMEM] * 9)(
+        place, near, far, bundle, before, after, coeffs_before, coeffs_after, take, give
     )
     product, copies = call(
         product_body, [sds((8, 128), F32), sds((GROUPS, 1, 128), F32)], [VMEM] * 4
     )(to_all(parts, "dev"), rank_rows, krylov, gram)
-    copies = call(spread_body, sds((DEVS, 1, 128), F32), [VMEM])(to_all(copies, "group"))
-    pieces = to_all(copies, "dev")
+    first, second = all_reduce_sets()
+    copies = call(spread_body, sds((DEVS, 1, 128), F32), [VMEM])(
+        to_all(copies, ("group", "dev"), first)
+    )
+    pieces = to_all(copies, ("group", "dev"), second)
     count = float(panels * DEVS * GROUPS)
 
     def finish(*refs):

time: 75.2 us -> 79 us (1.051)
  blocking collectives: 40.7 us -> 43.9 us
  Pallas kernels: 6.72 us -> 8.46 us
  waiting for transfers between devices: 7.56 us -> 6.46 us
    all_to_all x3, blocking collectives: 40.7 us -> 43.9 us  [to_all(): lax.all_to_all(value, axis, split_axis=0, concat_axis=0, tiled=True, axis...]
    pallas_call x8 -> x9, Pallas kernels: 6.72 us -> 8.46 us  [run(): kernel(*(pltpu.with_memory_space_constraint(arg, pltpu.HBM) if spec is HB...]
    ppermute x4, waiting for transfers between devices: 2.01 us -> 0.91 us  [group_shift(): lax.ppermute(value, 'group', [(g, (g + step) % GROUPS) for g in range(GRO...]
  transfers between devices with their start and end apart: 5 -> 5, of which waited for: 2 -> 2; matrix products, arithmetic and copies ran while one was open for 0% -> 0% of each run, Pallas kernels for 4% -> 5%
where the time goes in v3:
time: 79 us; the launch traced here: 78.7 us
  blocking collectives  43.9 us (56%)
  starting transfers between devices  19.1 us (24%)
  Pallas kernels  8.46 us (11%)
  waiting for transfers between devices  6.46 us (8%)
    all_to_all x3, blocking collectives, to_all(): lax.all_to_all(value, axis, split_axis=0, concat_axis=0, tiled=True, axis...  43.9 us
    all_to_all x1, starting transfers between devices, to_all(): lax.all_to_all(value, axis, split_axis=0, concat_axis=0, tiled=True, axis...  13.7 us
    pallas_call x9, Pallas kernels, run(): kernel(*(pltpu.with_memory_space_constraint(arg, pltpu.HBM) if spec is HB...  8.46 us
    all_to_all x1, waiting for transfers between devices, to_all(): lax.all_to_all(value, axis, split_axis=0, concat_axis=0, tiled=True, axis...  5.55 us
    ppermute x4, starting transfers between devices, group_shift(): lax.ppermute(value, 'group', [(g, (g + step) % GROUPS) for g in range(GRO...  5.4 us
  transfers between devices with their start and end apart: 5, of which 2 were waited for; matrix products, arithmetic and copies ran while one was open for 0% of the time, Pallas kernels for 5%

profile of v3, /device:TPU:1, one launch (start us, length us, event | category | flops | bytes accessed | tf_op | source)
XLA Modules:
  0.0 78.7 jit_solution(9636479865468618170)
XLA Ops:
  0.6 1.7 %shard_map.104 = bf16[32,16,128]{2,1,0:T(8,128)(2,1)} custom-call(f32[8,128]{1,0:T(8,128)} %bitcast.14, bf16[128,256]{1,0:T(8,128)(2,1)} %bitcast.12), custom_call_target="tpu_custom_call" | custom-call | tf_op jit(solution)/shard_map/pallas_call | solution.py:30
  2.3 13.7 %all-to-all-start = ((bf16[32,16,128]{2,1,0:T(8,128)(2,1)}), bf16[32,16,128]{2,1,0:T(8,128)(2,1)S(1)}, u32[]{:S(2)}, u32[]{:S(2)}) async-start(bf16[32,16,128]{2,1,0:T(8,128)(2,1)} %shard_map.104), calls=%async_computation | async-start | bytes 262144 | tf_op jit(solution)/shard_map/all_to_all | solution.py:78
  16.1 1.6 %shard_map.105 = (bf16[80,1024]{1,0:T(8,128)(2,1)S(1)}, bf16[12,256,256]{2,1,0:T(8,128)(2,1)S(1)}, bf16[64,512]{1,0:T(8,128)(2,1)S(1)}, bf16[256,128]{1,0:T(8,12...) custom-call(bf16[12,256,256]{2,1,0:T(8,128)(2,1)} %tiles_hbm.1, ...), custom_call_target="tpu_custom_call" | custom-call | tf_op jit(solution)/shard_map/pallas_call | solution.py:30
  17.7 2.1 %collective-permute-start = (bf16[80,1024]{1,0:T(8,128)(2,1)S(1)}, bf16[80,1024]{1,0:T(8,128)(2,1)S(1)}, u32[]{:S(2)}, u32[]{:S(2)}) collective-permute-start(bf16[80,1024]{1,0:T(8,128)(2,1)S(1)} %get-tuple-element.16.bundle_ref.own_ref), channel_id=1, source_target_pairs={{0,32},{32,64},{64,96},{96,128},{128,160},{160,192},{192,224},{224... | collective-permute-start | bytes 491528 | tf_op jit(solution)/shard_map/ppermute | solution.py:84
  19.9 0.0 collective-permute-start.1
  19.9 5.5 %all-to-all-done = bf16[32,16,128]{2,1,0:T(8,128)(2,1)S(1)} async-done(((bf16[32,16,128]{2,1,0:T(8,128)(2,1)}), bf16[32,16,128]{2,1,0:T(8,128)(2,1)S(1)}, u32[]{:S(2)}, u32[]{:S(2)}) %all-to-all-start) | async-done | bytes 131104 | tf_op jit(solution)/shard_map/all_to_all | solution.py:78
  25.4 0.1 shard_map.107.coef_ref
  25.5 3.2 %collective-permute-start.2 = (bf16[32,128]{1,0:T(8,128)(2,1)S(1)}, bf16[32,128]{1,0:T(8,128)(2,1)S(1)}, u32[]{:S(2)}, u32[]{:S(2)}) collective-permute-start(bf16[32,128]{1,0:T(8,128)(2,1)S(1)} %shard_map.107.coef_ref), channel_id=1, source_target_pairs={{0,32},{32,64},{64,96},{96,128},{128,160},{160,192},{192,224},{224... | collective-permute-start | bytes 24584 | tf_op jit(solution)/shard_map/ppermute | solution.py:84
  28.8 0.0 collective-permute-start.3
  28.8 1.0 %shard_map.106.near_ref = f32[256,128]{1,0:T(8,128)S(1)} custom-call(bf16[512,128]{1,0:T(8,128)(2,1)S(1)} %bitcast.11, bf16[64,512]{1,0:T(8,128)(2,1)S(1)} %get-tuple-element.13.gather_ref, bf16[256,128]{1,0:T(8,128)(2,1)S(1)} %get-tuple-element.14.scatter_ref, bf16[12,256,256]{2,1,0:T(8,128)(2,1)S(1)} %get-tuple-element.15.tiles_ref), custom_call_target="tpu_custom_call" | custom-call | tf_op jit(solution)/shard_map/pallas_call | solution.py:30
  29.8 0.0 copy-start
  29.8 0.0 copy-start.1
  29.9 1.1 %shard_map.108.far_ref = f32[32,128]{1,0:T(8,128)S(1)} custom-call(s32[1]{0:T(128)} %bitcast.place_ref, bf16[80,1024]{1,0:T(8,128)(2,1)S(1)} %get-tuple-element.16.bundle_ref.own_ref, bf16[32,128]{1,0:T(8,128)(2,1)S(1)} %shard_map.107.coef_ref, bf16[128,1024]{1,0:T(8,128)(2,1)S(1)} %get-tuple-element.17.take_ref, ...), custom_call_target="tpu_custom_call" | custom-call | tf_op jit(solution)/shard_map/pallas_call | solution.py:30
  30.9 0.0 collective-permute-done.before_ref
  31.0 0.0 collective-permute-done.1.after_ref
  31.0 0.0 collective-permute-done.2.before_coef_ref
  31.0 0.9 %collective-permute-done.3.after_coef_ref = bf16[32,128]{1,0:T(8,128)(2,1)S(1)} collective-permute-done((bf16[32,128]{1,0:T(8,128)(2,1)S(1)}, bf16[32,128]{1,0:T(8,128)(2,1)S(1)}, u32[]{:S(2)}, u32[]{:S(2)}) %collective-permute-start.3) | collective-permute-done | bytes 8224 | tf_op jit(solution)/shard_map/ppermute | solution.py:84
  31.9 1.8 %shard_map.109 = bf16[32,24,128]{2,1,0:T(8,128)(2,1)S(1)} custom-call(s32[1]{0:T(128)} %bitcast.place_ref, f32[256,128]{1,0:T(8,128)S(1)} %shard_map.106.near_ref, f32[32,128]{1,0:T(8,128)S(1)} %shard_map.108.far_ref, bf16[80,1024]{1,0:T(8,128)(2,1)S(1)} %get-tuple-element.16.bundle_ref.own_ref, bf16[80,1024]{1,0:T(8,128)(2,1)S(1)} %collective-permute-done.before_ref, ...), custom_call_target="tpu_custom_call" | custom-call | tf_op jit(solution)/shard_map/pallas_call | solution.py:30
  33.7 13.0 %all_to_all.20.pieces_ref = bf16[32,24,128]{2,1,0:T(8,128)(2,1)S(1)} all-to-all(bf16[32,24,128]{2,1,0:T(8,128)(2,1)S(1)} %shard_map.109), channel_id=1, replica_groups=mesh['group'=16,'dev'=32] {'dev'}, dimensions={0} | all-to-all | bytes 393216 | tf_op jit(solution)/shard_map/all_to_all | solution.py:78
  46.6 0.0 copy-done
  46.6 0.0 copy-done.1
  46.6 0.3 shard_map.110
  46.9 17.0 %all_to_all.21.pieces_ref = f32[16,1,128]{2,1,0:T(1,128)S(1)} all-to-all(f32[16,1,128]{2,1,0:T(1,128)S(1)} %get-tuple-element.20), channel_id=1, replica_groups={{0,2,64,66,128,130,192,194,256,258,320,322,384,386,448,450},{1,3,65,67,..., dimensions={0} | all-to-all | bytes 16384 | tf_op jit(solution)/shard_map/all_to_all | solution.py:78
  63.9 14.0 %all_to_all.22.refs_0_ = f32[32,1,128]{2,1,0:T(1,128)S(1)} all-to-all(f32[32,1,128]{2,1,0:T(1,128)S(1)} %shard_map.111), channel_id=1, replica_groups={{0,1,4,5,8,9,12,13,16,17,20,21,24,25,28,29,32,33,36,37,40,41,44,45,48,4..., dimensions={0} | all-to-all | bytes 32768 | tf_op jit(solution)/shard_map/all_to_all | solution.py:78
  77.9 0.8 %shard_map.112 = (f32[8,128]{1,0:T(8,128)}, f32[1,8]{1,0:T(1,128)}) custom-call(f32[32,1,128]{2,1,0:T(1,128)S(1)} %all_to_all.22.refs_0_, f32[8,128]{1,0:T(8,128)S(1)} %get-tuple-element.21.refs_1_, f32[8,1024]{1,0:T(8,128)S(1)} %copy-done), custom_call_target="tpu_custom_call" | custom-call | tf_op jit(solution)/shard_map/pallas_call | solution.py:30
  (1 shorter events, 0.0 us)
Async XLA Ops:
  2.3 23.1 %all-to-all-start = ((bf16[32,16,128]{2,1,0:T(8,128)(2,1)}), bf16[32,16,128]{2,1,0:T(8,128)(2,1)S(1)}, u32[]{:S(2)}, u32[]{:S(2)}) async-start(bf16[32,16,128]{2,1,0:T(8,128)(2,1)} %shard_map.104), calls=%async_computation | async-start | bytes 262144 | tf_op jit(solution)/shard_map/all_to_all | solution.py:78
  17.7 13.2 %collective-permute-start = (bf16[80,1024]{1,0:T(8,128)(2,1)S(1)}, bf16[80,1024]{1,0:T(8,128)(2,1)S(1)}, u32[]{:S(2)}, u32[]{:S(2)}) collective-permute-start(bf16[80,1024]{1,0:T(8,128)(2,1)S(1)} %get-tuple-element.16.bundle_ref.own_ref), channel_id=1, source_target_pairs={{0,32},{32,64},{64,96},{96,128},{128,160},{160,192},{192,224},{224... | collective-permute-start | bytes 491528 | tf_op jit(solution)/shard_map/ppermute | solution.py:84
  19.9 11.1 %collective-permute-start.1 = (bf16[80,1024]{1,0:T(8,128)(2,1)S(1)}, bf16[80,1024]{1,0:T(8,128)(2,1)S(1)}, u32[]{:S(2)}, u32[]{:S(2)}) collective-permute-start(bf16[80,1024]{1,0:T(8,128)(2,1)S(1)} %get-tuple-element.16.bundle_ref.own_ref), channel_id=1, source_target_pairs={{0,480},{32,0},{64,32},{96,64},{128,96},{160,128},{192,160},{224,1... | collective-permute-start | bytes 491528 | tf_op jit(solution)/shard_map/ppermute | solution.py:84
  25.5 5.4 %collective-permute-start.2 = (bf16[32,128]{1,0:T(8,128)(2,1)S(1)}, bf16[32,128]{1,0:T(8,128)(2,1)S(1)}, u32[]{:S(2)}, u32[]{:S(2)}) collective-permute-start(bf16[32,128]{1,0:T(8,128)(2,1)S(1)} %shard_map.107.coef_ref), channel_id=1, source_target_pairs={{0,32},{32,64},{64,96},{96,128},{128,160},{160,192},{192,224},{224... | collective-permute-start | bytes 24584 | tf_op jit(solution)/shard_map/ppermute | solution.py:84
  28.8 3.1 %collective-permute-start.3 = (bf16[32,128]{1,0:T(8,128)(2,1)S(1)}, bf16[32,128]{1,0:T(8,128)(2,1)S(1)}, u32[]{:S(2)}, u32[]{:S(2)}) collective-permute-start(bf16[32,128]{1,0:T(8,128)(2,1)S(1)} %shard_map.107.coef_ref), channel_id=1, source_target_pairs={{0,480},{32,0},{64,32},{96,64},{128,96},{160,128},{192,160},{224,1... | collective-permute-start | bytes 24584 | tf_op jit(solution)/shard_map/ppermute | solution.py:84
  29.8 16.8 %copy-start = (f32[8,1024]{1,0:T(8,128)S(1)}, f32[8,1024]{1,0:T(8,128)}, u32[]{:S(2)}) copy-start(f32[8,1024]{1,0:T(8,128)} %refs_2_.1) | copy-start | bytes 98308
  29.8 16.8 %copy-start.1 = (bf16[4,32,256]{2,1,0:T(8,128)(2,1)S(1)}, bf16[4,32,256]{2,1,0:T(8,128)(2,1)}, u32[]{:S(2)}) copy-start(bf16[4,32,256]{2,1,0:T(8,128)(2,1)} %param.11) | copy-start | bytes 196612

commit v4 on v2

--- a/solution.py
+++ b/solution.py
@@ -12,7 +12,6 @@
 DEVS, GROUPS = NZ * NX, 2 * NY
 VMEM = pl.BlockSpec(memory_space=pltpu.VMEM)
 HBM = pl.BlockSpec(memory_space=pltpu.HBM)
-SMEM = pl.BlockSpec(memory_space=pltpu.SMEM)
 sds = jax.ShapeDtypeStruct
 
 
@@ -123,9 +122,13 @@
     for copy in copies:
         copy.wait()
     i_row, j_row = pairs_ref[0:1, :], pairs_ref[1:2, :]
+    step = ((j_row >> 7) - (i_row >> 7)) & (GROUPS - 1)
+    which = jnp.where(step == 0, 0, jnp.where(step == 1, 2, 1))
+    live = mask_ref[...]
+    both = jnp.where(i_row == j_row, 0, live)
     row = iota((16, slots), 0)
     digits = jnp.zeros((16, slots), I32)
-    for k, value in enumerate((i_row >> 7, i_row & 127, j_row >> 7, j_row & 127, mask_ref[...])):
+    for k, value in enumerate((i_row & 127, j_row & 127, which, live, both)):
         digits = jnp.where(row == k, value, digits)
     out_ref[slots : slots + 16, :] = jnp.zeros((16, out_ref.shape[1]), BF16)
     out_ref[slots : slots + 16, 0:slots] = small(digits)
@@ -185,26 +188,25 @@
     out_ref[...] = mm(scatter_ref[...], jnp.concatenate(halves(values), axis=0))
 
 
-def far_body(place_ref, near_ref, own_ref, before_ref, after_ref, own_coef_ref, before_coef_ref,
+def far_body(near_ref, own_ref, before_ref, after_ref, own_coef_ref, before_coef_ref,
              after_coef_ref, out_ref):
-    group = place_ref[0]
     bundles = (own_ref, before_ref, after_ref)
     slots = own_ref.shape[0] - 16
     total_slots = 3 * slots
     rows = [b[slots : slots + 16, 0:slots].astype(F32).astype(I32) for b in bundles]
     cols = jnp.concatenate([columns(r) for r in rows], axis=0)
-    i_group, i_low, j_group, j_low, live = (cols[:, k : k + 1] for k in range(5))
+    i_low, j_low, which, live, both = (cols[:, k : k + 1] for k in range(5))
     coeffs = jnp.concatenate([own_coef_ref[...], before_coef_ref[...], after_coef_ref[...]], axis=0)
 
-    def gather(c_group, c_low):
-        step = (c_group - group) & (GROUPS - 1)
-        which = jnp.where(step == 0, 0, jnp.where(step == 1, 2, 1))
-        n = c_low.shape[0]
-        taken = mm(one_hot(iota((n, 3 * DEVS), 1) == which * DEVS + (c_low >> 2)), coeffs)
-        return jnp.where((iota((n, 128), 1) >> 5) == (c_low & 3), taken, 0.0).astype(BF16)
-
-    right = gather(j_group[0:slots], j_low[0:slots])
-    left = gather(i_group, i_low)
+    def gather(index, low):
+        n = low.shape[0]
+        taken = mm(one_hot(iota((n, 3 * DEVS), 1) == index), coeffs)
+        return jnp.where((iota((n, 128), 1) >> 5) == (low & 3), taken, 0.0).astype(BF16)
+
+    slot = iota((total_slots, 1), 0)
+    source = jnp.where(slot < slots, 0, jnp.where(slot < 2 * slots, 1, 2))
+    right = gather(which[0:slots] * DEVS + (j_low[0:slots] >> 2), j_low[0:slots])
+    left = gather(source * DEVS + (i_low >> 2), i_low)
     sub, lane = iota((128, 128), 0), iota((128, 128), 1)
     tiled = mm(right, one_hot((sub & 31) == (lane & 31)))
     forward = jnp.zeros((slots, 128), F32)
@@ -222,16 +224,16 @@
     forward = jnp.where(
         (live[0:slots] == 1) & (lane_block[0:slots] == (i_low[0:slots] & 3)), forward, 0.0
     )
-    different = (i_group != j_group) | (i_low != j_low)
-    mine = (live == 1) & (j_group == group) & different
+    wanted = jnp.where(source == 0, 0, jnp.where(source == 1, 2, 1))
+    mine = (both == 1) & (which == wanted)
     backward = jnp.where(mine & (lane_block == (j_low & 3)), backward, 0.0)
     owner = iota((DEVS, slots), 0)
     total = jnp.zeros((DEVS, 128), F32)
-    pick = one_hot(owner == (rows[0][1:2, :] >> 2))
+    pick = one_hot(owner == (rows[0][0:1, :] >> 2))
     for part in halves(forward):
         total = total + mm(pick, part)
     for k in range(3):
-        pick = one_hot(owner == (rows[k][3:4, :] >> 2))
+        pick = one_hot(owner == (rows[k][1:2, :] >> 2))
         for part in halves(backward[k * slots : k * slots + slots]):
             total = total + mm(pick, part)
     row = iota((8, 128), 0)
@@ -294,12 +296,11 @@
 ):
     panels = direction.shape[0]
     rank_rows = bases.reshape(-1, bases.shape[2])
-    place = lax.axis_index("group").astype(I32)[None]
     slots, far_slots = near_tiles.shape[0], far_blocks.shape[0]
 
     copies = call(
         pack_body,
-        sds((DEVS, 16, 128), BF16),
+        pltpu.VMEM((DEVS, 16, 128), BF16),
         [HBM, HBM],
         [pltpu.VMEM((8, 128), F32), pltpu.VMEM(rank_rows.shape, BF16), pltpu.SemaphoreType.DMA((2,))],
     )(direction.reshape(8, 128), rank_rows)
@@ -329,8 +330,8 @@
     coeffs = call(coeffs_body, sds((DEVS, 128), BF16), [VMEM])(gathered)
     coeffs_before, coeffs_after = group_shift(coeffs, 1), group_shift(coeffs, -1)
     near = call(near_body, sds((DEVS * 8, 128), F32), [VMEM] * 4)(gathered, gather, scatter, tiles)
-    parts = call(far_body, sds((DEVS, 24, 128), BF16), [SMEM] + [VMEM] * 7)(
-        place, near, bundle, before, after, coeffs, coeffs_before, coeffs_after
+    parts = call(far_body, sds((DEVS, 24, 128), BF16), [VMEM] * 7)(
+        near, bundle, before, after, coeffs, coeffs_before, coeffs_after
     )
     product, copies = call(
         product_body, [sds((8, 128), F32), sds((GROUPS, 1, 128), F32)], [VMEM] * 4

time: 75.2 us -> 75.2 us (level)
  no operation moved by 1% of the time
where the time goes in v4:
time: 75.2 us; the launch traced here: 74.8 us
  blocking collectives  40.7 us (54%)
  starting transfers between devices  19.1 us (25%)
  waiting for transfers between devices  7.56 us (10%)
  Pallas kernels  6.7 us (9%)
    all_to_all x3, blocking collectives, to_all(): return lax.all_to_all(value, axis, split_axis=0, concat_axis=0, tiled=True)  40.7 us
    all_to_all x1, starting transfers between devices, to_all(): return lax.all_to_all(value, axis, split_axis=0, concat_axis=0, tiled=True)  13.7 us
    pallas_call x8, Pallas kernels, run(): kernel(*(pltpu.with_memory_space_constraint(arg, pltpu.HBM) if spec is HB...  6.7 us
    all_to_all x1, waiting for transfers between devices, to_all(): return lax.all_to_all(value, axis, split_axis=0, concat_axis=0, tiled=True)  5.55 us
    ppermute x4, starting transfers between devices, group_shift(): lax.ppermute(value, 'group', [(g, (g + step) % GROUPS) for g in range(GRO...  5.4 us
    ppermute x4, waiting for transfers between devices, group_shift(): lax.ppermute(value, 'group', [(g, (g + step) % GROUPS) for g in range(GRO...  2.01 us
  transfers between devices with their start and end apart: 5, of which 2 were waited for; matrix products, arithmetic and copies ran while one was open for 0% of the time, Pallas kernels for 4%

profile of v4, /device:TPU:1, one launch (start us, length us, event | category | flops | bytes accessed | tf_op | source)
XLA Modules:
  0.0 74.8 jit_solution(2211143924754154961)
XLA Ops:
  0.6 1.7 %shard_map.104 = bf16[32,16,128]{2,1,0:T(8,128)(2,1)} custom-call(f32[8,128]{1,0:T(8,128)} %bitcast.13, bf16[128,256]{1,0:T(8,128)(2,1)} %bitcast.11), custom_call_target="tpu_custom_call" | custom-call | tf_op jit(solution)/shard_map/pallas_call | solution.py:29
  2.3 13.7 %all-to-all-start = ((bf16[32,16,128]{2,1,0:T(8,128)(2,1)}), bf16[32,16,128]{2,1,0:T(8,128)(2,1)S(1)}, u32[]{:S(2)}, u32[]{:S(2)}) async-start(bf16[32,16,128]{2,1,0:T(8,128)(2,1)} %shard_map.104), calls=%async_computation | async-start | bytes 262144 | tf_op jit(solution)/shard_map/all_to_all | solution.py:77
  16.1 1.6 %shard_map.105 = (bf16[80,1024]{1,0:T(8,128)(2,1)S(1)}, bf16[12,256,256]{2,1,0:T(8,128)(2,1)S(1)}, bf16[64,512]{1,0:T(8,128)(2,1)S(1)}, bf16[256,128]{1,0:T(8,128)(2,1)S(1)}, f32[1,128]{1,0:T(1,128)S(1)}) custom-call(bf16[12,256,256]{2,1,0:T(8,128)(2,1)} %tiles_hbm.1, bf16[64,1024]{1,0:T(8,128)(2,1)} %blocks_hbm.1, s32[2,64]{1,0:T(2,128)} %bitcast.14, ...), custom_call_target="tpu_custom_call" | custom-call | tf_op jit(solution)/shard_map/pallas_call | solution.py:29
  17.7 2.1 %collective-permute-start = (bf16[80,1024]{1,0:T(8,128)(2,1)S(1)}, bf16[80,1024]{1,0:T(8,128)(2,1)S(1)}, u32[]{:S(2)}, u32[]{:S(2)}) collective-permute-start(bf16[80,1024]{1,0:T(8,128)(2,1)S(1)} %get-tuple-element.14.own_ref), channel_id=1, source_target_pairs={{0,32},{32,64},{64,96},{96,128},{128,160},{160,192},{192,224},{224... | collective-permute-start | bytes 491528 | tf_op jit(solution)/shard_map/ppermute | solution.py:81
  19.9 0.0 collective-permute-start.1
  19.9 5.5 %all-to-all-done = bf16[32,16,128]{2,1,0:T(8,128)(2,1)S(1)} async-done(((bf16[32,16,128]{2,1,0:T(8,128)(2,1)}), bf16[32,16,128]{2,1,0:T(8,128)(2,1)S(1)}, u32[]{:S(2)}, u32[]{:S(2)}) %all-to-all-start) | async-done | bytes 131104 | tf_op jit(solution)/shard_map/all_to_all | solution.py:77
  25.4 0.1 shard_map.107.own_coef_ref
  25.5 3.2 %collective-permute-start.2 = (bf16[32,128]{1,0:T(8,128)(2,1)S(1)}, bf16[32,128]{1,0:T(8,128)(2,1)S(1)}, u32[]{:S(2)}, u32[]{:S(2)}) collective-permute-start(bf16[32,128]{1,0:T(8,128)(2,1)S(1)} %shard_map.107.own_coef_ref), channel_id=1, source_target_pairs={{0,32},{32,64},{64,96},{96,128},{128,160},{160,192},{192,224},{224... | collective-permute-start | bytes 24584 | tf_op jit(solution)/shard_map/ppermute | solution.py:81
  28.8 0.0 collective-permute-start.3
  28.8 0.0 copy-start
  28.8 0.0 copy-start.1
  28.8 1.0 %shard_map.106.near_ref = f32[256,128]{1,0:T(8,128)S(1)} custom-call(bf16[512,128]{1,0:T(8,128)(2,1)S(1)} %bitcast.10, bf16[64,512]{1,0:T(8,128)(2,1)S(1)} %get-tuple-element.11.gather_ref, bf16[256,128]{1,0:T(8,128)(2,1)S(1)} %get-tuple-element.12.scatter_ref, bf16[12,256,256]{2,1,0:T(8,128)(2,1)S(1)} %get-tuple-element.13.tiles_ref), custom_call_target="tpu_custom_call" | custom-call | tf_op jit(solution)/shard_map/pallas_call | solution.py:29
  29.8 0.0 collective-permute-done.before_ref
  29.8 0.0 collective-permute-done.1.after_ref
  29.9 0.0 collective-permute-done.2.before_coef_ref
  29.9 2.0 %collective-permute-done.3.after_coef_ref = bf16[32,128]{1,0:T(8,128)(2,1)S(1)} collective-permute-done((bf16[32,128]{1,0:T(8,128)(2,1)S(1)}, bf16[32,128]{1,0:T(8,128)(2,1)S(1)}, u32[]{:S(2)}, u32[]{:S(2)}) %collective-permute-start.3) | collective-permute-done | bytes 8224 | tf_op jit(solution)/shard_map/ppermute | solution.py:81
  31.9 1.1 %shard_map.108 = bf16[32,24,128]{2,1,0:T(8,128)(2,1)S(1)} custom-call(f32[256,128]{1,0:T(8,128)S(1)} %shard_map.106.near_ref, bf16[80,1024]{1,0:T(8,128)(2,1)S(1)} %get-tuple-element.14.own_ref, bf16[80,1024]{1,0:T(8,128)(2,1)S(1)} %collective-permute-done.before_ref, bf16[80,1024]{1,0:T(8,128)(2,1)S(1)} %collective-permute-done.1.after_ref, ...), custom_call_target="tpu_custom_call" | custom-call | tf_op jit(solution)/shard_map/pallas_call | solution.py:29
  33.0 13.6 %all_to_all.20.pieces_ref = bf16[32,24,128]{2,1,0:T(8,128)(2,1)S(1)} all-to-all(bf16[32,24,128]{2,1,0:T(8,128)(2,1)S(1)} %shard_map.108), channel_id=1, replica_groups=mesh['group'=16,'dev'=32] {'dev'}, dimensions={0} | all-to-all | bytes 393216 | tf_op jit(solution)/shard_map/all_to_all | solution.py:77
  46.6 0.0 copy-done
  46.6 0.0 copy-done.1
  46.6 0.3 shard_map.109
  46.9 15.5 %all_to_all.21.pieces_ref = f32[16,1,128]{2,1,0:T(1,128)S(1)} all-to-all(f32[16,1,128]{2,1,0:T(1,128)S(1)} %get-tuple-element.16), channel_id=1, replica_groups=mesh['group'=16,'dev'=32] {'group'}, dimensions={0} | all-to-all | bytes 16384 | tf_op jit(solution)/shard_map/all_to_all | solution.py:77
  62.4 11.6 %all_to_all.22.refs_0_ = f32[32,1,128]{2,1,0:T(1,128)S(1)} all-to-all(f32[32,1,128]{2,1,0:T(1,128)S(1)} %shard_map.110), channel_id=1, replica_groups=mesh['group'=16,'dev'=32] {'dev'}, dimensions={0} | all-to-all | bytes 32768 | tf_op jit(solution)/shard_map/all_to_all | solution.py:77
  74.0 0.8 %shard_map.111 = (f32[8,128]{1,0:T(8,128)}, f32[1,8]{1,0:T(1,128)}) custom-call(f32[32,1,128]{2,1,0:T(1,128)S(1)} %all_to_all.22.refs_0_, f32[8,128]{1,0:T(8,128)S(1)} %get-tuple-element.17.refs_1_, f32[8,1024]{1,0:T(8,128)S(1)} %copy-done), custom_call_target="tpu_custom_call" | custom-call | tf_op jit(solution)/shard_map/pallas_call | solution.py:29
  (1 shorter events, 0.0 us)
Async XLA Ops:
  2.3 23.1 %all-to-all-start = ((bf16[32,16,128]{2,1,0:T(8,128)(2,1)}), bf16[32,16,128]{2,1,0:T(8,128)(2,1)S(1)}, u32[]{:S(2)}, u32[]{:S(2)}) async-start(bf16[32,16,128]{2,1,0:T(8,128)(2,1)} %shard_map.104), calls=%async_computation | async-start | bytes 262144 | tf_op jit(solution)/shard_map/all_to_all | solution.py:77
  17.7 12.1 %collective-permute-start = (bf16[80,1024]{1,0:T(8,128)(2,1)S(1)}, bf16[80,1024]{1,0:T(8,128)(2,1)S(1)}, u32[]{:S(2)}, u32[]{:S(2)}) collective-permute-start(bf16[80,1024]{1,0:T(8,128)(2,1)S(1)} %get-tuple-element.14.own_ref), channel_id=1, source_target_pairs={{0,32},{32,64},{64,96},{96,128},{128,160},{160,192},{192,224},{224... | collective-permute-start | bytes 491528 | tf_op jit(solution)/shard_map/ppermute | solution.py:81
  19.9 10.0 %collective-permute-start.1 = (bf16[80,1024]{1,0:T(8,128)(2,1)S(1)}, bf16[80,1024]{1,0:T(8,128)(2,1)S(1)}, u32[]{:S(2)}, u32[]{:S(2)}) collective-permute-start(bf16[80,1024]{1,0:T(8,128)(2,1)S(1)} %get-tuple-element.14.own_ref), channel_id=1, source_target_pairs={{0,480},{32,0},{64,32},{96,64},{128,96},{160,128},{192,160},{224,1... | collective-permute-start | bytes 491528 | tf_op jit(solution)/shard_map/ppermute | solution.py:81
  25.5 4.3 %collective-permute-start.2 = (bf16[32,128]{1,0:T(8,128)(2,1)S(1)}, bf16[32,128]{1,0:T(8,128)(2,1)S(1)}, u32[]{:S(2)}, u32[]{:S(2)}) collective-permute-start(bf16[32,128]{1,0:T(8,128)(2,1)S(1)} %shard_map.107.own_coef_ref), channel_id=1, source_target_pairs={{0,32},{32,64},{64,96},{96,128},{128,160},{160,192},{192,224},{224... | collective-permute-start | bytes 24584 | tf_op jit(solution)/shard_map/ppermute | solution.py:81
  28.8 3.1 %collective-permute-start.3 = (bf16[32,128]{1,0:T(8,128)(2,1)S(1)}, bf16[32,128]{1,0:T(8,128)(2,1)S(1)}, u32[]{:S(2)}, u32[]{:S(2)}) collective-permute-start(bf16[32,128]{1,0:T(8,128)(2,1)S(1)} %shard_map.107.own_coef_ref), channel_id=1, source_target_pairs={{0,480},{32,0},{64,32},{96,64},{128,96},{160,128},{192,160},{224,1... | collective-permute-start | bytes 24584 | tf_op jit(solution)/shard_map/ppermute | solution.py:81
  28.8 17.8 %copy-start = (f32[8,1024]{1,0:T(8,128)S(1)}, f32[8,1024]{1,0:T(8,128)}, u32[]{:S(2)}) copy-start(f32[8,1024]{1,0:T(8,128)} %refs_2_.1) | copy-start | bytes 98308
  28.8 17.8 %copy-start.1 = (bf16[4,32,256]{2,1,0:T(8,128)(2,1)S(1)}, bf16[4,32,256]{2,1,0:T(8,128)(2,1)}, u32[]{:S(2)}) copy-start(bf16[4,32,256]{2,1,0:T(8,128)(2,1)} %param.11) | copy-start | bytes 196612

commit v5 on v4

--- a/solution.py
+++ b/solution.py
@@ -188,69 +188,71 @@
     out_ref[...] = mm(scatter_ref[...], jnp.concatenate(halves(values), axis=0))
 
 
+def far_prep_body(own_ref, before_ref, after_ref, pick_ref, lanes_ref, keep_ref, owner_ref,
+                  take_ref, give_ref):
+    slots = own_ref.shape[0] - 16
+    rows = [
+        ref[slots : slots + 16, 0:slots].astype(F32).astype(I32)
+        for ref in (own_ref, before_ref, after_ref)
+    ]
+    cols = jnp.concatenate([columns(r) for r in [rows[0]] + rows], axis=0)
+    i_low, j_low, which, live, both = (cols[:, k : k + 1] for k in range(5))
+    slot = iota((4 * slots, 1), 0) // slots
+    ahead = slot == 0
+    low = jnp.where(ahead, j_low, i_low)
+    source = jnp.where(ahead, which, slot - 1)
+    pick_ref[...] = one_hot(iota((4 * slots, 3 * DEVS), 1) == source * DEVS + (low >> 2))
+    block = iota((4 * slots, 128), 1) >> 5
+    lanes_ref[...] = jnp.where(block == (low & 3), 1.0, 0.0)
+    wanted = jnp.where(slot == 2, 2, jnp.where(slot == 3, 1, 0))
+    used = jnp.where(ahead, live, jnp.where(which == wanted, both, 0))
+    target = jnp.where(ahead, i_low, j_low)
+    keep_ref[...] = jnp.where((used == 1) & (block == (target & 3)), 1.0, 0.0)
+    owner = iota((DEVS, slots), 0)
+    for k, row in enumerate([rows[0][0:1, :]] + [r[1:2, :] for r in rows]):
+        owner_ref[k] = one_hot(owner == (row >> 2))
+    for k in range(8):
+        sub, lane = iota((128, 128), 0), iota((128, 128), 1)
+        take_ref[k] = one_hot((sub & 31) == 4 * k + (lane >> 5))
+        give_ref[k] = one_hot((lane & 31) == 4 * k + (sub >> 5))
+
+
 def far_body(near_ref, own_ref, before_ref, after_ref, own_coef_ref, before_coef_ref,
-             after_coef_ref, out_ref):
+             after_coef_ref, pick_ref, lanes_ref, keep_ref, owner_ref, take_ref, give_ref, out_ref):
     bundles = (own_ref, before_ref, after_ref)
     slots = own_ref.shape[0] - 16
-    total_slots = 3 * slots
-    rows = [b[slots : slots + 16, 0:slots].astype(F32).astype(I32) for b in bundles]
-    cols = jnp.concatenate([columns(r) for r in rows], axis=0)
-    i_low, j_low, which, live, both = (cols[:, k : k + 1] for k in range(5))
     coeffs = jnp.concatenate([own_coef_ref[...], before_coef_ref[...], after_coef_ref[...]], axis=0)
-
-    def gather(index, low):
-        n = low.shape[0]
-        taken = mm(one_hot(iota((n, 3 * DEVS), 1) == index), coeffs)
-        return jnp.where((iota((n, 128), 1) >> 5) == (low & 3), taken, 0.0).astype(BF16)
-
-    slot = iota((total_slots, 1), 0)
-    source = jnp.where(slot < slots, 0, jnp.where(slot < 2 * slots, 1, 2))
-    right = gather(which[0:slots] * DEVS + (j_low[0:slots] >> 2), j_low[0:slots])
-    left = gather(source * DEVS + (i_low >> 2), i_low)
+    taken = (mm(pick_ref[...], coeffs) * lanes_ref[...]).astype(BF16)
+    right, left = taken[0:slots], taken[slots:]
     sub, lane = iota((128, 128), 0), iota((128, 128), 1)
     tiled = mm(right, one_hot((sub & 31) == (lane & 31)))
     forward = jnp.zeros((slots, 128), F32)
-    backward = jnp.zeros((total_slots, 128), F32)
+    backward = jnp.zeros(left.shape, F32)
     for k in range(8):
         parts = [b[0:slots, k * 128 : k * 128 + 128] for b in bundles]
         part = jnp.concatenate(parts, axis=0).astype(F32)
-        backward = backward + part * mm(left, one_hot((sub & 31) == 4 * k + (lane >> 5)))
-        give = one_hot((lane & 31) == 4 * k + (sub >> 5))
+        backward = backward + part * mm(left, take_ref[k])
         for piece in halves(part[0:slots] * tiled):
-            forward = forward + mm(piece, give)
+            forward = forward + mm(piece, give_ref[k])
     backward = backward + pltpu.roll(backward, 64, 1)
     backward = backward + pltpu.roll(backward, 32, 1)
-    lane_block = iota((total_slots, 128), 1) >> 5
-    forward = jnp.where(
-        (live[0:slots] == 1) & (lane_block[0:slots] == (i_low[0:slots] & 3)), forward, 0.0
-    )
-    wanted = jnp.where(source == 0, 0, jnp.where(source == 1, 2, 1))
-    mine = (both == 1) & (which == wanted)
-    backward = jnp.where(mine & (lane_block == (j_low & 3)), backward, 0.0)
-    owner = iota((DEVS, slots), 0)
+    sums = jnp.concatenate([forward, backward], axis=0) * keep_ref[...]
     total = jnp.zeros((DEVS, 128), F32)
-    pick = one_hot(owner == (rows[0][0:1, :] >> 2))
-    for part in halves(forward):
-        total = total + mm(pick, part)
-    for k in range(3):
-        pick = one_hot(owner == (rows[k][1:2, :] >> 2))
-        for part in halves(backward[k * slots : k * slots + slots]):
-            total = total + mm(pick, part)
+    for k in range(4):
+        for part in halves(sums[k * slots : k * slots + slots]):
+            total = total + mm(owner_ref[k], part)
     row = iota((8, 128), 0)
     for d in range(DEVS):
         near = near_ref[d * 8 : d * 8 + 8, :]
-        near_high = near.astype(BF16).astype(F32)
-        far = total[d : d + 1, :]
-        far_high = far.astype(BF16).astype(F32)
-        tail = jnp.where(row == 0, far_high, jnp.where(row == 1, far - far_high, 0.0))
-        out_ref[d] = jnp.concatenate([near_high, near - near_high, tail], axis=0).astype(BF16)
+        low = jnp.where(row == 7, total[d : d + 1, :], near - near.astype(BF16).astype(F32))
+        out_ref[d] = jnp.concatenate([near, low], axis=0).astype(BF16)
 
 
 def product_body(pieces_ref, bases_ref, krylov_ref, gram_ref, product_ref, copies_ref):
     total = jnp.sum(pieces_ref[...].astype(F32), axis=0)
-    near = total[0:8, :] + total[8:16, :]
-    coef = (total[16:17, :] + total[17:18, :]).astype(BF16).astype(F32)
     row, lane = iota((8, 128), 0), iota((8, 128), 1)
+    near = total[0:8, :] + jnp.where(row == 7, 0.0, total[8:16, :])
+    coef = total[15:16, :].astype(BF16).astype(F32)
     spread = jnp.where((lane >> 5) == (row >> 1), coef, 0.0).astype(BF16)
     low = mm(spread, bases_ref[:, :128])
     high = mm(spread, bases_ref[:, 128:])
@@ -300,7 +302,7 @@
 
     copies = call(
         pack_body,
-        pltpu.VMEM((DEVS, 16, 128), BF16),
+        sds((DEVS, 16, 128), BF16),
         [HBM, HBM],
         [pltpu.VMEM((8, 128), F32), pltpu.VMEM(rank_rows.shape, BF16), pltpu.SemaphoreType.DMA((2,))],
     )(direction.reshape(8, 128), rank_rows)
@@ -330,8 +332,20 @@
     coeffs = call(coeffs_body, sds((DEVS, 128), BF16), [VMEM])(gathered)
     coeffs_before, coeffs_after = group_shift(coeffs, 1), group_shift(coeffs, -1)
     near = call(near_body, sds((DEVS * 8, 128), F32), [VMEM] * 4)(gathered, gather, scatter, tiles)
-    parts = call(far_body, sds((DEVS, 24, 128), BF16), [VMEM] * 7)(
-        near, bundle, before, after, coeffs, coeffs_before, coeffs_after
+    far_prep = call(
+        far_prep_body,
+        [
+            pltpu.VMEM((4 * far_slots, 3 * DEVS), BF16),
+            pltpu.VMEM((4 * far_slots, 128), F32),
+            pltpu.VMEM((4 * far_slots, 128), F32),
+            pltpu.VMEM((4, DEVS, far_slots), BF16),
+            pltpu.VMEM((8, 128, 128), BF16),
+            pltpu.VMEM((8, 128, 128), BF16),
+        ],
+        [VMEM] * 3,
+    )(bundle, before, after)
+    parts = call(far_body, sds((DEVS, 16, 128), BF16), [VMEM] * 13)(
+        near, bundle, before, after, coeffs, coeffs_before, coeffs_after, *far_prep
     )
     product, copies = call(
         product_body, [sds((8, 128), F32), sds((GROUPS, 1, 128), F32)], [VMEM] * 4

time: 75.2 us -> 74.3 us (0.988)
    pallas_call x8 -> x9, Pallas kernels: 6.7 us -> 6.97 us  [run(): kernel(*(pltpu.with_memory_space_constraint(arg, pltpu.HBM) if spec is HB...]
  transfers between devices with their start and end apart: 5 -> 5, of which waited for: 2 -> 2; matrix products, arithmetic and copies ran while one was open for 0% -> 0% of each run, Pallas kernels for 4% -> 5%
where the time goes in v5:
time: 74.3 us; the launch traced here: 73.9 us
  blocking collectives  40.1 us (54%)
  starting transfers between devices  19.1 us (26%)
  waiting for transfers between devices  6.98 us (9%)
  Pallas kernels  6.97 us (9%)
    all_to_all x3, blocking collectives, to_all(): return lax.all_to_all(value, axis, split_axis=0, concat_axis=0, tiled=True)  40.1 us
    all_to_all x1, starting transfers between devices, to_all(): return lax.all_to_all(value, axis, split_axis=0, concat_axis=0, tiled=True)  13.7 us
    pallas_call x9, Pallas kernels, run(): kernel(*(pltpu.with_memory_space_constraint(arg, pltpu.HBM) if spec is HB...  6.97 us
    all_to_all x1, waiting for transfers between devices, to_all(): return lax.all_to_all(value, axis, split_axis=0, concat_axis=0, tiled=True)  5.55 us
    ppermute x4, starting transfers between devices, group_shift(): lax.ppermute(value, 'group', [(g, (g + step) % GROUPS) for g in range(GRO...  5.4 us
  transfers between devices with their start and end apart: 5, of which 2 were waited for; matrix products, arithmetic and copies ran while one was open for 0% of the time, Pallas kernels for 5%

profile of v5, /device:TPU:1, one launch (start us, length us, event | category | flops | bytes accessed | tf_op | source)
XLA Modules:
  0.0 73.9 jit_solution(2059489394164397114)
XLA Ops:
  0.6 1.7 %shard_map.104 = bf16[32,16,128]{2,1,0:T(8,128)(2,1)} custom-call(f32[8,128]{1,0:T(8,128)} %bitcast.13, bf16[128,256]{1,0:T(8,128)(2,1)} %bitcast.11), custom_call_target="tpu_custom_call" | custom-call | tf_op jit(solution)/shard_map/pallas_call | solution.py:29
  2.3 13.7 %all-to-all-start = ((bf16[32,16,128]{2,1,0:T(8,128)(2,1)}), bf16[32,16,128]{2,1,0:T(8,128)(2,1)S(1)}, u32[]{:S(2)}, u32[]{:S(2)}) async-start(bf16[32,16,128]{2,1,0:T(8,128)(2,1)} %shard_map.104), calls=%async_computation | async-start | bytes 262144 | tf_op jit(solution)/shard_map/all_to_all | solution.py:77
  16.1 1.6 %shard_map.105 = (bf16[80,1024]{1,0:T(8,128)(2,1)S(1)}, bf16[12,256,256]{2,1,0:T(8,128)(2,1)S(1)}, bf16[64,512]{1,0:T(8,128)(2,1)S(1)}, bf16[256,128]{1,0:T(8,128)(2,1)S(1)}, f32[1,128]{1,0:T(1,128)S(1)}) custom-call(bf16[12,256,256]{2,1,0:T(8,128)(2,1)} %tiles_hbm.1, bf16[64,1024]{1,0:T(8,128)(2,1)} %blocks_hbm.1, s32[2,64]{1,0:T(2,128)} %bitcast.14, ...), custom_call_target="tpu_custom_call" | custom-call | tf_op jit(solution)/shard_map/pallas_call | solution.py:29
  17.7 2.1 %collective-permute-start = (bf16[80,1024]{1,0:T(8,128)(2,1)S(1)}, bf16[80,1024]{1,0:T(8,128)(2,1)S(1)}, u32[]{:S(2)}, u32[]{:S(2)}) collective-permute-start(bf16[80,1024]{1,0:T(8,128)(2,1)S(1)} %get-tuple-element.20.own_ref), channel_id=1, source_target_pairs={{0,32},{32,64},{64,96},{96,128},{128,160},{160,192},{192,224},{224... | collective-permute-start | bytes 491528 | tf_op jit(solution)/shard_map/ppermute | solution.py:81
  19.8 0.0 collective-permute-start.1
  19.9 5.5 %all-to-all-done = bf16[32,16,128]{2,1,0:T(8,128)(2,1)S(1)} async-done(((bf16[32,16,128]{2,1,0:T(8,128)(2,1)}), bf16[32,16,128]{2,1,0:T(8,128)(2,1)S(1)}, u32[]{:S(2)}, u32[]{:S(2)}) %all-to-all-start) | async-done | bytes 131104 | tf_op jit(solution)/shard_map/all_to_all | solution.py:77
  25.4 0.1 shard_map.107.own_coef_ref
  25.5 3.2 %collective-permute-start.2 = (bf16[32,128]{1,0:T(8,128)(2,1)S(1)}, bf16[32,128]{1,0:T(8,128)(2,1)S(1)}, u32[]{:S(2)}, u32[]{:S(2)}) collective-permute-start(bf16[32,128]{1,0:T(8,128)(2,1)S(1)} %shard_map.107.own_coef_ref), channel_id=1, source_target_pairs={{0,32},{32,64},{64,96},{96,128},{128,160},{160,192},{192,224},{224... | collective-permute-start | bytes 24584 | tf_op jit(solution)/shard_map/ppermute | solution.py:81
  28.8 0.0 collective-permute-start.3
  28.8 0.0 collective-permute-done.before_ref
  28.8 0.0 collective-permute-done.1.after_ref
  28.8 0.6 shard_map.108
  29.4 0.0 copy-start
  29.4 0.0 copy-start.1
  29.4 1.0 %shard_map.106.near_ref = f32[256,128]{1,0:T(8,128)S(1)} custom-call(bf16[512,128]{1,0:T(8,128)(2,1)S(1)} %bitcast.10, bf16[64,512]{1,0:T(8,128)(2,1)S(1)} %get-tuple-element.17.gather_ref, bf16[256,128]{1,0:T(8,128)(2,1)S(1)} %get-tuple-element.18.scatter_ref, bf16[12,256,256]{2,1,0:T(8,128)(2,1)S(1)} %get-tuple-element.19.tiles_ref), custom_call_target="tpu_custom_call" | custom-call | tf_op jit(solution)/shard_map/pallas_call | solution.py:29
  30.4 0.0 collective-permute-done.2.before_coef_ref
  30.4 1.4 %collective-permute-done.3.after_coef_ref = bf16[32,128]{1,0:T(8,128)(2,1)S(1)} collective-permute-done((bf16[32,128]{1,0:T(8,128)(2,1)S(1)}, bf16[32,128]{1,0:T(8,128)(2,1)S(1)}, u32[]{:S(2)}, u32[]{:S(2)}) %collective-permute-start.3) | collective-permute-done | bytes 8224 | tf_op jit(solution)/shard_map/ppermute | solution.py:81
  31.9 0.8 %shard_map.109 = bf16[32,16,128]{2,1,0:T(8,128)(2,1)S(1)} custom-call(f32[256,128]{1,0:T(8,128)S(1)} %shard_map.106.near_ref, bf16[80,1024]{1,0:T(8,128)(2,1)S(1)} %get-tuple-element.20.own_ref, bf16[80,1024]{1,0:T(8,128)(2,1)S(1)} %collective-permute-done.before_ref, bf16[80,1024]{1,0:T(8,128)(2,1)S(1)} %collective-permute-done.1.after_ref, ...), custom_call_target="tpu_custom_call" | custom-call | tf_op jit(solution)/shard_map/pallas_call | solution.py:29
  32.7 13.5 %all_to_all.20.pieces_ref = bf16[32,16,128]{2,1,0:T(8,128)(2,1)S(1)} all-to-all(bf16[32,16,128]{2,1,0:T(8,128)(2,1)S(1)} %shard_map.109), channel_id=1, replica_groups=mesh['group'=16,'dev'=32] {'dev'}, dimensions={0} | all-to-all | bytes 262144 | tf_op jit(solution)/shard_map/all_to_all | solution.py:77
  46.2 0.0 copy-done
  46.2 0.0 copy-done.1
  46.2 0.3 shard_map.110
  46.5 15.0 %all_to_all.21.pieces_ref = f32[16,1,128]{2,1,0:T(1,128)S(1)} all-to-all(f32[16,1,128]{2,1,0:T(1,128)S(1)} %get-tuple-element.28), channel_id=1, replica_groups=mesh['group'=16,'dev'=32] {'group'}, dimensions={0} | all-to-all | bytes 16384 | tf_op jit(solution)/shard_map/all_to_all | solution.py:77
  61.5 11.6 %all_to_all.22.refs_0_ = f32[32,1,128]{2,1,0:T(1,128)S(1)} all-to-all(f32[32,1,128]{2,1,0:T(1,128)S(1)} %shard_map.111), channel_id=1, replica_groups=mesh['group'=16,'dev'=32] {'dev'}, dimensions={0} | all-to-all | bytes 32768 | tf_op jit(solution)/shard_map/all_to_all | solution.py:77
  73.1 0.8 %shard_map.112 = (f32[8,128]{1,0:T(8,128)}, f32[1,8]{1,0:T(1,128)}) custom-call(f32[32,1,128]{2,1,0:T(1,128)S(1)} %all_to_all.22.refs_0_, f32[8,128]{1,0:T(8,128)S(1)} %get-tuple-element.29.refs_1_, f32[8,1024]{1,0:T(8,128)S(1)} %copy-done), custom_call_target="tpu_custom_call" | custom-call | tf_op jit(solution)/shard_map/pallas_call | solution.py:29
  (1 shorter events, 0.0 us)
Async XLA Ops:
  2.3 23.1 %all-to-all-start = ((bf16[32,16,128]{2,1,0:T(8,128)(2,1)}), bf16[32,16,128]{2,1,0:T(8,128)(2,1)S(1)}, u32[]{:S(2)}, u32[]{:S(2)}) async-start(bf16[32,16,128]{2,1,0:T(8,128)(2,1)} %shard_map.104), calls=%async_computation | async-start | bytes 262144 | tf_op jit(solution)/shard_map/all_to_all | solution.py:77
  17.7 11.1 %collective-permute-start = (bf16[80,1024]{1,0:T(8,128)(2,1)S(1)}, bf16[80,1024]{1,0:T(8,128)(2,1)S(1)}, u32[]{:S(2)}, u32[]{:S(2)}) collective-permute-start(bf16[80,1024]{1,0:T(8,128)(2,1)S(1)} %get-tuple-element.20.own_ref), channel_id=1, source_target_pairs={{0,32},{32,64},{64,96},{96,128},{128,160},{160,192},{192,224},{224... | collective-permute-start | bytes 491528 | tf_op jit(solution)/shard_map/ppermute | solution.py:81
  19.8 8.9 %collective-permute-start.1 = (bf16[80,1024]{1,0:T(8,128)(2,1)S(1)}, bf16[80,1024]{1,0:T(8,128)(2,1)S(1)}, u32[]{:S(2)}, u32[]{:S(2)}) collective-permute-start(bf16[80,1024]{1,0:T(8,128)(2,1)S(1)} %get-tuple-element.20.own_ref), channel_id=1, source_target_pairs={{0,480},{32,0},{64,32},{96,64},{128,96},{160,128},{192,160},{224,1... | collective-permute-start | bytes 491528 | tf_op jit(solution)/shard_map/ppermute | solution.py:81
  25.5 4.9 %collective-permute-start.2 = (bf16[32,128]{1,0:T(8,128)(2,1)S(1)}, bf16[32,128]{1,0:T(8,128)(2,1)S(1)}, u32[]{:S(2)}, u32[]{:S(2)}) collective-permute-start(bf16[32,128]{1,0:T(8,128)(2,1)S(1)} %shard_map.107.own_coef_ref), channel_id=1, source_target_pairs={{0,32},{32,64},{64,96},{96,128},{128,160},{160,192},{192,224},{224... | collective-permute-start | bytes 24584 | tf_op jit(solution)/shard_map/ppermute | solution.py:81
  28.8 3.1 %collective-permute-start.3 = (bf16[32,128]{1,0:T(8,128)(2,1)S(1)}, bf16[32,128]{1,0:T(8,128)(2,1)S(1)}, u32[]{:S(2)}, u32[]{:S(2)}) collective-permute-start(bf16[32,128]{1,0:T(8,128)(2,1)S(1)} %shard_map.107.own_coef_ref), channel_id=1, source_target_pairs={{0,480},{32,0},{64,32},{96,64},{128,96},{160,128},{192,160},{224,1... | collective-permute-start | bytes 24584 | tf_op jit(solution)/shard_map/ppermute | solution.py:81
  29.4 16.8 %copy-start = (f32[8,1024]{1,0:T(8,128)S(1)}, f32[8,1024]{1,0:T(8,128)}, u32[]{:S(2)}) copy-start(f32[8,1024]{1,0:T(8,128)} %refs_2_.1) | copy-start | bytes 98308
  29.4 16.8 %copy-start.1 = (bf16[4,32,256]{2,1,0:T(8,128)(2,1)S(1)}, bf16[4,32,256]{2,1,0:T(8,128)(2,1)}, u32[]{:S(2)}) copy-start(bf16[4,32,256]{2,1,0:T(8,128)(2,1)} %param.11) | copy-start | bytes 196612

commit v6 on v5

--- a/solution.py
+++ b/solution.py
@@ -171,7 +171,9 @@
     out_ref[...] = mm(pick, gathered_ref[...]).astype(BF16)
 
 
-def near_body(gathered_ref, gather_ref, scatter_ref, tiles_ref, out_ref):
+def near_body(gathered_ref, gather_ref, scatter_ref, tiles_ref, own_ref, before_ref, after_ref,
+              out_ref, *far_refs):
+    far_prep(own_ref, before_ref, after_ref, *far_refs)
     taken = mm(gather_ref[...], gathered_ref[...])
     right = jnp.concatenate([taken[0:16], taken[16:32]], axis=1).astype(BF16)
     left = jnp.concatenate([taken[32:48], taken[48:64]], axis=1).astype(BF16)
@@ -188,8 +190,8 @@
     out_ref[...] = mm(scatter_ref[...], jnp.concatenate(halves(values), axis=0))
 
 
-def far_prep_body(own_ref, before_ref, after_ref, pick_ref, lanes_ref, keep_ref, owner_ref,
-                  take_ref, give_ref):
+def far_prep(own_ref, before_ref, after_ref, pick_ref, lanes_ref, keep_ref, owner_ref, take_ref,
+             give_ref):
     slots = own_ref.shape[0] - 16
     rows = [
         ref[slots : slots + 16, 0:slots].astype(F32).astype(I32)
@@ -331,10 +333,10 @@
 
     coeffs = call(coeffs_body, sds((DEVS, 128), BF16), [VMEM])(gathered)
     coeffs_before, coeffs_after = group_shift(coeffs, 1), group_shift(coeffs, -1)
-    near = call(near_body, sds((DEVS * 8, 128), F32), [VMEM] * 4)(gathered, gather, scatter, tiles)
-    far_prep = call(
-        far_prep_body,
+    near, *far_prepared = call(
+        near_body,
         [
+            sds((DEVS * 8, 128), F32),
             pltpu.VMEM((4 * far_slots, 3 * DEVS), BF16),
             pltpu.VMEM((4 * far_slots, 128), F32),
             pltpu.VMEM((4 * far_slots, 128), F32),
@@ -342,10 +344,10 @@
             pltpu.VMEM((8, 128, 128), BF16),
             pltpu.VMEM((8, 128, 128), BF16),
         ],
-        [VMEM] * 3,
-    )(bundle, before, after)
+        [VMEM] * 7,
+    )(gathered, gather, scatter, tiles, bundle, before, after)
     parts = call(far_body, sds((DEVS, 16, 128), BF16), [VMEM] * 13)(
-        near, bundle, before, after, coeffs, coeffs_before, coeffs_after, *far_prep
+        near, bundle, before, after, coeffs, coeffs_before, coeffs_after, *far_prepared
     )
     product, copies = call(
         product_body, [sds((8, 128), F32), sds((GROUPS, 1, 128), F32)], [VMEM] * 4

time: 74.3 us -> 74 us (level)
    pallas_call x9 -> x8, Pallas kernels: 6.97 us -> 6.51 us  [run(): kernel(*(pltpu.with_memory_space_constraint(arg, pltpu.HBM) if spec is HB...]
  transfers between devices with their start and end apart: 5 -> 5, of which waited for: 2 -> 2; matrix products, arithmetic and copies ran while one was open for 0% -> 0% of each run, Pallas kernels for 5% -> 4%
where the time goes in v6:
time: 74 us; the launch traced here: 73.6 us
  blocking collectives  39.8 us (54%)
  starting transfers between devices  19.1 us (26%)
  waiting for transfers between devices  7.45 us (10%)
  Pallas kernels  6.51 us (9%)
    all_to_all x3, blocking collectives, to_all(): return lax.all_to_all(value, axis, split_axis=0, concat_axis=0, tiled=True)  39.8 us
    all_to_all x1, starting transfers between devices, to_all(): return lax.all_to_all(value, axis, split_axis=0, concat_axis=0, tiled=True)  13.7 us
    pallas_call x8, Pallas kernels, run(): kernel(*(pltpu.with_memory_space_constraint(arg, pltpu.HBM) if spec is HB...  6.51 us
    all_to_all x1, waiting for transfers between devices, to_all(): return lax.all_to_all(value, axis, split_axis=0, concat_axis=0, tiled=True)  5.55 us
    ppermute x4, starting transfers between devices, group_shift(): lax.ppermute(value, 'group', [(g, (g + step) % GROUPS) for g in range(GRO...  5.4 us
    ppermute x4, waiting for transfers between devices, group_shift(): lax.ppermute(value, 'group', [(g, (g + step) % GROUPS) for g in range(GRO...  1.9 us
  transfers between devices with their start and end apart: 5, of which 2 were waited for; matrix products, arithmetic and copies ran while one was open for 0% of the time, Pallas kernels for 4%

profile of v6, /device:TPU:1, one launch (start us, length us, event | category | flops | bytes accessed | tf_op | source)
XLA Modules:
  0.0 73.6 jit_solution(11345225503005879570)
XLA Ops:
  0.6 1.7 %shard_map.104 = bf16[32,16,128]{2,1,0:T(8,128)(2,1)} custom-call(f32[8,128]{1,0:T(8,128)} %bitcast.13, bf16[128,256]{1,0:T(8,128)(2,1)} %bitcast.11), custom_call_target="tpu_custom_call" | custom-call | tf_op jit(solution)/shard_map/pallas_call | solution.py:29
  2.3 13.7 %all-to-all-start = ((bf16[32,16,128]{2,1,0:T(8,128)(2,1)}), bf16[32,16,128]{2,1,0:T(8,128)(2,1)S(1)}, u32[]{:S(2)}, u32[]{:S(2)}) async-start(bf16[32,16,128]{2,1,0:T(8,128)(2,1)} %shard_map.104), calls=%async_computation | async-start | bytes 262144 | tf_op jit(solution)/shard_map/all_to_all | solution.py:77
  16.1 1.6 %shard_map.105 = (bf16[80,1024]{1,0:T(8,128)(2,1)S(1)}, bf16[12,256,256]{2,1,0:T(8,128)(2,1)S(1)}, bf16[64,512]{1,0:T(8,128)(2,1)S(1)}, bf16[256,128]{1,0:T(8,128)(2,1)S(1)}, f32[1,128]{1,0:T(1,128)S(1)}) custom-call(bf16[12,256,256]{2,1,0:T(8,128)(2,1)} %tiles_hbm.1, bf16[64,1024]{1,0:T(8,128)(2,1)} %blocks_hbm.1, s32[2,64]{1,0:T(2,128)} %bitcast.14, ...), custom_call_target="tpu_custom_call" | custom-call | tf_op jit(solution)/shard_map/pallas_call | solution.py:29
  17.7 2.1 %collective-permute-start = (bf16[80,1024]{1,0:T(8,128)(2,1)S(1)}, bf16[80,1024]{1,0:T(8,128)(2,1)S(1)}, u32[]{:S(2)}, u32[]{:S(2)}) collective-permute-start(bf16[80,1024]{1,0:T(8,128)(2,1)S(1)} %get-tuple-element.21.own_ref), channel_id=1, source_target_pairs={{0,32},{32,64},{64,96},{96,128},{128,160},{160,192},{192,224},{224... | collective-permute-start | bytes 491528 | tf_op jit(solution)/shard_map/ppermute | solution.py:81
  19.8 0.0 collective-permute-start.1
  19.9 5.5 %all-to-all-done = bf16[32,16,128]{2,1,0:T(8,128)(2,1)S(1)} async-done(((bf16[32,16,128]{2,1,0:T(8,128)(2,1)}), bf16[32,16,128]{2,1,0:T(8,128)(2,1)S(1)}, u32[]{:S(2)}, u32[]{:S(2)}) %all-to-all-start) | async-done | bytes 131104 | tf_op jit(solution)/shard_map/all_to_all | solution.py:77
  25.4 0.1 shard_map.107.own_coef_ref
  25.5 3.2 %collective-permute-start.2 = (bf16[32,128]{1,0:T(8,128)(2,1)S(1)}, bf16[32,128]{1,0:T(8,128)(2,1)S(1)}, u32[]{:S(2)}, u32[]{:S(2)}) collective-permute-start(bf16[32,128]{1,0:T(8,128)(2,1)S(1)} %shard_map.107.own_coef_ref), channel_id=1, source_target_pairs={{0,32},{32,64},{64,96},{96,128},{128,160},{160,192},{192,224},{224... | collective-permute-start | bytes 24584 | tf_op jit(solution)/shard_map/ppermute | solution.py:81
  28.8 0.0 collective-permute-start.3
  28.8 0.0 collective-permute-done.before_ref
  28.8 0.0 collective-permute-done.1.after_ref
  28.8 0.0 copy-start
  28.8 0.0 copy-start.1
  28.8 1.1 %shard_map.106 = (f32[256,128]{1,0:T(8,128)S(1)}, bf16[256,96]{1,0:T(8,128)(2,1)S(1)}, f32[256,128]{1,0:T(8,128)S(1)}, f32[256,128]{1,0:T(8,128)S(1)}, bf16[4,32...) custom-call(bf16[512,128]{1,0:T(8,128)(2,1)S(1)} %bitcast.10, ...), custom_call_target="tpu_custom_call" | custom-call | tf_op jit(solution)/shard_map/pallas_call | solution.py:29
  30.0 0.0 collective-permute-done.2.before_coef_ref
  30.0 1.9 %collective-permute-done.3.after_coef_ref = bf16[32,128]{1,0:T(8,128)(2,1)S(1)} collective-permute-done((bf16[32,128]{1,0:T(8,128)(2,1)S(1)}, bf16[32,128]{1,0:T(8,128)(2,1)S(1)}, u32[]{:S(2)}, u32[]{:S(2)}) %collective-permute-start.3) | collective-permute-done | bytes 8224 | tf_op jit(solution)/shard_map/ppermute | solution.py:81
  31.9 0.8 %shard_map.108 = bf16[32,16,128]{2,1,0:T(8,128)(2,1)S(1)} custom-call(f32[256,128]{1,0:T(8,128)S(1)} %get-tuple-element.22.near_ref, bf16[80,1024]{1,0:T(8,128)(2,1)S(1)} %get-tuple-element.21.own_ref, bf16[80,1024]{1,0:T(8,128)(2,1)S(1)} %collective-permute-done.before_ref, bf16[80,1024]{1,0:T(8,128)(2,1)S(1)} %collective-permute-done.1.after_ref, ...), custom_call_target="tpu_custom_call" | custom-call | tf_op jit(solution)/shard_map/pallas_call | solution.py:29
  32.7 12.5 %all_to_all.20.pieces_ref = bf16[32,16,128]{2,1,0:T(8,128)(2,1)S(1)} all-to-all(bf16[32,16,128]{2,1,0:T(8,128)(2,1)S(1)} %shard_map.108), channel_id=1, replica_groups=mesh['group'=16,'dev'=32] {'dev'}, dimensions={0} | all-to-all | bytes 262144 | tf_op jit(solution)/shard_map/all_to_all | solution.py:77
  45.2 0.0 copy-done
  45.2 0.0 copy-done.1
  45.2 0.3 shard_map.109
  45.5 15.7 %all_to_all.21.pieces_ref = f32[16,1,128]{2,1,0:T(1,128)S(1)} all-to-all(f32[16,1,128]{2,1,0:T(1,128)S(1)} %get-tuple-element.30), channel_id=1, replica_groups=mesh['group'=16,'dev'=32] {'group'}, dimensions={0} | all-to-all | bytes 16384 | tf_op jit(solution)/shard_map/all_to_all | solution.py:77
  61.3 11.5 %all_to_all.22.refs_0_ = f32[32,1,128]{2,1,0:T(1,128)S(1)} all-to-all(f32[32,1,128]{2,1,0:T(1,128)S(1)} %shard_map.110), channel_id=1, replica_groups=mesh['group'=16,'dev'=32] {'dev'}, dimensions={0} | all-to-all | bytes 32768 | tf_op jit(solution)/shard_map/all_to_all | solution.py:77
  72.8 0.8 %shard_map.111 = (f32[8,128]{1,0:T(8,128)}, f32[1,8]{1,0:T(1,128)}) custom-call(f32[32,1,128]{2,1,0:T(1,128)S(1)} %all_to_all.22.refs_0_, f32[8,128]{1,0:T(8,128)S(1)} %get-tuple-element.31.refs_1_, f32[8,1024]{1,0:T(8,128)S(1)} %copy-done), custom_call_target="tpu_custom_call" | custom-call | tf_op jit(solution)/shard_map/pallas_call | solution.py:29
  (1 shorter events, 0.0 us)
Async XLA Ops:
  2.3 23.1 %all-to-all-start = ((bf16[32,16,128]{2,1,0:T(8,128)(2,1)}), bf16[32,16,128]{2,1,0:T(8,128)(2,1)S(1)}, u32[]{:S(2)}, u32[]{:S(2)}) async-start(bf16[32,16,128]{2,1,0:T(8,128)(2,1)} %shard_map.104), calls=%async_computation | async-start | bytes 262144 | tf_op jit(solution)/shard_map/all_to_all | solution.py:77
  17.7 11.1 %collective-permute-start = (bf16[80,1024]{1,0:T(8,128)(2,1)S(1)}, bf16[80,1024]{1,0:T(8,128)(2,1)S(1)}, u32[]{:S(2)}, u32[]{:S(2)}) collective-permute-start(bf16[80,1024]{1,0:T(8,128)(2,1)S(1)} %get-tuple-element.21.own_ref), channel_id=1, source_target_pairs={{0,32},{32,64},{64,96},{96,128},{128,160},{160,192},{192,224},{224... | collective-permute-start | bytes 491528 | tf_op jit(solution)/shard_map/ppermute | solution.py:81
  19.8 8.9 %collective-permute-start.1 = (bf16[80,1024]{1,0:T(8,128)(2,1)S(1)}, bf16[80,1024]{1,0:T(8,128)(2,1)S(1)}, u32[]{:S(2)}, u32[]{:S(2)}) collective-permute-start(bf16[80,1024]{1,0:T(8,128)(2,1)S(1)} %get-tuple-element.21.own_ref), channel_id=1, source_target_pairs={{0,480},{32,0},{64,32},{96,64},{128,96},{160,128},{192,160},{224,1... | collective-permute-start | bytes 491528 | tf_op jit(solution)/shard_map/ppermute | solution.py:81
  25.5 4.4 %collective-permute-start.2 = (bf16[32,128]{1,0:T(8,128)(2,1)S(1)}, bf16[32,128]{1,0:T(8,128)(2,1)S(1)}, u32[]{:S(2)}, u32[]{:S(2)}) collective-permute-start(bf16[32,128]{1,0:T(8,128)(2,1)S(1)} %shard_map.107.own_coef_ref), channel_id=1, source_target_pairs={{0,32},{32,64},{64,96},{96,128},{128,160},{160,192},{192,224},{224... | collective-permute-start | bytes 24584 | tf_op jit(solution)/shard_map/ppermute | solution.py:81
  28.8 3.1 %collective-permute-start.3 = (bf16[32,128]{1,0:T(8,128)(2,1)S(1)}, bf16[32,128]{1,0:T(8,128)(2,1)S(1)}, u32[]{:S(2)}, u32[]{:S(2)}) collective-permute-start(bf16[32,128]{1,0:T(8,128)(2,1)S(1)} %shard_map.107.own_coef_ref), channel_id=1, source_target_pairs={{0,480},{32,0},{64,32},{96,64},{128,96},{160,128},{192,160},{224,1... | collective-permute-start | bytes 24584 | tf_op jit(solution)/shard_map/ppermute | solution.py:81
  28.8 16.4 %copy-start = (f32[8,1024]{1,0:T(8,128)S(1)}, f32[8,1024]{1,0:T(8,128)}, u32[]{:S(2)}) copy-start(f32[8,1024]{1,0:T(8,128)} %refs_2_.1) | copy-start | bytes 98308
  28.8 16.4 %copy-start.1 = (bf16[4,32,256]{2,1,0:T(8,128)(2,1)S(1)}, bf16[4,32,256]{2,1,0:T(8,128)(2,1)}, u32[]{:S(2)}) copy-start(bf16[4,32,256]{2,1,0:T(8,128)(2,1)} %param.11) | copy-start | bytes 196612

commit v7 on v6

--- a/solution.py
+++ b/solution.py
@@ -12,6 +12,7 @@
 DEVS, GROUPS = NZ * NX, 2 * NY
 VMEM = pl.BlockSpec(memory_space=pltpu.VMEM)
 HBM = pl.BlockSpec(memory_space=pltpu.HBM)
+SMEM = pl.BlockSpec(memory_space=pltpu.SMEM)
 sds = jax.ShapeDtypeStruct
 
 
@@ -59,6 +60,12 @@
     return high, (value - high.astype(F32)).astype(BF16)
 
 
+def thirds(value):
+    first = value.astype(BF16).astype(F32)
+    second = (value - first).astype(BF16).astype(F32)
+    return first, second, (value - first - second).astype(BF16).astype(F32)
+
+
 def one_hot(mask):
     return mask.astype(F32).astype(BF16)
 
@@ -73,8 +80,10 @@
     return mm_t(same, small(rows)).astype(I32)
 
 
-def to_all(value, axis):
-    return lax.all_to_all(value, axis, split_axis=0, concat_axis=0, tiled=True)
+def to_all(value, axis, index_groups=None):
+    return lax.all_to_all(
+        value, axis, split_axis=0, concat_axis=0, tiled=True, axis_index_groups=index_groups
+    )
 
 
 def group_shift(value, step):
@@ -104,8 +113,8 @@
         out_ref[d] = packed
 
 
-def prep_body(tiles_hbm, blocks_hbm, pairs_hbm, mask_hbm, near_pairs_hbm, near_mask_hbm, krylov_hbm,
-              out_ref, tiles_ref, gather_ref, scatter_ref, gram_ref,
+def prep_body(x_ref, tiles_hbm, blocks_hbm, pairs_hbm, mask_hbm, near_pairs_hbm, near_mask_hbm,
+              krylov_hbm, bases_hbm, out_ref, tiles_ref, gather_ref, scatter_ref, row_ref, here_ref,
               pairs_ref, mask_ref, near_pairs_ref, near_mask_ref, krylov_ref, sems, tile_sem):
     fetched = pltpu.make_async_copy(tiles_hbm, tiles_ref, tile_sem)
     slots = blocks_hbm.shape[0]
@@ -116,6 +125,7 @@
         (near_pairs_hbm, near_pairs_ref),
         (near_mask_hbm, near_mask_ref),
         (krylov_hbm, krylov_ref),
+        (bases_hbm, row_ref.at[0:128]),
     )
     copies = started(ends, sems)
     fetched.start()
@@ -159,9 +169,19 @@
     lane, row = iota((8, 128), 1) - 8, iota((8, 128), 0)
     inside = (lane >= 0) & (lane < 64)
     wide = mm_exact(gram, jnp.where(inside & ((lane & 7) == row), 1.0, 0.0), ((1,), (0,)))
-    gram_ref[...] = jnp.sum(
-        jnp.where(inside & ((lane >> 3) == row), wide, 0.0), axis=0, keepdims=True
-    )
+    gram = jnp.sum(jnp.where(inside & ((lane >> 3) == row), wide, 0.0), axis=0, keepdims=True)
+    for t, part in enumerate(thirds(rows)):
+        for b in range(2):
+            left, right = part[:, b * 512 : b * 512 + 256], part[:, b * 512 + 256 : b * 512 + 512]
+            at = 128 + t * 32 + b * 16
+            row_ref[at : at + 16, :] = jnp.concatenate([left, right], axis=0).astype(BF16)
+    row = iota((16, 128), 0)
+    tail = jnp.zeros((16, 128), F32)
+    for t, part in enumerate(thirds(gram)):
+        tail = jnp.where(row == t, part, tail)
+    row_ref[224:240, 0:128] = tail.astype(BF16)
+    row_ref[224:240, 128:256] = jnp.zeros((16, 128), BF16)
+    here_ref[...] = jnp.where(iota((NX, 8, 128), 0) == x_ref[0], 1.0, 0.0)
     fetched.wait()
 
 
@@ -220,7 +240,8 @@
 
 
 def far_body(near_ref, own_ref, before_ref, after_ref, own_coef_ref, before_coef_ref,
-             after_coef_ref, pick_ref, lanes_ref, keep_ref, owner_ref, take_ref, give_ref, out_ref):
+             after_coef_ref, pick_ref, lanes_ref, keep_ref, owner_ref, take_ref, give_ref, row_ref, out_ref,
+             rows_ref):
     bundles = (own_ref, before_ref, after_ref)
     slots = own_ref.shape[0] - 16
     coeffs = jnp.concatenate([own_coef_ref[...], before_coef_ref[...], after_coef_ref[...]], axis=0)
@@ -247,26 +268,56 @@
     for d in range(DEVS):
         near = near_ref[d * 8 : d * 8 + 8, :]
         low = jnp.where(row == 7, total[d : d + 1, :], near - near.astype(BF16).astype(F32))
-        out_ref[d] = jnp.concatenate([near, low], axis=0).astype(BF16)
-
-
-def product_body(pieces_ref, bases_ref, krylov_ref, gram_ref, product_ref, copies_ref):
+        at = d % NX * 16
+        out_ref[d // NX, at : at + 16, :] = jnp.concatenate([near, low], axis=0).astype(BF16)
+    for x in range(NX):
+        rows_ref[x] = row_ref[...]
+
+
+def middle_body(pieces_ref, out_ref):
     total = jnp.sum(pieces_ref[...].astype(F32), axis=0)
+    row = iota((8, 128), 0)
+    nears = []
+    fars = jnp.zeros((8, 128), F32)
+    for x in range(NX):
+        high, low = total[x * 16 : x * 16 + 8, :], total[x * 16 + 8 : x * 16 + 16, :]
+        nears.append(high + jnp.where(row == 7, 0.0, low))
+        fars = jnp.where(row == x, low[7:8, :], fars)
+    both = jnp.concatenate(nears + [fars], axis=0)
+    for x in range(NX):
+        out_ref[x] = both
+
+
+def product_body(pieces_ref, rows_ref, here_ref, product_ref, copies_ref):
+    total = jnp.sum(pieces_ref[...], axis=0)
     row, lane = iota((8, 128), 0), iota((8, 128), 1)
-    near = total[0:8, :] + jnp.where(row == 7, 0.0, total[8:16, :])
-    coef = total[15:16, :].astype(BF16).astype(F32)
-    spread = jnp.where((lane >> 5) == (row >> 1), coef, 0.0).astype(BF16)
-    low = mm(spread, bases_ref[:, :128])
-    high = mm(spread, bases_ref[:, 128:])
-    product = near + jnp.where((row & 1) == 0, low, high)
-    product_ref[...] = product
-    acc = jnp.zeros((8, 128), F32)
-    for r in range(8):
-        acc = acc + krylov_ref[:, r * 128 : r * 128 + 128] * product[r : r + 1, :]
+    acc, square, own = (jnp.zeros((8, 128), F32) for _ in range(3))
+    gram = jnp.zeros((1, 128), F32)
+    for m in range(NX):
+        coef = total[32 + m : 33 + m, :].astype(BF16).astype(F32)
+        spread = jnp.where((lane >> 5) == (row >> 1), coef, 0.0).astype(BF16)
+        low = mm(spread, rows_ref[m, 0:128, 0:128])
+        high = mm(spread, rows_ref[m, 0:128, 128:256])
+        product = total[m * 8 : m * 8 + 8, :] + jnp.where((row & 1) == 0, low, high)
+        own = jnp.where(here_ref[m] > 0.5, product, own)
+        square = square + product * product
+        for b in range(2):
+            parts = [
+                rows_ref[m, 128 + t * 32 + b * 16 : 144 + t * 32 + b * 16, :].astype(F32)
+                for t in range(3)
+            ]
+            krylov = (parts[0] + parts[1]) + parts[2]
+            for r in range(4):
+                at = (r >> 1) * 8, (r & 1) * 128
+                part = krylov[at[0] : at[0] + 8, at[1] : at[1] + 128]
+                acc = acc + part * product[b * 4 + r : b * 4 + r + 1, :]
+        parts = rows_ref[m, 224:240, 0:128].astype(F32)
+        gram = gram + ((parts[0:1, :] + parts[1:2, :]) + parts[2:3, :])
+    product_ref[...] = own
     proj = jnp.sum(acc, axis=1, keepdims=True)
-    square = jnp.sum(product * product, axis=1, keepdims=True)
+    square = jnp.sum(square, axis=1, keepdims=True)
     values = jnp.where(lane == row, proj, 0.0) + jnp.where(lane == 72, square, 0.0)
-    payload = jnp.sum(values, axis=0, keepdims=True) + gram_ref[...]
+    payload = jnp.sum(values, axis=0, keepdims=True) + gram
     for d in range(copies_ref.shape[0]):
         copies_ref[d] = payload
 
@@ -309,26 +360,31 @@
         [pltpu.VMEM((8, 128), F32), pltpu.VMEM(rank_rows.shape, BF16), pltpu.SemaphoreType.DMA((2,))],
     )(direction.reshape(8, 128), rank_rows)
     gathered = to_all(copies, "dev").reshape(-1, 128)
-    bundle, tiles, gather, scatter, gram = call(
+    x = (lax.axis_index("dev") & (NX - 1)).astype(I32)[None]
+    bundle, tiles, gather, scatter, row, here = call(
         prep_body,
         [
             sds((far_slots + 16, far_blocks.shape[1]), BF16),
             pltpu.VMEM(near_tiles.shape, BF16),
             sds((64, DEVS * 16), BF16),
             sds((DEVS * 8, 128), BF16),
-            sds((1, 128), F32),
+            sds((240, 256), BF16),
+            pltpu.VMEM((NX, 8, 128), F32),
         ],
-        [HBM] * 7,
+        [SMEM] + [HBM] * 8,
         [
             pltpu.VMEM((2, far_slots), I32),
             pltpu.VMEM((1, far_slots), I32),
             pltpu.VMEM((2, slots), I32),
             pltpu.VMEM((1, slots), I32),
             pltpu.VMEM(krylov.shape, F32),
-            pltpu.SemaphoreType.DMA((6,)),
+            pltpu.SemaphoreType.DMA((7,)),
             pltpu.SemaphoreType.DMA,
         ],
-    )(near_tiles, far_blocks, far_pairs.T, far_mask[None], near_pairs.T, near_mask[None], krylov)
+    )(
+        x, near_tiles, far_blocks, far_pairs.T, far_mask[None], near_pairs.T, near_mask[None], krylov,
+        rank_rows,
+    )
     before, after = group_shift(bundle, 1), group_shift(bundle, -1)
 
     coeffs = call(coeffs_body, sds((DEVS, 128), BF16), [VMEM])(gathered)
@@ -346,14 +402,21 @@
         ],
         [VMEM] * 7,
     )(gathered, gather, scatter, tiles, bundle, before, after)
-    parts = call(far_body, sds((DEVS, 16, 128), BF16), [VMEM] * 13)(
-        near, bundle, before, after, coeffs, coeffs_before, coeffs_after, *far_prepared
-    )
+    parts, rows = call(
+        far_body,
+        [sds((NZ, NX * 16, 128), BF16), sds((NX, 240, 256), BF16)],
+        [VMEM] * 14,
+    )(near, bundle, before, after, coeffs, coeffs_before, coeffs_after, *far_prepared, row)
+    along_x = [[z * NX + x for x in range(NX)] for z in range(NZ)]
+    along_z = [[z * NX + x for z in range(NZ)] for x in range(NX)]
+    parts = to_all(parts, "dev", along_z)
+    rows = to_all(rows, "dev", along_x)
+    parts = call(middle_body, sds((NX, 40, 128), F32), [VMEM])(parts)
     product, copies = call(
-        product_body, [sds((8, 128), F32), sds((GROUPS, 1, 128), F32)], [VMEM] * 4
-    )(to_all(parts, "dev"), rank_rows, krylov, gram)
-    copies = call(spread_body, sds((DEVS, 1, 128), F32), [VMEM])(to_all(copies, "group"))
-    pieces = to_all(copies, "dev")
+        product_body, [sds((8, 128), F32), sds((GROUPS, 1, 128), F32)], [VMEM] * 3
+    )(to_all(parts, "dev", along_x), rows, here)
+    copies = call(spread_body, sds((NZ, 1, 128), F32), [VMEM])(to_all(copies, "group"))
+    pieces = to_all(copies, "dev", along_z)
     count = float(panels * DEVS * GROUPS)
 
     def finish(*refs):

time: 74 us -> 87.4 us (1.18)
  blocking collectives: 39.8 us -> 53.1 us
    all_to_all x3 -> x5, blocking collectives: 39.8 us -> 53.1 us  [to_all(): lax.all_to_all(value, axis, split_axis=0, concat_axis=0, tiled=True, axis...]
    pallas_call x8 -> x9, Pallas kernels: 6.51 us -> 6.57 us  [run(): kernel(*(pltpu.with_memory_space_constraint(arg, pltpu.HBM) if spec is HB...]
  transfers between devices with their start and end apart: 5 -> 5, of which waited for: 2 -> 2; matrix products, arithmetic and copies ran while one was open for 0% -> 0% of each run, Pallas kernels for 4% -> 3%
where the time goes in v7:
time: 87.4 us; the launch traced here: 87 us
  blocking collectives  53.1 us (61%)
  starting transfers between devices  19.1 us (22%)
  waiting for transfers between devices  7.43 us (9%)
  Pallas kernels  6.57 us (8%)
    all_to_all x5, blocking collectives, to_all(): lax.all_to_all(value, axis, split_axis=0, concat_axis=0, tiled=True, axis...  53.1 us
    all_to_all x1, starting transfers between devices, to_all(): lax.all_to_all(value, axis, split_axis=0, concat_axis=0, tiled=True, axis...  13.7 us
    pallas_call x9, Pallas kernels, run(): kernel(*(pltpu.with_memory_space_constraint(arg, pltpu.HBM) if spec is HB...  6.57 us
    all_to_all x1, waiting for transfers between devices, to_all(): lax.all_to_all(value, axis, split_axis=0, concat_axis=0, tiled=True, axis...  5.5 us
    ppermute x4, starting transfers between devices, group_shift(): lax.ppermute(value, 'group', [(g, (g + step) % GROUPS) for g in range(GRO...  5.4 us
    ppermute x4, waiting for transfers between devices, group_shift(): lax.ppermute(value, 'group', [(g, (g + step) % GROUPS) for g in range(GRO...  1.93 us
  transfers between devices with their start and end apart: 5, of which 2 were waited for; matrix products, arithmetic and copies ran while one was open for 0% of the time, Pallas kernels for 3%

profile of v7, /device:TPU:1, one launch (start us, length us, event | category | flops | bytes accessed | tf_op | source)
XLA Modules:
  0.0 87.0 jit_solution(10317355954353573644)
XLA Ops:
  0.6 1.7 %shard_map.104 = bf16[32,16,128]{2,1,0:T(8,128)(2,1)} custom-call(f32[8,128]{1,0:T(8,128)} %bitcast.14, bf16[128,256]{1,0:T(8,128)(2,1)} %bitcast.12), custom_call_target="tpu_custom_call" | custom-call | tf_op jit(solution)/shard_map/pallas_call | solution.py:30
  2.3 13.7 %all-to-all-start = ((bf16[32,16,128]{2,1,0:T(8,128)(2,1)}), bf16[32,16,128]{2,1,0:T(8,128)(2,1)S(1)}, u32[]{:S(2)}, u32[]{:S(2)}) async-start(bf16[32,16,128]{2,1,0:T(8,128)(2,1)} %shard_map.104), calls=%async_computation | async-start | bytes 262144 | tf_op jit(solution)/shard_map/all_to_all | solution.py:84
  16.1 1.7 %shard_map.105 = (bf16[80,1024]{1,0:T(8,128)(2,1)S(1)}, bf16[12,256,256]{2,1,0:T(8,128)(2,1)S(1)}, bf16[64,512]{1,0:T(8,128)(2,1)S(1)}, bf16[256,128]{1,0:T(8,12...) custom-call(s32[1]{0:T(128)} %bitcast.3.x_ref, bf16[12,256,256]{2,1,0:T(8,128)(2,1)} %tiles_hbm.1, ...), custom_call_target="tpu_custom_call" | custom-call | tf_op jit(solution)/shard_map/pallas_call | solution.py:30
  17.7 2.1 %collective-permute-start = (bf16[80,1024]{1,0:T(8,128)(2,1)S(1)}, bf16[80,1024]{1,0:T(8,128)(2,1)S(1)}, u32[]{:S(2)}, u32[]{:S(2)}) collective-permute-start(bf16[80,1024]{1,0:T(8,128)(2,1)S(1)} %get-tuple-element.24.own_ref), channel_id=1, source_target_pairs={{0,32},{32,64},{64,96},{96,128},{128,160},{160,192},{192,224},{224... | collective-permute-start | bytes 491528 | tf_op jit(solution)/shard_map/ppermute | solution.py:90
  19.9 0.0 collective-permute-start.1
  19.9 5.5 %all-to-all-done = bf16[32,16,128]{2,1,0:T(8,128)(2,1)S(1)} async-done(((bf16[32,16,128]{2,1,0:T(8,128)(2,1)}), bf16[32,16,128]{2,1,0:T(8,128)(2,1)S(1)}, u32[]{:S(2)}, u32[]{:S(2)}) %all-to-all-start) | async-done | bytes 131104 | tf_op jit(solution)/shard_map/all_to_all | solution.py:84
  25.4 0.1 shard_map.107.own_coef_ref
  25.5 3.2 %collective-permute-start.2 = (bf16[32,128]{1,0:T(8,128)(2,1)S(1)}, bf16[32,128]{1,0:T(8,128)(2,1)S(1)}, u32[]{:S(2)}, u32[]{:S(2)}) collective-permute-start(bf16[32,128]{1,0:T(8,128)(2,1)S(1)} %shard_map.107.own_coef_ref), channel_id=1, source_target_pairs={{0,32},{32,64},{64,96},{96,128},{128,160},{160,192},{192,224},{224... | collective-permute-start | bytes 24584 | tf_op jit(solution)/shard_map/ppermute | solution.py:90
  28.8 0.0 collective-permute-start.3
  28.8 0.0 collective-permute-done.before_ref
  28.8 0.0 collective-permute-done.1.after_ref
  28.8 1.1 %shard_map.106 = (f32[256,128]{1,0:T(8,128)S(1)}, bf16[256,96]{1,0:T(8,128)(2,1)S(1)}, f32[256,128]{1,0:T(8,128)S(1)}, f32[256,128]{1,0:T(8,128)S(1)}, bf16[4,32...) custom-call(bf16[512,128]{1,0:T(8,128)(2,1)S(1)} %bitcast.11, ...), custom_call_target="tpu_custom_call" | custom-call | tf_op jit(solution)/shard_map/pallas_call | solution.py:30
  29.9 0.0 collective-permute-done.2.before_coef_ref
  29.9 1.9 %collective-permute-done.3.after_coef_ref = bf16[32,128]{1,0:T(8,128)(2,1)S(1)} collective-permute-done((bf16[32,128]{1,0:T(8,128)(2,1)S(1)}, bf16[32,128]{1,0:T(8,128)(2,1)S(1)}, u32[]{:S(2)}, u32[]{:S(2)}) %collective-permute-start.3) | collective-permute-done | bytes 8224 | tf_op jit(solution)/shard_map/ppermute | solution.py:90
  31.9 0.0 copy-start
  31.9 0.8 shard_map.108
  32.7 11.4 %all_to_all.30.pieces_ref = bf16[8,64,128]{2,1,0:T(8,128)(2,1)S(1)} all-to-all(bf16[8,64,128]{2,1,0:T(8,128)(2,1)S(1)} %get-tuple-element.33), channel_id=1, replica_groups={{0,4,8,12,16,20,24,28},{1,5,9,13,17,21,25,29},{2,6,10,14,18,22,26,30},{..., dimensions={0} | all-to-all | bytes 262144 | tf_op jit(solution)/shard_map/all_to_all | solution.py:84
  44.1 6.9 %all_to_all.31.pieces_ref = f32[4,40,128]{2,1,0:T(8,128)S(1)} all-to-all(f32[4,40,128]{2,1,0:T(8,128)S(1)} %shard_map.109), channel_id=1, replica_groups={{0,1,2,3},{4,5,6,7},{8,9,10,11},{12,13,14,15},{16,17,18,19},{20,21,22,2..., dimensions={0} | all-to-all | bytes 163840 | tf_op jit(solution)/shard_map/all_to_all | solution.py:84
  51.0 9.1 %all_to_all.32.rows_ref = bf16[4,240,256]{2,1,0:T(8,128)(2,1)S(1)} all-to-all(bf16[4,240,256]{2,1,0:T(8,128)(2,1)S(1)} %get-tuple-element.34), channel_id=1, replica_groups={{0,1,2,3},{4,5,6,7},{8,9,10,11},{12,13,14,15},{16,17,18,19},{20,21,22,2..., dimensions={0} | all-to-all | bytes 983040 | tf_op jit(solution)/shard_map/all_to_all | solution.py:84
  60.2 0.3 shard_map.110
  60.4 16.8 %all_to_all.33.pieces_ref = f32[16,1,128]{2,1,0:T(1,128)S(1)} all-to-all(f32[16,1,128]{2,1,0:T(1,128)S(1)} %get-tuple-element.36), channel_id=1, replica_groups=mesh['group'=16,'dev'=32] {'group'}, dimensions={0} | all-to-all | bytes 16384 | tf_op jit(solution)/shard_map/all_to_all | solution.py:84
  77.3 8.9 %all_to_all.34.refs_0_ = f32[8,1,128]{2,1,0:T(1,128)S(1)} all-to-all(f32[8,1,128]{2,1,0:T(1,128)S(1)} %shard_map.111), channel_id=1, replica_groups={{0,4,8,12,16,20,24,28},{1,5,9,13,17,21,25,29},{2,6,10,14,18,22,26,30},{..., dimensions={0} | all-to-all | bytes 8192 | tf_op jit(solution)/shard_map/all_to_all | solution.py:84
  86.2 0.0 copy-done
  86.2 0.8 shard_map.112
  (2 shorter events, 0.0 us)
Async XLA Ops:
  2.3 23.1 %all-to-all-start = ((bf16[32,16,128]{2,1,0:T(8,128)(2,1)}), bf16[32,16,128]{2,1,0:T(8,128)(2,1)S(1)}, u32[]{:S(2)}, u32[]{:S(2)}) async-start(bf16[32,16,128]{2,1,0:T(8,128)(2,1)} %shard_map.104), calls=%async_computation | async-start | bytes 262144 | tf_op jit(solution)/shard_map/all_to_all | solution.py:84
  17.7 11.0 %collective-permute-start = (bf16[80,1024]{1,0:T(8,128)(2,1)S(1)}, bf16[80,1024]{1,0:T(8,128)(2,1)S(1)}, u32[]{:S(2)}, u32[]{:S(2)}) collective-permute-start(bf16[80,1024]{1,0:T(8,128)(2,1)S(1)} %get-tuple-element.24.own_ref), channel_id=1, source_target_pairs={{0,32},{32,64},{64,96},{96,128},{128,160},{160,192},{192,224},{224... | collective-permute-start | bytes 491528 | tf_op jit(solution)/shard_map/ppermute | solution.py:90
  19.9 8.9 %collective-permute-start.1 = (bf16[80,1024]{1,0:T(8,128)(2,1)S(1)}, bf16[80,1024]{1,0:T(8,128)(2,1)S(1)}, u32[]{:S(2)}, u32[]{:S(2)}) collective-permute-start(bf16[80,1024]{1,0:T(8,128)(2,1)S(1)} %get-tuple-element.24.own_ref), channel_id=1, source_target_pairs={{0,480},{32,0},{64,32},{96,64},{128,96},{160,128},{192,160},{224,1... | collective-permute-start | bytes 491528 | tf_op jit(solution)/shard_map/ppermute | solution.py:90
  25.5 4.4 %collective-permute-start.2 = (bf16[32,128]{1,0:T(8,128)(2,1)S(1)}, bf16[32,128]{1,0:T(8,128)(2,1)S(1)}, u32[]{:S(2)}, u32[]{:S(2)}) collective-permute-start(bf16[32,128]{1,0:T(8,128)(2,1)S(1)} %shard_map.107.own_coef_ref), channel_id=1, source_target_pairs={{0,32},{32,64},{64,96},{96,128},{128,160},{160,192},{192,224},{224... | collective-permute-start | bytes 24584 | tf_op jit(solution)/shard_map/ppermute | solution.py:90
  28.8 3.1 %collective-permute-start.3 = (bf16[32,128]{1,0:T(8,128)(2,1)S(1)}, bf16[32,128]{1,0:T(8,128)(2,1)S(1)}, u32[]{:S(2)}, u32[]{:S(2)}) collective-permute-start(bf16[32,128]{1,0:T(8,128)(2,1)S(1)} %shard_map.107.own_coef_ref), channel_id=1, source_target_pairs={{0,480},{32,0},{64,32},{96,64},{128,96},{160,128},{192,160},{224,1... | collective-permute-start | bytes 24584 | tf_op jit(solution)/shard_map/ppermute | solution.py:90
  31.9 54.3 %copy-start = (f32[8,1024]{1,0:T(8,128)S(1)}, f32[8,1024]{1,0:T(8,128)}, u32[]{:S(2)}) copy-start(f32[8,1024]{1,0:T(8,128)} %refs_2_.1) | copy-start | bytes 98308

commit v8 on v6

--- a/solution.py
+++ b/solution.py
@@ -73,8 +73,15 @@
     return mm_t(same, small(rows)).astype(I32)
 
 
+def snake(dev):
+    return dev ^ (((dev >> 2) & 1) * (NX - 1))
+
+
 def to_all(value, axis):
-    return lax.all_to_all(value, axis, split_axis=0, concat_axis=0, tiled=True)
+    order = [[snake(k) for k in range(DEVS)]] if axis == "dev" else None
+    return lax.all_to_all(
+        value, axis, split_axis=0, concat_axis=0, tiled=True, axis_index_groups=order
+    )
 
 
 def group_shift(value, step):
@@ -143,7 +150,7 @@
     i_col, j_col = info_cols[:, 0:1], info_cols[:, 1:2]
     m = iota((64, 1), 0) >> 4
     c = jnp.where(m < 2, j_col, i_col)
-    place = (c >> 2) * 16 + (c & 3) * 2 + (m & 1)
+    place = snake(c >> 2) * 16 + (c & 3) * 2 + (m & 1)
     gather_ref[...] = one_hot(iota((64, DEVS * 16), 1) == place)
     lane = iota((near_slots, 128), 1)
     pick = one_hot((lane & 15) == iota((near_slots, 128), 0))
@@ -166,7 +173,7 @@
 
 
 def coeffs_body(gathered_ref, out_ref):
-    rows = iota((DEVS, DEVS * 16), 0) * 16 + 8
+    rows = snake(iota((DEVS, DEVS * 16), 0)) * 16 + 8
     pick = one_hot(iota((DEVS, DEVS * 16), 1) == rows)
     out_ref[...] = mm(pick, gathered_ref[...]).astype(BF16)
 
@@ -247,7 +254,7 @@
     for d in range(DEVS):
         near = near_ref[d * 8 : d * 8 + 8, :]
         low = jnp.where(row == 7, total[d : d + 1, :], near - near.astype(BF16).astype(F32))
-        out_ref[d] = jnp.concatenate([near, low], axis=0).astype(BF16)
+        out_ref[snake(d)] = jnp.concatenate([near, low], axis=0).astype(BF16)
 
 
 def product_body(pieces_ref, bases_ref, krylov_ref, gram_ref, product_ref, copies_ref):

time: 74 us -> 74 us (level)
  no operation moved by 1% of the time
where the time goes in v8:
time: 74 us; the launch traced here: 73.6 us
  blocking collectives  39.8 us (54%)
  starting transfers between devices  19 us (26%)
  waiting for transfers between devices  7.57 us (10%)
  Pallas kernels  6.51 us (9%)
    all_to_all x3, blocking collectives, to_all(): lax.all_to_all(value, axis, split_axis=0, concat_axis=0, tiled=True, axis...  39.8 us
    all_to_all x1, starting transfers between devices, to_all(): lax.all_to_all(value, axis, split_axis=0, concat_axis=0, tiled=True, axis...  13.7 us
    pallas_call x8, Pallas kernels, run(): kernel(*(pltpu.with_memory_space_constraint(arg, pltpu.HBM) if spec is HB...  6.51 us
    all_to_all x1, waiting for transfers between devices, to_all(): lax.all_to_all(value, axis, split_axis=0, concat_axis=0, tiled=True, axis...  5.67 us
    ppermute x4, starting transfers between devices, group_shift(): lax.ppermute(value, 'group', [(g, (g + step) % GROUPS) for g in range(GRO...  5.29 us
    ppermute x4, waiting for transfers between devices, group_shift(): lax.ppermute(value, 'group', [(g, (g + step) % GROUPS) for g in range(GRO...  1.9 us
  transfers between devices with their start and end apart: 5, of which 2 were waited for; matrix products, arithmetic and copies ran while one was open for 0% of the time, Pallas kernels for 4%

profile of v8, /device:TPU:1, one launch (start us, length us, event | category | flops | bytes accessed | tf_op | source)
XLA Modules:
  0.0 73.6 jit_solution(4521652505076647286)
XLA Ops:
  0.6 1.7 %shard_map.104 = bf16[32,16,128]{2,1,0:T(8,128)(2,1)} custom-call(f32[8,128]{1,0:T(8,128)} %bitcast.13, bf16[128,256]{1,0:T(8,128)(2,1)} %bitcast.11), custom_call_target="tpu_custom_call" | custom-call | tf_op jit(solution)/shard_map/pallas_call | solution.py:29
  2.3 13.7 %all-to-all-start = ((bf16[32,16,128]{2,1,0:T(8,128)(2,1)}), bf16[32,16,128]{2,1,0:T(8,128)(2,1)S(1)}, u32[]{:S(2)}, u32[]{:S(2)}) async-start(bf16[32,16,128]{2,1,0:T(8,128)(2,1)} %shard_map.104), calls=%async_computation | async-start | bytes 262144 | tf_op jit(solution)/shard_map/all_to_all | solution.py:82
  16.1 1.6 %shard_map.105 = (bf16[80,1024]{1,0:T(8,128)(2,1)S(1)}, bf16[12,256,256]{2,1,0:T(8,128)(2,1)S(1)}, bf16[64,512]{1,0:T(8,128)(2,1)S(1)}, bf16[256,128]{1,0:T(8,128)(2,1)S(1)}, f32[1,128]{1,0:T(1,128)S(1)}) custom-call(bf16[12,256,256]{2,1,0:T(8,128)(2,1)} %tiles_hbm.1, bf16[64,1024]{1,0:T(8,128)(2,1)} %blocks_hbm.1, s32[2,64]{1,0:T(2,128)} %bitcast.14, ...), custom_call_target="tpu_custom_call" | custom-call | tf_op jit(solution)/shard_map/pallas_call | solution.py:29
  17.7 2.1 %collective-permute-start = (bf16[80,1024]{1,0:T(8,128)(2,1)S(1)}, bf16[80,1024]{1,0:T(8,128)(2,1)S(1)}, u32[]{:S(2)}, u32[]{:S(2)}) collective-permute-start(bf16[80,1024]{1,0:T(8,128)(2,1)S(1)} %get-tuple-element.21.own_ref), channel_id=1, source_target_pairs={{0,32},{32,64},{64,96},{96,128},{128,160},{160,192},{192,224},{224... | collective-permute-start | bytes 491528 | tf_op jit(solution)/shard_map/ppermute | solution.py:88
  19.8 0.0 collective-permute-start.1
  19.9 5.7 %all-to-all-done = bf16[32,16,128]{2,1,0:T(8,128)(2,1)S(1)} async-done(((bf16[32,16,128]{2,1,0:T(8,128)(2,1)}), bf16[32,16,128]{2,1,0:T(8,128)(2,1)S(1)}, u32[]{:S(2)}, u32[]{:S(2)}) %all-to-all-start) | async-done | bytes 131104 | tf_op jit(solution)/shard_map/all_to_all | solution.py:82
  25.5 0.1 shard_map.107.own_coef_ref
  25.7 3.1 %collective-permute-start.2 = (bf16[32,128]{1,0:T(8,128)(2,1)S(1)}, bf16[32,128]{1,0:T(8,128)(2,1)S(1)}, u32[]{:S(2)}, u32[]{:S(2)}) collective-permute-start(bf16[32,128]{1,0:T(8,128)(2,1)S(1)} %shard_map.107.own_coef_ref), channel_id=1, source_target_pairs={{0,32},{32,64},{64,96},{96,128},{128,160},{160,192},{192,224},{224... | collective-permute-start | bytes 24584 | tf_op jit(solution)/shard_map/ppermute | solution.py:88
  28.8 0.0 collective-permute-start.3
  28.8 0.0 collective-permute-done.before_ref
  28.8 0.0 collective-permute-done.1.after_ref
  28.8 0.0 copy-start
  28.8 0.0 copy-start.1
  28.8 1.1 %shard_map.106 = (f32[256,128]{1,0:T(8,128)S(1)}, bf16[256,96]{1,0:T(8,128)(2,1)S(1)}, f32[256,128]{1,0:T(8,128)S(1)}, f32[256,128]{1,0:T(8,128)S(1)}, bf16[4,32...) custom-call(bf16[512,128]{1,0:T(8,128)(2,1)S(1)} %bitcast.10, ...), custom_call_target="tpu_custom_call" | custom-call | tf_op jit(solution)/shard_map/pallas_call | solution.py:29
  30.0 0.0 collective-permute-done.2.before_coef_ref
  30.0 1.9 %collective-permute-done.3.after_coef_ref = bf16[32,128]{1,0:T(8,128)(2,1)S(1)} collective-permute-done((bf16[32,128]{1,0:T(8,128)(2,1)S(1)}, bf16[32,128]{1,0:T(8,128)(2,1)S(1)}, u32[]{:S(2)}, u32[]{:S(2)}) %collective-permute-start.3) | collective-permute-done | bytes 8224 | tf_op jit(solution)/shard_map/ppermute | solution.py:88
  31.9 0.8 %shard_map.108 = bf16[32,16,128]{2,1,0:T(8,128)(2,1)S(1)} custom-call(f32[256,128]{1,0:T(8,128)S(1)} %get-tuple-element.22.near_ref, bf16[80,1024]{1,0:T(8,128)(2,1)S(1)} %get-tuple-element.21.own_ref, bf16[80,1024]{1,0:T(8,128)(2,1)S(1)} %collective-permute-done.before_ref, bf16[80,1024]{1,0:T(8,128)(2,1)S(1)} %collective-permute-done.1.after_ref, ...), custom_call_target="tpu_custom_call" | custom-call | tf_op jit(solution)/shard_map/pallas_call | solution.py:29
  32.7 12.5 %all_to_all.20.pieces_ref = bf16[32,16,128]{2,1,0:T(8,128)(2,1)S(1)} all-to-all(bf16[32,16,128]{2,1,0:T(8,128)(2,1)S(1)} %shard_map.108), channel_id=1, replica_groups={{0,1,2,3,7,6,5,4,8,9,10,11,15,14,13,12,16,17,18,19,23,22,21,20,24,25,26..., dimensions={0} | all-to-all | bytes 262144 | tf_op jit(solution)/shard_map/all_to_all | solution.py:82
  45.2 0.0 copy-done
  45.2 0.0 copy-done.1
  45.2 0.3 shard_map.109
  45.5 15.8 %all_to_all.21.pieces_ref = f32[16,1,128]{2,1,0:T(1,128)S(1)} all-to-all(f32[16,1,128]{2,1,0:T(1,128)S(1)} %get-tuple-element.30), channel_id=1, replica_groups=mesh['group'=16,'dev'=32] {'group'}, dimensions={0} | all-to-all | bytes 16384 | tf_op jit(solution)/shard_map/all_to_all | solution.py:82
  61.3 11.6 %all_to_all.22.refs_0_ = f32[32,1,128]{2,1,0:T(1,128)S(1)} all-to-all(f32[32,1,128]{2,1,0:T(1,128)S(1)} %shard_map.110), channel_id=1, replica_groups={{0,1,2,3,7,6,5,4,8,9,10,11,15,14,13,12,16,17,18,19,23,22,21,20,24,25,26..., dimensions={0} | all-to-all | bytes 32768 | tf_op jit(solution)/shard_map/all_to_all | solution.py:82
  72.8 0.8 %shard_map.111 = (f32[8,128]{1,0:T(8,128)}, f32[1,8]{1,0:T(1,128)}) custom-call(f32[32,1,128]{2,1,0:T(1,128)S(1)} %all_to_all.22.refs_0_, f32[8,128]{1,0:T(8,128)S(1)} %get-tuple-element.31.refs_1_, f32[8,1024]{1,0:T(8,128)S(1)} %copy-done), custom_call_target="tpu_custom_call" | custom-call | tf_op jit(solution)/shard_map/pallas_call | solution.py:29
  (1 shorter events, 0.0 us)
Async XLA Ops:
  2.3 23.2 %all-to-all-start = ((bf16[32,16,128]{2,1,0:T(8,128)(2,1)}), bf16[32,16,128]{2,1,0:T(8,128)(2,1)S(1)}, u32[]{:S(2)}, u32[]{:S(2)}) async-start(bf16[32,16,128]{2,1,0:T(8,128)(2,1)} %shard_map.104), calls=%async_computation | async-start | bytes 262144 | tf_op jit(solution)/shard_map/all_to_all | solution.py:82
  17.7 11.1 %collective-permute-start = (bf16[80,1024]{1,0:T(8,128)(2,1)S(1)}, bf16[80,1024]{1,0:T(8,128)(2,1)S(1)}, u32[]{:S(2)}, u32[]{:S(2)}) collective-permute-start(bf16[80,1024]{1,0:T(8,128)(2,1)S(1)} %get-tuple-element.21.own_ref), channel_id=1, source_target_pairs={{0,32},{32,64},{64,96},{96,128},{128,160},{160,192},{192,224},{224... | collective-permute-start | bytes 491528 | tf_op jit(solution)/shard_map/ppermute | solution.py:88
  19.8 8.9 %collective-permute-start.1 = (bf16[80,1024]{1,0:T(8,128)(2,1)S(1)}, bf16[80,1024]{1,0:T(8,128)(2,1)S(1)}, u32[]{:S(2)}, u32[]{:S(2)}) collective-permute-start(bf16[80,1024]{1,0:T(8,128)(2,1)S(1)} %get-tuple-element.21.own_ref), channel_id=1, source_target_pairs={{0,480},{32,0},{64,32},{96,64},{128,96},{160,128},{192,160},{224,1... | collective-permute-start | bytes 491528 | tf_op jit(solution)/shard_map/ppermute | solution.py:88
  25.7 4.3 %collective-permute-start.2 = (bf16[32,128]{1,0:T(8,128)(2,1)S(1)}, bf16[32,128]{1,0:T(8,128)(2,1)S(1)}, u32[]{:S(2)}, u32[]{:S(2)}) collective-permute-start(bf16[32,128]{1,0:T(8,128)(2,1)S(1)} %shard_map.107.own_coef_ref), channel_id=1, source_target_pairs={{0,32},{32,64},{64,96},{96,128},{128,160},{160,192},{192,224},{224... | collective-permute-start | bytes 24584 | tf_op jit(solution)/shard_map/ppermute | solution.py:88
  28.8 3.1 %collective-permute-start.3 = (bf16[32,128]{1,0:T(8,128)(2,1)S(1)}, bf16[32,128]{1,0:T(8,128)(2,1)S(1)}, u32[]{:S(2)}, u32[]{:S(2)}) collective-permute-start(bf16[32,128]{1,0:T(8,128)(2,1)S(1)} %shard_map.107.own_coef_ref), channel_id=1, source_target_pairs={{0,480},{32,0},{64,32},{96,64},{128,96},{160,128},{192,160},{224,1... | collective-permute-start | bytes 24584 | tf_op jit(solution)/shard_map/ppermute | solution.py:88
  28.8 16.4 %copy-start = (f32[8,1024]{1,0:T(8,128)S(1)}, f32[8,1024]{1,0:T(8,128)}, u32[]{:S(2)}) copy-start(f32[8,1024]{1,0:T(8,128)} %refs_2_.1) | copy-start | bytes 98308
  28.8 16.4 %copy-start.1 = (bf16[4,32,256]{2,1,0:T(8,128)(2,1)S(1)}, bf16[4,32,256]{2,1,0:T(8,128)(2,1)}, u32[]{:S(2)}) copy-start(bf16[4,32,256]{2,1,0:T(8,128)(2,1)} %param.11) | copy-start | bytes 196612

commit v9 on v6

--- a/solution.py
+++ b/solution.py
@@ -171,7 +171,7 @@
     out_ref[...] = mm(pick, gathered_ref[...]).astype(BF16)
 
 
-def near_body(gathered_ref, gather_ref, scatter_ref, tiles_ref, own_ref, before_ref, after_ref,
+def near_body(gathered_ref, gather_ref, scatter_ref, tiles_ref, own_ref, after_ref, before_ref,
               out_ref, *far_refs):
     far_prep(own_ref, before_ref, after_ref, *far_refs)
     taken = mm(gather_ref[...], gathered_ref[...])
@@ -219,8 +219,8 @@
         give_ref[k] = one_hot((lane & 31) == 4 * k + (sub >> 5))
 
 
-def far_body(near_ref, own_ref, before_ref, after_ref, own_coef_ref, before_coef_ref,
-             after_coef_ref, pick_ref, lanes_ref, keep_ref, owner_ref, take_ref, give_ref, out_ref):
+def far_body(near_ref, own_ref, after_ref, before_ref, own_coef_ref, after_coef_ref,
+             before_coef_ref, pick_ref, lanes_ref, keep_ref, owner_ref, take_ref, give_ref, out_ref):
     bundles = (own_ref, before_ref, after_ref)
     slots = own_ref.shape[0] - 16
     coeffs = jnp.concatenate([own_coef_ref[...], before_coef_ref[...], after_coef_ref[...]], axis=0)
@@ -329,10 +329,10 @@
             pltpu.SemaphoreType.DMA,
         ],
     )(near_tiles, far_blocks, far_pairs.T, far_mask[None], near_pairs.T, near_mask[None], krylov)
-    before, after = group_shift(bundle, 1), group_shift(bundle, -1)
+    after, before = group_shift(bundle, -1), group_shift(bundle, 1)
 
     coeffs = call(coeffs_body, sds((DEVS, 128), BF16), [VMEM])(gathered)
-    coeffs_before, coeffs_after = group_shift(coeffs, 1), group_shift(coeffs, -1)
+    coeffs_after, coeffs_before = group_shift(coeffs, -1), group_shift(coeffs, 1)
     near, *far_prepared = call(
         near_body,
         [
@@ -345,9 +345,9 @@
             pltpu.VMEM((8, 128, 128), BF16),
         ],
         [VMEM] * 7,
-    )(gathered, gather, scatter, tiles, bundle, before, after)
+    )(gathered, gather, scatter, tiles, bundle, after, before)
     parts = call(far_body, sds((DEVS, 16, 128), BF16), [VMEM] * 13)(
-        near, bundle, before, after, coeffs, coeffs_before, coeffs_after, *far_prepared
+        near, bundle, after, before, coeffs, coeffs_after, coeffs_before, *far_prepared
     )
     product, copies = call(
         product_body, [sds((8, 128), F32), sds((GROUPS, 1, 128), F32)], [VMEM] * 4

time: 74 us -> 73.9 us (level)
  waiting for transfers between devices: 7.45 us -> 5.69 us
  blocking collectives: 39.8 us -> 41.5 us
    ppermute x4, waiting for transfers between devices: 1.9 us -> 0.16 us  [group_shift(): lax.ppermute(value, 'group', [(g, (g + step) % GROUPS) for g in range(GRO...]
    all_to_all x3, blocking collectives: 39.8 us -> 41.5 us  [to_all(): return lax.all_to_all(value, axis, split_axis=0, concat_axis=0, tiled=True)]
where the time goes in v9:
time: 73.9 us; the launch traced here: 73.6 us
  blocking collectives  41.5 us (56%)
  starting transfers between devices  19.2 us (26%)
  Pallas kernels  6.51 us (9%)
  waiting for transfers between devices  5.69 us (8%)
    all_to_all x3, blocking collectives, to_all(): return lax.all_to_all(value, axis, split_axis=0, concat_axis=0, tiled=True)  41.5 us
    all_to_all x1, starting transfers between devices, to_all(): return lax.all_to_all(value, axis, split_axis=0, concat_axis=0, tiled=True)  13.7 us
    pallas_call x8, Pallas kernels, run(): kernel(*(pltpu.with_memory_space_constraint(arg, pltpu.HBM) if spec is HB...  6.51 us
    all_to_all x1, waiting for transfers between devices, to_all(): return lax.all_to_all(value, axis, split_axis=0, concat_axis=0, tiled=True)  5.53 us
    ppermute x4, starting transfers between devices, group_shift(): lax.ppermute(value, 'group', [(g, (g + step) % GROUPS) for g in range(GRO...  5.44 us
  transfers between devices with their start and end apart: 5, of which 2 were waited for; matrix products, arithmetic and copies ran while one was open for 0% of the time, Pallas kernels for 4%

profile of v9, /device:TPU:1, one launch (start us, length us, event | category | flops | bytes accessed | tf_op | source)
XLA Modules:
  0.0 73.6 jit_solution(902238806747346024)
XLA Ops:
  0.6 1.7 %shard_map.104 = bf16[32,16,128]{2,1,0:T(8,128)(2,1)} custom-call(f32[8,128]{1,0:T(8,128)} %bitcast.13, bf16[128,256]{1,0:T(8,128)(2,1)} %bitcast.11), custom_call_target="tpu_custom_call" | custom-call | tf_op jit(solution)/shard_map/pallas_call | solution.py:29
  2.3 13.7 %all-to-all-start = ((bf16[32,16,128]{2,1,0:T(8,128)(2,1)}), bf16[32,16,128]{2,1,0:T(8,128)(2,1)S(1)}, u32[]{:S(2)}, u32[]{:S(2)}) async-start(bf16[32,16,128]{2,1,0:T(8,128)(2,1)} %shard_map.104), calls=%async_computation | async-start | bytes 262144 | tf_op jit(solution)/shard_map/all_to_all | solution.py:77
  16.1 1.6 %shard_map.105 = (bf16[80,1024]{1,0:T(8,128)(2,1)S(1)}, bf16[12,256,256]{2,1,0:T(8,128)(2,1)S(1)}, bf16[64,512]{1,0:T(8,128)(2,1)S(1)}, bf16[256,128]{1,0:T(8,128)(2,1)S(1)}, f32[1,128]{1,0:T(1,128)S(1)}) custom-call(bf16[12,256,256]{2,1,0:T(8,128)(2,1)} %tiles_hbm.1, bf16[64,1024]{1,0:T(8,128)(2,1)} %blocks_hbm.1, s32[2,64]{1,0:T(2,128)} %bitcast.14, ...), custom_call_target="tpu_custom_call" | custom-call | tf_op jit(solution)/shard_map/pallas_call | solution.py:29
  17.7 1.0 %collective-permute-start = (bf16[80,1024]{1,0:T(8,128)(2,1)S(1)}, bf16[80,1024]{1,0:T(8,128)(2,1)S(1)}, u32[]{:S(2)}, u32[]{:S(2)}) collective-permute-start(bf16[80,1024]{1,0:T(8,128)(2,1)S(1)} %get-tuple-element.21.own_ref), channel_id=1, source_target_pairs={{0,480},{32,0},{64,32},{96,64},{128,96},{160,128},{192,160},{224,1... | collective-permute-start | bytes 491528 | tf_op jit(solution)/shard_map/ppermute | solution.py:81
  18.7 1.2 %collective-permute-start.1 = (bf16[80,1024]{1,0:T(8,128)(2,1)S(1)}, bf16[80,1024]{1,0:T(8,128)(2,1)S(1)}, u32[]{:S(2)}, u32[]{:S(2)}) collective-permute-start(bf16[80,1024]{1,0:T(8,128)(2,1)S(1)} %get-tuple-element.21.own_ref), channel_id=1, source_target_pairs={{0,32},{32,64},{64,96},{96,128},{128,160},{160,192},{192,224},{224... | collective-permute-start | bytes 491528 | tf_op jit(solution)/shard_map/ppermute | solution.py:81
  19.9 5.5 %all-to-all-done = bf16[32,16,128]{2,1,0:T(8,128)(2,1)S(1)} async-done(((bf16[32,16,128]{2,1,0:T(8,128)(2,1)}), bf16[32,16,128]{2,1,0:T(8,128)(2,1)S(1)}, u32[]{:S(2)}, u32[]{:S(2)}) %all-to-all-start) | async-done | bytes 131104 | tf_op jit(solution)/shard_map/all_to_all | solution.py:77
  25.4 0.1 shard_map.107.own_coef_ref
  25.5 2.1 %collective-permute-start.2 = (bf16[32,128]{1,0:T(8,128)(2,1)S(1)}, bf16[32,128]{1,0:T(8,128)(2,1)S(1)}, u32[]{:S(2)}, u32[]{:S(2)}) collective-permute-start(bf16[32,128]{1,0:T(8,128)(2,1)S(1)} %shard_map.107.own_coef_ref), channel_id=1, source_target_pairs={{0,480},{32,0},{64,32},{96,64},{128,96},{160,128},{192,160},{224,1... | collective-permute-start | bytes 24584 | tf_op jit(solution)/shard_map/ppermute | solution.py:81
  27.6 1.2 %collective-permute-start.3 = (bf16[32,128]{1,0:T(8,128)(2,1)S(1)}, bf16[32,128]{1,0:T(8,128)(2,1)S(1)}, u32[]{:S(2)}, u32[]{:S(2)}) collective-permute-start(bf16[32,128]{1,0:T(8,128)(2,1)S(1)} %shard_map.107.own_coef_ref), channel_id=1, source_target_pairs={{0,32},{32,64},{64,96},{96,128},{128,160},{160,192},{192,224},{224... | collective-permute-start | bytes 24584 | tf_op jit(solution)/shard_map/ppermute | solution.py:81
  28.8 0.0 collective-permute-done.after_ref
  28.8 0.0 collective-permute-done.1.before_ref
  28.8 0.0 copy-start
  28.8 0.0 copy-start.1
  28.8 1.1 %shard_map.106 = (f32[256,128]{1,0:T(8,128)S(1)}, bf16[256,96]{1,0:T(8,128)(2,1)S(1)}, f32[256,128]{1,0:T(8,128)S(1)}, f32[256,128]{1,0:T(8,128)S(1)}, bf16[4,32...) custom-call(bf16[512,128]{1,0:T(8,128)(2,1)S(1)} %bitcast.10, ...), custom_call_target="tpu_custom_call" | custom-call | tf_op jit(solution)/shard_map/pallas_call | solution.py:29
  30.0 0.2 collective-permute-done.2.after_coef_ref
  30.1 0.0 collective-permute-done.3.before_coef_ref
  30.1 0.8 %shard_map.108 = bf16[32,16,128]{2,1,0:T(8,128)(2,1)S(1)} custom-call(f32[256,128]{1,0:T(8,128)S(1)} %get-tuple-element.22.near_ref, bf16[80,1024]{1,0:T(8,128)(2,1)S(1)} %get-tuple-element.21.own_ref, bf16[80,1024]{1,0:T(8,128)(2,1)S(1)} %collective-permute-done.after_ref, bf16[80,1024]{1,0:T(8,128)(2,1)S(1)} %collective-permute-done.1.before_ref, ...), custom_call_target="tpu_custom_call" | custom-call | tf_op jit(solution)/shard_map/pallas_call | solution.py:29
  31.0 13.3 %all_to_all.20.pieces_ref = bf16[32,16,128]{2,1,0:T(8,128)(2,1)S(1)} all-to-all(bf16[32,16,128]{2,1,0:T(8,128)(2,1)S(1)} %shard_map.108), channel_id=1, replica_groups=mesh['group'=16,'dev'=32] {'dev'}, dimensions={0} | all-to-all | bytes 262144 | tf_op jit(solution)/shard_map/all_to_all | solution.py:77
  44.3 0.0 copy-done
  44.3 0.0 copy-done.1
  44.3 0.3 shard_map.109
  44.5 16.6 %all_to_all.21.pieces_ref = f32[16,1,128]{2,1,0:T(1,128)S(1)} all-to-all(f32[16,1,128]{2,1,0:T(1,128)S(1)} %get-tuple-element.30), channel_id=1, replica_groups=mesh['group'=16,'dev'=32] {'group'}, dimensions={0} | all-to-all | bytes 16384 | tf_op jit(solution)/shard_map/all_to_all | solution.py:77
  61.2 11.6 %all_to_all.22.refs_0_ = f32[32,1,128]{2,1,0:T(1,128)S(1)} all-to-all(f32[32,1,128]{2,1,0:T(1,128)S(1)} %shard_map.110), channel_id=1, replica_groups=mesh['group'=16,'dev'=32] {'dev'}, dimensions={0} | all-to-all | bytes 32768 | tf_op jit(solution)/shard_map/all_to_all | solution.py:77
  72.7 0.8 %shard_map.111 = (f32[8,128]{1,0:T(8,128)}, f32[1,8]{1,0:T(1,128)}) custom-call(f32[32,1,128]{2,1,0:T(1,128)S(1)} %all_to_all.22.refs_0_, f32[8,128]{1,0:T(8,128)S(1)} %get-tuple-element.31.refs_1_, f32[8,1024]{1,0:T(8,128)S(1)} %copy-done), custom_call_target="tpu_custom_call" | custom-call | tf_op jit(solution)/shard_map/pallas_call | solution.py:29
  (1 shorter events, 0.0 us)
Async XLA Ops:
  2.3 23.1 %all-to-all-start = ((bf16[32,16,128]{2,1,0:T(8,128)(2,1)}), bf16[32,16,128]{2,1,0:T(8,128)(2,1)S(1)}, u32[]{:S(2)}, u32[]{:S(2)}) async-start(bf16[32,16,128]{2,1,0:T(8,128)(2,1)} %shard_map.104), calls=%async_computation | async-start | bytes 262144 | tf_op jit(solution)/shard_map/all_to_all | solution.py:77
  17.7 11.1 %collective-permute-start = (bf16[80,1024]{1,0:T(8,128)(2,1)S(1)}, bf16[80,1024]{1,0:T(8,128)(2,1)S(1)}, u32[]{:S(2)}, u32[]{:S(2)}) collective-permute-start(bf16[80,1024]{1,0:T(8,128)(2,1)S(1)} %get-tuple-element.21.own_ref), channel_id=1, source_target_pairs={{0,480},{32,0},{64,32},{96,64},{128,96},{160,128},{192,160},{224,1... | collective-permute-start | bytes 491528 | tf_op jit(solution)/shard_map/ppermute | solution.py:81
  18.7 10.1 %collective-permute-start.1 = (bf16[80,1024]{1,0:T(8,128)(2,1)S(1)}, bf16[80,1024]{1,0:T(8,128)(2,1)S(1)}, u32[]{:S(2)}, u32[]{:S(2)}) collective-permute-start(bf16[80,1024]{1,0:T(8,128)(2,1)S(1)} %get-tuple-element.21.own_ref), channel_id=1, source_target_pairs={{0,32},{32,64},{64,96},{96,128},{128,160},{160,192},{192,224},{224... | collective-permute-start | bytes 491528 | tf_op jit(solution)/shard_map/ppermute | solution.py:81
  25.5 4.6 %collective-permute-start.2 = (bf16[32,128]{1,0:T(8,128)(2,1)S(1)}, bf16[32,128]{1,0:T(8,128)(2,1)S(1)}, u32[]{:S(2)}, u32[]{:S(2)}) collective-permute-start(bf16[32,128]{1,0:T(8,128)(2,1)S(1)} %shard_map.107.own_coef_ref), channel_id=1, source_target_pairs={{0,480},{32,0},{64,32},{96,64},{128,96},{160,128},{192,160},{224,1... | collective-permute-start | bytes 24584 | tf_op jit(solution)/shard_map/ppermute | solution.py:81
  27.6 2.5 %collective-permute-start.3 = (bf16[32,128]{1,0:T(8,128)(2,1)S(1)}, bf16[32,128]{1,0:T(8,128)(2,1)S(1)}, u32[]{:S(2)}, u32[]{:S(2)}) collective-permute-start(bf16[32,128]{1,0:T(8,128)(2,1)S(1)} %shard_map.107.own_coef_ref), channel_id=1, source_target_pairs={{0,32},{32,64},{64,96},{96,128},{128,160},{160,192},{192,224},{224... | collective-permute-start | bytes 24584 | tf_op jit(solution)/shard_map/ppermute | solution.py:81
  28.8 15.5 %copy-start = (f32[8,1024]{1,0:T(8,128)S(1)}, f32[8,1024]{1,0:T(8,128)}, u32[]{:S(2)}) copy-start(f32[8,1024]{1,0:T(8,128)} %refs_2_.1) | copy-start | bytes 98308
  28.8 15.5 %copy-start.1 = (bf16[4,32,256]{2,1,0:T(8,128)(2,1)S(1)}, bf16[4,32,256]{2,1,0:T(8,128)(2,1)}, u32[]{:S(2)}) copy-start(bf16[4,32,256]{2,1,0:T(8,128)(2,1)} %param.11) | copy-start | bytes 196612

commit v10 on v6

--- a/solution.py
+++ b/solution.py
@@ -224,10 +224,10 @@
     bundles = (own_ref, before_ref, after_ref)
     slots = own_ref.shape[0] - 16
     coeffs = jnp.concatenate([own_coef_ref[...], before_coef_ref[...], after_coef_ref[...]], axis=0)
-    taken = (mm(pick_ref[...], coeffs) * lanes_ref[...]).astype(BF16)
-    right, left = taken[0:slots], taken[slots:]
-    sub, lane = iota((128, 128), 0), iota((128, 128), 1)
-    tiled = mm(right, one_hot((sub & 31) == (lane & 31)))
+    taken = mm(pick_ref[...], coeffs) * lanes_ref[...]
+    right, left = taken[0:slots], taken[slots:].astype(BF16)
+    tiled = right + pltpu.roll(right, 64, 1)
+    tiled = tiled + pltpu.roll(tiled, 32, 1)
     forward = jnp.zeros((slots, 128), F32)
     backward = jnp.zeros(left.shape, F32)
     for k in range(8):
@@ -244,17 +244,20 @@
         for part in halves(sums[k * slots : k * slots + slots]):
             total = total + mm(owner_ref[k], part)
     row = iota((8, 128), 0)
+    far_high = total.astype(BF16).astype(F32)
+    far_low = total - far_high
     for d in range(DEVS):
         near = near_ref[d * 8 : d * 8 + 8, :]
-        low = jnp.where(row == 7, total[d : d + 1, :], near - near.astype(BF16).astype(F32))
-        out_ref[d] = jnp.concatenate([near, low], axis=0).astype(BF16)
+        near_low = near - near.astype(BF16).astype(F32)
+        tail = jnp.where(row == 0, far_high[d : d + 1, :], far_low[d : d + 1, :])
+        out_ref[d] = jnp.concatenate([near, near_low, tail], axis=0).astype(BF16)
 
 
 def product_body(pieces_ref, bases_ref, krylov_ref, gram_ref, product_ref, copies_ref):
     total = jnp.sum(pieces_ref[...].astype(F32), axis=0)
     row, lane = iota((8, 128), 0), iota((8, 128), 1)
-    near = total[0:8, :] + jnp.where(row == 7, 0.0, total[8:16, :])
-    coef = total[15:16, :].astype(BF16).astype(F32)
+    near = total[0:8, :] + total[8:16, :]
+    coef = (total[16:17, :] + total[17:18, :]).astype(BF16).astype(F32)
     spread = jnp.where((lane >> 5) == (row >> 1), coef, 0.0).astype(BF16)
     low = mm(spread, bases_ref[:, :128])
     high = mm(spread, bases_ref[:, 128:])
@@ -346,7 +349,7 @@
         ],
         [VMEM] * 7,
     )(gathered, gather, scatter, tiles, bundle, before, after)
-    parts = call(far_body, sds((DEVS, 16, 128), BF16), [VMEM] * 13)(
+    parts = call(far_body, sds((DEVS, 24, 128), BF16), [VMEM] * 13)(
         near, bundle, before, after, coeffs, coeffs_before, coeffs_after, *far_prepared
     )
     product, copies = call(

time: 74 us -> 75.1 us (1.015)
  blocking collectives: 39.8 us -> 41 us
    all_to_all x3, blocking collectives: 39.8 us -> 41 us  [to_all(): return lax.all_to_all(value, axis, split_axis=0, concat_axis=0, tiled=True)]
where the time goes in v10:
time: 75.1 us; the launch traced here: 74.8 us
  blocking collectives  41 us (55%)
  starting transfers between devices  19.1 us (25%)
  waiting for transfers between devices  7.45 us (10%)
  Pallas kernels  6.53 us (9%)
    all_to_all x3, blocking collectives, to_all(): return lax.all_to_all(value, axis, split_axis=0, concat_axis=0, tiled=True)  41 us
    all_to_all x1, starting transfers between devices, to_all(): return lax.all_to_all(value, axis, split_axis=0, concat_axis=0, tiled=True)  13.7 us
    pallas_call x8, Pallas kernels, run(): kernel(*(pltpu.with_memory_space_constraint(arg, pltpu.HBM) if spec is HB...  6.53 us
    all_to_all x1, waiting for transfers between devices, to_all(): return lax.all_to_all(value, axis, split_axis=0, concat_axis=0, tiled=True)  5.55 us
    ppermute x4, starting transfers between devices, group_shift(): lax.ppermute(value, 'group', [(g, (g + step) % GROUPS) for g in range(GRO...  5.4 us
    ppermute x4, waiting for transfers between devices, group_shift(): lax.ppermute(value, 'group', [(g, (g + step) % GROUPS) for g in range(GRO...  1.9 us
  transfers between devices with their start and end apart: 5, of which 2 were waited for; matrix products, arithmetic and copies ran while one was open for 0% of the time, Pallas kernels for 4%

profile of v10, /device:TPU:1, one launch (start us, length us, event | category | flops | bytes accessed | tf_op | source)
XLA Modules:
  0.0 74.8 jit_solution(1890375147600801238)
XLA Ops:
  0.6 1.7 %shard_map.104 = bf16[32,16,128]{2,1,0:T(8,128)(2,1)} custom-call(f32[8,128]{1,0:T(8,128)} %bitcast.13, bf16[128,256]{1,0:T(8,128)(2,1)} %bitcast.11), custom_call_target="tpu_custom_call" | custom-call | tf_op jit(solution)/shard_map/pallas_call | solution.py:29
  2.3 13.7 %all-to-all-start = ((bf16[32,16,128]{2,1,0:T(8,128)(2,1)}), bf16[32,16,128]{2,1,0:T(8,128)(2,1)S(1)}, u32[]{:S(2)}, u32[]{:S(2)}) async-start(bf16[32,16,128]{2,1,0:T(8,128)(2,1)} %shard_map.104), calls=%async_computation | async-start | bytes 262144 | tf_op jit(solution)/shard_map/all_to_all | solution.py:77
  16.1 1.6 %shard_map.105 = (bf16[80,1024]{1,0:T(8,128)(2,1)S(1)}, bf16[12,256,256]{2,1,0:T(8,128)(2,1)S(1)}, bf16[64,512]{1,0:T(8,128)(2,1)S(1)}, bf16[256,128]{1,0:T(8,128)(2,1)S(1)}, f32[1,128]{1,0:T(1,128)S(1)}) custom-call(bf16[12,256,256]{2,1,0:T(8,128)(2,1)} %tiles_hbm.1, bf16[64,1024]{1,0:T(8,128)(2,1)} %blocks_hbm.1, s32[2,64]{1,0:T(2,128)} %bitcast.14, ...), custom_call_target="tpu_custom_call" | custom-call | tf_op jit(solution)/shard_map/pallas_call | solution.py:29
  17.7 2.1 %collective-permute-start = (bf16[80,1024]{1,0:T(8,128)(2,1)S(1)}, bf16[80,1024]{1,0:T(8,128)(2,1)S(1)}, u32[]{:S(2)}, u32[]{:S(2)}) collective-permute-start(bf16[80,1024]{1,0:T(8,128)(2,1)S(1)} %get-tuple-element.21.own_ref), channel_id=1, source_target_pairs={{0,32},{32,64},{64,96},{96,128},{128,160},{160,192},{192,224},{224... | collective-permute-start | bytes 491528 | tf_op jit(solution)/shard_map/ppermute | solution.py:81
  19.8 0.0 collective-permute-start.1
  19.9 5.5 %all-to-all-done = bf16[32,16,128]{2,1,0:T(8,128)(2,1)S(1)} async-done(((bf16[32,16,128]{2,1,0:T(8,128)(2,1)}), bf16[32,16,128]{2,1,0:T(8,128)(2,1)S(1)}, u32[]{:S(2)}, u32[]{:S(2)}) %all-to-all-start) | async-done | bytes 131104 | tf_op jit(solution)/shard_map/all_to_all | solution.py:77
  25.4 0.1 shard_map.107.own_coef_ref
  25.5 3.2 %collective-permute-start.2 = (bf16[32,128]{1,0:T(8,128)(2,1)S(1)}, bf16[32,128]{1,0:T(8,128)(2,1)S(1)}, u32[]{:S(2)}, u32[]{:S(2)}) collective-permute-start(bf16[32,128]{1,0:T(8,128)(2,1)S(1)} %shard_map.107.own_coef_ref), channel_id=1, source_target_pairs={{0,32},{32,64},{64,96},{96,128},{128,160},{160,192},{192,224},{224... | collective-permute-start | bytes 24584 | tf_op jit(solution)/shard_map/ppermute | solution.py:81
  28.8 0.0 collective-permute-start.3
  28.8 0.0 collective-permute-done.before_ref
  28.8 0.0 collective-permute-done.1.after_ref
  28.8 1.1 %shard_map.106 = (f32[256,128]{1,0:T(8,128)S(1)}, bf16[256,96]{1,0:T(8,128)(2,1)S(1)}, f32[256,128]{1,0:T(8,128)S(1)}, f32[256,128]{1,0:T(8,128)S(1)}, bf16[4,32...) custom-call(bf16[512,128]{1,0:T(8,128)(2,1)S(1)} %bitcast.10, ...), custom_call_target="tpu_custom_call" | custom-call | tf_op jit(solution)/shard_map/pallas_call | solution.py:29
  29.9 0.0 copy-start
  29.9 0.0 copy-start.1
  30.0 0.0 collective-permute-done.2.before_coef_ref
  30.0 1.9 %collective-permute-done.3.after_coef_ref = bf16[32,128]{1,0:T(8,128)(2,1)S(1)} collective-permute-done((bf16[32,128]{1,0:T(8,128)(2,1)S(1)}, bf16[32,128]{1,0:T(8,128)(2,1)S(1)}, u32[]{:S(2)}, u32[]{:S(2)}) %collective-permute-start.3) | collective-permute-done | bytes 8224 | tf_op jit(solution)/shard_map/ppermute | solution.py:81
  31.9 0.9 %shard_map.108 = bf16[32,24,128]{2,1,0:T(8,128)(2,1)S(1)} custom-call(f32[256,128]{1,0:T(8,128)S(1)} %get-tuple-element.22.near_ref, bf16[80,1024]{1,0:T(8,128)(2,1)S(1)} %get-tuple-element.21.own_ref, bf16[80,1024]{1,0:T(8,128)(2,1)S(1)} %collective-permute-done.before_ref, bf16[80,1024]{1,0:T(8,128)(2,1)S(1)} %collective-permute-done.1.after_ref, ...), custom_call_target="tpu_custom_call" | custom-call | tf_op jit(solution)/shard_map/pallas_call | solution.py:29
  32.7 13.8 %all_to_all.20.pieces_ref = bf16[32,24,128]{2,1,0:T(8,128)(2,1)S(1)} all-to-all(bf16[32,24,128]{2,1,0:T(8,128)(2,1)S(1)} %shard_map.108), channel_id=1, replica_groups=mesh['group'=16,'dev'=32] {'dev'}, dimensions={0} | all-to-all | bytes 393216 | tf_op jit(solution)/shard_map/all_to_all | solution.py:77
  46.5 0.0 copy-done
  46.5 0.0 copy-done.1
  46.5 0.3 shard_map.109
  46.8 15.4 %all_to_all.21.pieces_ref = f32[16,1,128]{2,1,0:T(1,128)S(1)} all-to-all(f32[16,1,128]{2,1,0:T(1,128)S(1)} %get-tuple-element.30), channel_id=1, replica_groups=mesh['group'=16,'dev'=32] {'group'}, dimensions={0} | all-to-all | bytes 16384 | tf_op jit(solution)/shard_map/all_to_all | solution.py:77
  62.2 11.8 %all_to_all.22.refs_0_ = f32[32,1,128]{2,1,0:T(1,128)S(1)} all-to-all(f32[32,1,128]{2,1,0:T(1,128)S(1)} %shard_map.110), channel_id=1, replica_groups=mesh['group'=16,'dev'=32] {'dev'}, dimensions={0} | all-to-all | bytes 32768 | tf_op jit(solution)/shard_map/all_to_all | solution.py:77
  74.0 0.8 %shard_map.111 = (f32[8,128]{1,0:T(8,128)}, f32[1,8]{1,0:T(1,128)}) custom-call(f32[32,1,128]{2,1,0:T(1,128)S(1)} %all_to_all.22.refs_0_, f32[8,128]{1,0:T(8,128)S(1)} %get-tuple-element.31.refs_1_, f32[8,1024]{1,0:T(8,128)S(1)} %copy-done), custom_call_target="tpu_custom_call" | custom-call | tf_op jit(solution)/shard_map/pallas_call | solution.py:29
  (1 shorter events, 0.0 us)
Async XLA Ops:
  2.3 23.1 %all-to-all-start = ((bf16[32,16,128]{2,1,0:T(8,128)(2,1)}), bf16[32,16,128]{2,1,0:T(8,128)(2,1)S(1)}, u32[]{:S(2)}, u32[]{:S(2)}) async-start(bf16[32,16,128]{2,1,0:T(8,128)(2,1)} %shard_map.104), calls=%async_computation | async-start | bytes 262144 | tf_op jit(solution)/shard_map/all_to_all | solution.py:77
  17.7 11.1 %collective-permute-start = (bf16[80,1024]{1,0:T(8,128)(2,1)S(1)}, bf16[80,1024]{1,0:T(8,128)(2,1)S(1)}, u32[]{:S(2)}, u32[]{:S(2)}) collective-permute-start(bf16[80,1024]{1,0:T(8,128)(2,1)S(1)} %get-tuple-element.21.own_ref), channel_id=1, source_target_pairs={{0,32},{32,64},{64,96},{96,128},{128,160},{160,192},{192,224},{224... | collective-permute-start | bytes 491528 | tf_op jit(solution)/shard_map/ppermute | solution.py:81
  19.8 8.9 %collective-permute-start.1 = (bf16[80,1024]{1,0:T(8,128)(2,1)S(1)}, bf16[80,1024]{1,0:T(8,128)(2,1)S(1)}, u32[]{:S(2)}, u32[]{:S(2)}) collective-permute-start(bf16[80,1024]{1,0:T(8,128)(2,1)S(1)} %get-tuple-element.21.own_ref), channel_id=1, source_target_pairs={{0,480},{32,0},{64,32},{96,64},{128,96},{160,128},{192,160},{224,1... | collective-permute-start | bytes 491528 | tf_op jit(solution)/shard_map/ppermute | solution.py:81
  25.5 4.4 %collective-permute-start.2 = (bf16[32,128]{1,0:T(8,128)(2,1)S(1)}, bf16[32,128]{1,0:T(8,128)(2,1)S(1)}, u32[]{:S(2)}, u32[]{:S(2)}) collective-permute-start(bf16[32,128]{1,0:T(8,128)(2,1)S(1)} %shard_map.107.own_coef_ref), channel_id=1, source_target_pairs={{0,32},{32,64},{64,96},{96,128},{128,160},{160,192},{192,224},{224... | collective-permute-start | bytes 24584 | tf_op jit(solution)/shard_map/ppermute | solution.py:81
  28.8 3.1 %collective-permute-start.3 = (bf16[32,128]{1,0:T(8,128)(2,1)S(1)}, bf16[32,128]{1,0:T(8,128)(2,1)S(1)}, u32[]{:S(2)}, u32[]{:S(2)}) collective-permute-start(bf16[32,128]{1,0:T(8,128)(2,1)S(1)} %shard_map.107.own_coef_ref), channel_id=1, source_target_pairs={{0,480},{32,0},{64,32},{96,64},{128,96},{160,128},{192,160},{224,1... | collective-permute-start | bytes 24584 | tf_op jit(solution)/shard_map/ppermute | solution.py:81
  29.9 16.6 %copy-start = (f32[8,1024]{1,0:T(8,128)S(1)}, f32[8,1024]{1,0:T(8,128)}, u32[]{:S(2)}) copy-start(f32[8,1024]{1,0:T(8,128)} %refs_2_.1) | copy-start | bytes 98308
  29.9 16.6 %copy-start.1 = (bf16[4,32,256]{2,1,0:T(8,128)(2,1)S(1)}, bf16[4,32,256]{2,1,0:T(8,128)(2,1)}, u32[]{:S(2)}) copy-start(bf16[4,32,256]{2,1,0:T(8,128)(2,1)} %param.11) | copy-start | bytes 196612

commit v11 on v6

--- a/solution.py
+++ b/solution.py
@@ -244,17 +244,20 @@
         for part in halves(sums[k * slots : k * slots + slots]):
             total = total + mm(owner_ref[k], part)
     row = iota((8, 128), 0)
+    far_high = total.astype(BF16).astype(F32)
+    far_low = total - far_high
     for d in range(DEVS):
         near = near_ref[d * 8 : d * 8 + 8, :]
-        low = jnp.where(row == 7, total[d : d + 1, :], near - near.astype(BF16).astype(F32))
+        low = jnp.where(row == 6, far_high[d : d + 1, :], near - near.astype(BF16).astype(F32))
+        low = jnp.where(row == 7, far_low[d : d + 1, :], low)
         out_ref[d] = jnp.concatenate([near, low], axis=0).astype(BF16)
 
 
 def product_body(pieces_ref, bases_ref, krylov_ref, gram_ref, product_ref, copies_ref):
     total = jnp.sum(pieces_ref[...].astype(F32), axis=0)
     row, lane = iota((8, 128), 0), iota((8, 128), 1)
-    near = total[0:8, :] + jnp.where(row == 7, 0.0, total[8:16, :])
-    coef = total[15:16, :].astype(BF16).astype(F32)
+    near = total[0:8, :] + jnp.where(row < 6, total[8:16, :], 0.0)
+    coef = (total[14:15, :] + total[15:16, :]).astype(BF16).astype(F32)
     spread = jnp.where((lane >> 5) == (row >> 1), coef, 0.0).astype(BF16)
     low = mm(spread, bases_ref[:, :128])
     high = mm(spread, bases_ref[:, 128:])

time: 74 us -> 74 us (level)
  no operation moved by 1% of the time
where the time goes in v11:
time: 74 us; the launch traced here: 73.6 us
  blocking collectives  39.8 us (54%)
  starting transfers between devices  19.1 us (26%)
  waiting for transfers between devices  7.45 us (10%)
  Pallas kernels  6.52 us (9%)
    all_to_all x3, blocking collectives, to_all(): return lax.all_to_all(value, axis, split_axis=0, concat_axis=0, tiled=True)  39.8 us
    all_to_all x1, starting transfers between devices, to_all(): return lax.all_to_all(value, axis, split_axis=0, concat_axis=0, tiled=True)  13.7 us
    pallas_call x8, Pallas kernels, run(): kernel(*(pltpu.with_memory_space_constraint(arg, pltpu.HBM) if spec is HB...  6.52 us
    all_to_all x1, waiting for transfers between devices, to_all(): return lax.all_to_all(value, axis, split_axis=0, concat_axis=0, tiled=True)  5.55 us
    ppermute x4, starting transfers between devices, group_shift(): lax.ppermute(value, 'group', [(g, (g + step) % GROUPS) for g in range(GRO...  5.4 us
    ppermute x4, waiting for transfers between devices, group_shift(): lax.ppermute(value, 'group', [(g, (g + step) % GROUPS) for g in range(GRO...  1.9 us
  transfers between devices with their start and end apart: 5, of which 2 were waited for; matrix products, arithmetic and copies ran while one was open for 0% of the time, Pallas kernels for 4%

profile of v11, /device:TPU:1, one launch (start us, length us, event | category | flops | bytes accessed | tf_op | source)
XLA Modules:
  0.0 73.6 jit_solution(2431357574046174794)
XLA Ops:
  0.6 1.7 %shard_map.104 = bf16[32,16,128]{2,1,0:T(8,128)(2,1)} custom-call(f32[8,128]{1,0:T(8,128)} %bitcast.13, bf16[128,256]{1,0:T(8,128)(2,1)} %bitcast.11), custom_call_target="tpu_custom_call" | custom-call | tf_op jit(solution)/shard_map/pallas_call | solution.py:29
  2.3 13.7 %all-to-all-start = ((bf16[32,16,128]{2,1,0:T(8,128)(2,1)}), bf16[32,16,128]{2,1,0:T(8,128)(2,1)S(1)}, u32[]{:S(2)}, u32[]{:S(2)}) async-start(bf16[32,16,128]{2,1,0:T(8,128)(2,1)} %shard_map.104), calls=%async_computation | async-start | bytes 262144 | tf_op jit(solution)/shard_map/all_to_all | solution.py:77
  16.1 1.6 %shard_map.105 = (bf16[80,1024]{1,0:T(8,128)(2,1)S(1)}, bf16[12,256,256]{2,1,0:T(8,128)(2,1)S(1)}, bf16[64,512]{1,0:T(8,128)(2,1)S(1)}, bf16[256,128]{1,0:T(8,128)(2,1)S(1)}, f32[1,128]{1,0:T(1,128)S(1)}) custom-call(bf16[12,256,256]{2,1,0:T(8,128)(2,1)} %tiles_hbm.1, bf16[64,1024]{1,0:T(8,128)(2,1)} %blocks_hbm.1, s32[2,64]{1,0:T(2,128)} %bitcast.14, ...), custom_call_target="tpu_custom_call" | custom-call | tf_op jit(solution)/shard_map/pallas_call | solution.py:29
  17.7 2.1 %collective-permute-start = (bf16[80,1024]{1,0:T(8,128)(2,1)S(1)}, bf16[80,1024]{1,0:T(8,128)(2,1)S(1)}, u32[]{:S(2)}, u32[]{:S(2)}) collective-permute-start(bf16[80,1024]{1,0:T(8,128)(2,1)S(1)} %get-tuple-element.21.own_ref), channel_id=1, source_target_pairs={{0,32},{32,64},{64,96},{96,128},{128,160},{160,192},{192,224},{224... | collective-permute-start | bytes 491528 | tf_op jit(solution)/shard_map/ppermute | solution.py:81
  19.8 0.0 collective-permute-start.1
  19.9 5.5 %all-to-all-done = bf16[32,16,128]{2,1,0:T(8,128)(2,1)S(1)} async-done(((bf16[32,16,128]{2,1,0:T(8,128)(2,1)}), bf16[32,16,128]{2,1,0:T(8,128)(2,1)S(1)}, u32[]{:S(2)}, u32[]{:S(2)}) %all-to-all-start) | async-done | bytes 131104 | tf_op jit(solution)/shard_map/all_to_all | solution.py:77
  25.4 0.1 shard_map.107.own_coef_ref
  25.5 3.2 %collective-permute-start.2 = (bf16[32,128]{1,0:T(8,128)(2,1)S(1)}, bf16[32,128]{1,0:T(8,128)(2,1)S(1)}, u32[]{:S(2)}, u32[]{:S(2)}) collective-permute-start(bf16[32,128]{1,0:T(8,128)(2,1)S(1)} %shard_map.107.own_coef_ref), channel_id=1, source_target_pairs={{0,32},{32,64},{64,96},{96,128},{128,160},{160,192},{192,224},{224... | collective-permute-start | bytes 24584 | tf_op jit(solution)/shard_map/ppermute | solution.py:81
  28.8 0.0 collective-permute-start.3
  28.8 0.0 collective-permute-done.before_ref
  28.8 0.0 collective-permute-done.1.after_ref
  28.8 0.0 copy-start
  28.8 0.0 copy-start.1
  28.8 1.1 %shard_map.106 = (f32[256,128]{1,0:T(8,128)S(1)}, bf16[256,96]{1,0:T(8,128)(2,1)S(1)}, f32[256,128]{1,0:T(8,128)S(1)}, f32[256,128]{1,0:T(8,128)S(1)}, bf16[4,32...) custom-call(bf16[512,128]{1,0:T(8,128)(2,1)S(1)} %bitcast.10, ...), custom_call_target="tpu_custom_call" | custom-call | tf_op jit(solution)/shard_map/pallas_call | solution.py:29
  30.0 0.0 collective-permute-done.2.before_coef_ref
  30.0 1.9 %collective-permute-done.3.after_coef_ref = bf16[32,128]{1,0:T(8,128)(2,1)S(1)} collective-permute-done((bf16[32,128]{1,0:T(8,128)(2,1)S(1)}, bf16[32,128]{1,0:T(8,128)(2,1)S(1)}, u32[]{:S(2)}, u32[]{:S(2)}) %collective-permute-start.3) | collective-permute-done | bytes 8224 | tf_op jit(solution)/shard_map/ppermute | solution.py:81
  31.9 0.8 %shard_map.108 = bf16[32,16,128]{2,1,0:T(8,128)(2,1)S(1)} custom-call(f32[256,128]{1,0:T(8,128)S(1)} %get-tuple-element.22.near_ref, bf16[80,1024]{1,0:T(8,128)(2,1)S(1)} %get-tuple-element.21.own_ref, bf16[80,1024]{1,0:T(8,128)(2,1)S(1)} %collective-permute-done.before_ref, bf16[80,1024]{1,0:T(8,128)(2,1)S(1)} %collective-permute-done.1.after_ref, ...), custom_call_target="tpu_custom_call" | custom-call | tf_op jit(solution)/shard_map/pallas_call | solution.py:29
  32.7 12.5 %all_to_all.20.pieces_ref = bf16[32,16,128]{2,1,0:T(8,128)(2,1)S(1)} all-to-all(bf16[32,16,128]{2,1,0:T(8,128)(2,1)S(1)} %shard_map.108), channel_id=1, replica_groups=mesh['group'=16,'dev'=32] {'dev'}, dimensions={0} | all-to-all | bytes 262144 | tf_op jit(solution)/shard_map/all_to_all | solution.py:77
  45.2 0.0 copy-done
  45.2 0.0 copy-done.1
  45.2 0.3 shard_map.109
  45.5 15.7 %all_to_all.21.pieces_ref = f32[16,1,128]{2,1,0:T(1,128)S(1)} all-to-all(f32[16,1,128]{2,1,0:T(1,128)S(1)} %get-tuple-element.30), channel_id=1, replica_groups=mesh['group'=16,'dev'=32] {'group'}, dimensions={0} | all-to-all | bytes 16384 | tf_op jit(solution)/shard_map/all_to_all | solution.py:77
  61.3 11.5 %all_to_all.22.refs_0_ = f32[32,1,128]{2,1,0:T(1,128)S(1)} all-to-all(f32[32,1,128]{2,1,0:T(1,128)S(1)} %shard_map.110), channel_id=1, replica_groups=mesh['group'=16,'dev'=32] {'dev'}, dimensions={0} | all-to-all | bytes 32768 | tf_op jit(solution)/shard_map/all_to_all | solution.py:77
  72.8 0.8 %shard_map.111 = (f32[8,128]{1,0:T(8,128)}, f32[1,8]{1,0:T(1,128)}) custom-call(f32[32,1,128]{2,1,0:T(1,128)S(1)} %all_to_all.22.refs_0_, f32[8,128]{1,0:T(8,128)S(1)} %get-tuple-element.31.refs_1_, f32[8,1024]{1,0:T(8,128)S(1)} %copy-done), custom_call_target="tpu_custom_call" | custom-call | tf_op jit(solution)/shard_map/pallas_call | solution.py:29
  (1 shorter events, 0.0 us)
Async XLA Ops:
  2.3 23.1 %all-to-all-start = ((bf16[32,16,128]{2,1,0:T(8,128)(2,1)}), bf16[32,16,128]{2,1,0:T(8,128)(2,1)S(1)}, u32[]{:S(2)}, u32[]{:S(2)}) async-start(bf16[32,16,128]{2,1,0:T(8,128)(2,1)} %shard_map.104), calls=%async_computation | async-start | bytes 262144 | tf_op jit(solution)/shard_map/all_to_all | solution.py:77
  17.7 11.1 %collective-permute-start = (bf16[80,1024]{1,0:T(8,128)(2,1)S(1)}, bf16[80,1024]{1,0:T(8,128)(2,1)S(1)}, u32[]{:S(2)}, u32[]{:S(2)}) collective-permute-start(bf16[80,1024]{1,0:T(8,128)(2,1)S(1)} %get-tuple-element.21.own_ref), channel_id=1, source_target_pairs={{0,32},{32,64},{64,96},{96,128},{128,160},{160,192},{192,224},{224... | collective-permute-start | bytes 491528 | tf_op jit(solution)/shard_map/ppermute | solution.py:81
  19.8 8.9 %collective-permute-start.1 = (bf16[80,1024]{1,0:T(8,128)(2,1)S(1)}, bf16[80,1024]{1,0:T(8,128)(2,1)S(1)}, u32[]{:S(2)}, u32[]{:S(2)}) collective-permute-start(bf16[80,1024]{1,0:T(8,128)(2,1)S(1)} %get-tuple-element.21.own_ref), channel_id=1, source_target_pairs={{0,480},{32,0},{64,32},{96,64},{128,96},{160,128},{192,160},{224,1... | collective-permute-start | bytes 491528 | tf_op jit(solution)/shard_map/ppermute | solution.py:81
  25.5 4.4 %collective-permute-start.2 = (bf16[32,128]{1,0:T(8,128)(2,1)S(1)}, bf16[32,128]{1,0:T(8,128)(2,1)S(1)}, u32[]{:S(2)}, u32[]{:S(2)}) collective-permute-start(bf16[32,128]{1,0:T(8,128)(2,1)S(1)} %shard_map.107.own_coef_ref), channel_id=1, source_target_pairs={{0,32},{32,64},{64,96},{96,128},{128,160},{160,192},{192,224},{224... | collective-permute-start | bytes 24584 | tf_op jit(solution)/shard_map/ppermute | solution.py:81
  28.8 3.1 %collective-permute-start.3 = (bf16[32,128]{1,0:T(8,128)(2,1)S(1)}, bf16[32,128]{1,0:T(8,128)(2,1)S(1)}, u32[]{:S(2)}, u32[]{:S(2)}) collective-permute-start(bf16[32,128]{1,0:T(8,128)(2,1)S(1)} %shard_map.107.own_coef_ref), channel_id=1, source_target_pairs={{0,480},{32,0},{64,32},{96,64},{128,96},{160,128},{192,160},{224,1... | collective-permute-start | bytes 24584 | tf_op jit(solution)/shard_map/ppermute | solution.py:81
  28.8 16.4 %copy-start = (f32[8,1024]{1,0:T(8,128)S(1)}, f32[8,1024]{1,0:T(8,128)}, u32[]{:S(2)}) copy-start(f32[8,1024]{1,0:T(8,128)} %refs_2_.1) | copy-start | bytes 98308
  28.8 16.4 %copy-start.1 = (bf16[4,32,256]{2,1,0:T(8,128)(2,1)S(1)}, bf16[4,32,256]{2,1,0:T(8,128)(2,1)}, u32[]{:S(2)}) copy-start(bf16[4,32,256]{2,1,0:T(8,128)(2,1)} %param.11) | copy-start | bytes 196612

commit v12 on v11

--- a/solution.py
+++ b/solution.py
@@ -166,9 +166,15 @@
 
 
 def coeffs_body(gathered_ref, out_ref):
-    rows = iota((DEVS, DEVS * 16), 0) * 16 + 8
-    pick = one_hot(iota((DEVS, DEVS * 16), 1) == rows)
-    out_ref[...] = mm(pick, gathered_ref[...]).astype(BF16)
+    parts = []
+    for k in range(DEVS // 8):
+        total = jnp.zeros((8, 128), F32)
+        for r in range(8):
+            at = (k * 8 + r) * 16
+            tail = gathered_ref[at : at + 16, :].astype(F32)[8:16, :]
+            total = total + (pltpu.roll(tail, r, 0) if r else tail)
+        parts.append(total)
+    out_ref[...] = jnp.concatenate(parts, axis=0).astype(BF16)
 
 
 def near_body(gathered_ref, gather_ref, scatter_ref, tiles_ref, own_ref, before_ref, after_ref,

time: 74 us -> 73.9 us (level)
  no operation moved by 1% of the time
where the time goes in v12:
time: 73.9 us; the launch traced here: 73.5 us
  blocking collectives  39.8 us (54%)
  starting transfers between devices  19.1 us (26%)
  waiting for transfers between devices  7.45 us (10%)
  Pallas kernels  6.4 us (9%)
    all_to_all x3, blocking collectives, to_all(): return lax.all_to_all(value, axis, split_axis=0, concat_axis=0, tiled=True)  39.8 us
    all_to_all x1, starting transfers between devices, to_all(): return lax.all_to_all(value, axis, split_axis=0, concat_axis=0, tiled=True)  13.7 us
    pallas_call x8, Pallas kernels, run(): kernel(*(pltpu.with_memory_space_constraint(arg, pltpu.HBM) if spec is HB...  6.4 us
    all_to_all x1, waiting for transfers between devices, to_all(): return lax.all_to_all(value, axis, split_axis=0, concat_axis=0, tiled=True)  5.55 us
    ppermute x4, starting transfers between devices, group_shift(): lax.ppermute(value, 'group', [(g, (g + step) % GROUPS) for g in range(GRO...  5.41 us
    ppermute x4, waiting for transfers between devices, group_shift(): lax.ppermute(value, 'group', [(g, (g + step) % GROUPS) for g in range(GRO...  1.9 us
  transfers between devices with their start and end apart: 5, of which 2 were waited for; matrix products, arithmetic and copies ran while one was open for 0% of the time, Pallas kernels for 4%

profile of v12, /device:TPU:1, one launch (start us, length us, event | category | flops | bytes accessed | tf_op | source)
XLA Modules:
  0.0 73.5 jit_solution(46262665427406368)
XLA Ops:
  0.6 1.7 %shard_map.104 = bf16[32,16,128]{2,1,0:T(8,128)(2,1)} custom-call(f32[8,128]{1,0:T(8,128)} %bitcast.13, bf16[128,256]{1,0:T(8,128)(2,1)} %bitcast.11), custom_call_target="tpu_custom_call" | custom-call | tf_op jit(solution)/shard_map/pallas_call | solution.py:29
  2.3 13.7 %all-to-all-start = ((bf16[32,16,128]{2,1,0:T(8,128)(2,1)}), bf16[32,16,128]{2,1,0:T(8,128)(2,1)S(1)}, u32[]{:S(2)}, u32[]{:S(2)}) async-start(bf16[32,16,128]{2,1,0:T(8,128)(2,1)} %shard_map.104), calls=%async_computation | async-start | bytes 262144 | tf_op jit(solution)/shard_map/all_to_all | solution.py:77
  16.1 1.6 %shard_map.105 = (bf16[80,1024]{1,0:T(8,128)(2,1)S(1)}, bf16[12,256,256]{2,1,0:T(8,128)(2,1)S(1)}, bf16[64,512]{1,0:T(8,128)(2,1)S(1)}, bf16[256,128]{1,0:T(8,128)(2,1)S(1)}, f32[1,128]{1,0:T(1,128)S(1)}) custom-call(bf16[12,256,256]{2,1,0:T(8,128)(2,1)} %tiles_hbm.1, bf16[64,1024]{1,0:T(8,128)(2,1)} %blocks_hbm.1, s32[2,64]{1,0:T(2,128)} %bitcast.14, ...), custom_call_target="tpu_custom_call" | custom-call | tf_op jit(solution)/shard_map/pallas_call | solution.py:29
  17.7 2.1 %collective-permute-start = (bf16[80,1024]{1,0:T(8,128)(2,1)S(1)}, bf16[80,1024]{1,0:T(8,128)(2,1)S(1)}, u32[]{:S(2)}, u32[]{:S(2)}) collective-permute-start(bf16[80,1024]{1,0:T(8,128)(2,1)S(1)} %get-tuple-element.21.own_ref), channel_id=1, source_target_pairs={{0,32},{32,64},{64,96},{96,128},{128,160},{160,192},{192,224},{224... | collective-permute-start | bytes 491528 | tf_op jit(solution)/shard_map/ppermute | solution.py:81
  19.8 0.0 collective-permute-start.1
  19.9 5.5 %all-to-all-done = bf16[32,16,128]{2,1,0:T(8,128)(2,1)S(1)} async-done(((bf16[32,16,128]{2,1,0:T(8,128)(2,1)}), bf16[32,16,128]{2,1,0:T(8,128)(2,1)S(1)}, u32[]{:S(2)}, u32[]{:S(2)}) %all-to-all-start) | async-done | bytes 131104 | tf_op jit(solution)/shard_map/all_to_all | solution.py:77
  25.4 3.3 %collective-permute-start.2 = (bf16[32,128]{1,0:T(8,128)(2,1)S(1)}, bf16[32,128]{1,0:T(8,128)(2,1)S(1)}, u32[]{:S(2)}, u32[]{:S(2)}) collective-permute-start(bf16[32,128]{1,0:T(8,128)(2,1)S(1)} %shard_map.107.own_coef_ref), channel_id=1, source_target_pairs={{0,32},{32,64},{64,96},{96,128},{128,160},{160,192},{192,224},{224... | collective-permute-start | bytes 24584 | tf_op jit(solution)/shard_map/ppermute | solution.py:81
  28.7 0.0 collective-permute-start.3
  28.7 0.0 collective-permute-done.before_ref
  28.7 0.0 collective-permute-done.1.after_ref
  28.7 0.0 copy-start
  28.7 0.0 copy-start.1
  28.7 1.1 %shard_map.106 = (f32[256,128]{1,0:T(8,128)S(1)}, bf16[256,96]{1,0:T(8,128)(2,1)S(1)}, f32[256,128]{1,0:T(8,128)S(1)}, f32[256,128]{1,0:T(8,128)S(1)}, bf16[4,32...) custom-call(bf16[512,128]{1,0:T(8,128)(2,1)S(1)} %bitcast.10, ...), custom_call_target="tpu_custom_call" | custom-call | tf_op jit(solution)/shard_map/pallas_call | solution.py:29
  29.8 0.0 collective-permute-done.2.before_coef_ref
  29.9 1.9 %collective-permute-done.3.after_coef_ref = bf16[32,128]{1,0:T(8,128)(2,1)S(1)} collective-permute-done((bf16[32,128]{1,0:T(8,128)(2,1)S(1)}, bf16[32,128]{1,0:T(8,128)(2,1)S(1)}, u32[]{:S(2)}, u32[]{:S(2)}) %collective-permute-start.3) | collective-permute-done | bytes 8224 | tf_op jit(solution)/shard_map/ppermute | solution.py:81
  31.8 0.8 %shard_map.108 = bf16[32,16,128]{2,1,0:T(8,128)(2,1)S(1)} custom-call(f32[256,128]{1,0:T(8,128)S(1)} %get-tuple-element.22.near_ref, bf16[80,1024]{1,0:T(8,128)(2,1)S(1)} %get-tuple-element.21.own_ref, bf16[80,1024]{1,0:T(8,128)(2,1)S(1)} %collective-permute-done.before_ref, bf16[80,1024]{1,0:T(8,128)(2,1)S(1)} %collective-permute-done.1.after_ref, ...), custom_call_target="tpu_custom_call" | custom-call | tf_op jit(solution)/shard_map/pallas_call | solution.py:29
  32.6 12.7 %all_to_all.20.pieces_ref = bf16[32,16,128]{2,1,0:T(8,128)(2,1)S(1)} all-to-all(bf16[32,16,128]{2,1,0:T(8,128)(2,1)S(1)} %shard_map.108), channel_id=1, replica_groups=mesh['group'=16,'dev'=32] {'dev'}, dimensions={0} | all-to-all | bytes 262144 | tf_op jit(solution)/shard_map/all_to_all | solution.py:77
  45.3 0.0 copy-done
  45.3 0.0 copy-done.1
  45.3 0.3 shard_map.109
  45.6 15.5 %all_to_all.21.pieces_ref = f32[16,1,128]{2,1,0:T(1,128)S(1)} all-to-all(f32[16,1,128]{2,1,0:T(1,128)S(1)} %get-tuple-element.30), channel_id=1, replica_groups=mesh['group'=16,'dev'=32] {'group'}, dimensions={0} | all-to-all | bytes 16384 | tf_op jit(solution)/shard_map/all_to_all | solution.py:77
  61.2 11.5 %all_to_all.22.refs_0_ = f32[32,1,128]{2,1,0:T(1,128)S(1)} all-to-all(f32[32,1,128]{2,1,0:T(1,128)S(1)} %shard_map.110), channel_id=1, replica_groups=mesh['group'=16,'dev'=32] {'dev'}, dimensions={0} | all-to-all | bytes 32768 | tf_op jit(solution)/shard_map/all_to_all | solution.py:77
  72.7 0.8 %shard_map.111 = (f32[8,128]{1,0:T(8,128)}, f32[1,8]{1,0:T(1,128)}) custom-call(f32[32,1,128]{2,1,0:T(1,128)S(1)} %all_to_all.22.refs_0_, f32[8,128]{1,0:T(8,128)S(1)} %get-tuple-element.31.refs_1_, f32[8,1024]{1,0:T(8,128)S(1)} %copy-done), custom_call_target="tpu_custom_call" | custom-call | tf_op jit(solution)/shard_map/pallas_call | solution.py:29
  (2 shorter events, 0.0 us)
Async XLA Ops:
  2.3 23.1 %all-to-all-start = ((bf16[32,16,128]{2,1,0:T(8,128)(2,1)}), bf16[32,16,128]{2,1,0:T(8,128)(2,1)S(1)}, u32[]{:S(2)}, u32[]{:S(2)}) async-start(bf16[32,16,128]{2,1,0:T(8,128)(2,1)} %shard_map.104), calls=%async_computation | async-start | bytes 262144 | tf_op jit(solution)/shard_map/all_to_all | solution.py:77
  17.7 11.0 %collective-permute-start = (bf16[80,1024]{1,0:T(8,128)(2,1)S(1)}, bf16[80,1024]{1,0:T(8,128)(2,1)S(1)}, u32[]{:S(2)}, u32[]{:S(2)}) collective-permute-start(bf16[80,1024]{1,0:T(8,128)(2,1)S(1)} %get-tuple-element.21.own_ref), channel_id=1, source_target_pairs={{0,32},{32,64},{64,96},{96,128},{128,160},{160,192},{192,224},{224... | collective-permute-start | bytes 491528 | tf_op jit(solution)/shard_map/ppermute | solution.py:81
  19.8 8.8 %collective-permute-start.1 = (bf16[80,1024]{1,0:T(8,128)(2,1)S(1)}, bf16[80,1024]{1,0:T(8,128)(2,1)S(1)}, u32[]{:S(2)}, u32[]{:S(2)}) collective-permute-start(bf16[80,1024]{1,0:T(8,128)(2,1)S(1)} %get-tuple-element.21.own_ref), channel_id=1, source_target_pairs={{0,480},{32,0},{64,32},{96,64},{128,96},{160,128},{192,160},{224,1... | collective-permute-start | bytes 491528 | tf_op jit(solution)/shard_map/ppermute | solution.py:81
  25.4 4.4 %collective-permute-start.2 = (bf16[32,128]{1,0:T(8,128)(2,1)S(1)}, bf16[32,128]{1,0:T(8,128)(2,1)S(1)}, u32[]{:S(2)}, u32[]{:S(2)}) collective-permute-start(bf16[32,128]{1,0:T(8,128)(2,1)S(1)} %shard_map.107.own_coef_ref), channel_id=1, source_target_pairs={{0,32},{32,64},{64,96},{96,128},{128,160},{160,192},{192,224},{224... | collective-permute-start | bytes 24584 | tf_op jit(solution)/shard_map/ppermute | solution.py:81
  28.7 3.1 %collective-permute-start.3 = (bf16[32,128]{1,0:T(8,128)(2,1)S(1)}, bf16[32,128]{1,0:T(8,128)(2,1)S(1)}, u32[]{:S(2)}, u32[]{:S(2)}) collective-permute-start(bf16[32,128]{1,0:T(8,128)(2,1)S(1)} %shard_map.107.own_coef_ref), channel_id=1, source_target_pairs={{0,480},{32,0},{64,32},{96,64},{128,96},{160,128},{192,160},{224,1... | collective-permute-start | bytes 24584 | tf_op jit(solution)/shard_map/ppermute | solution.py:81
  28.7 16.7 %copy-start = (f32[8,1024]{1,0:T(8,128)S(1)}, f32[8,1024]{1,0:T(8,128)}, u32[]{:S(2)}) copy-start(f32[8,1024]{1,0:T(8,128)} %refs_2_.1) | copy-start | bytes 98308
  28.7 16.6 %copy-start.1 = (bf16[4,32,256]{2,1,0:T(8,128)(2,1)S(1)}, bf16[4,32,256]{2,1,0:T(8,128)(2,1)}, u32[]{:S(2)}) copy-start(bf16[4,32,256]{2,1,0:T(8,128)(2,1)} %param.11) | copy-start | bytes 196612

commit v13 on v12

--- a/solution.py
+++ b/solution.py
@@ -234,21 +234,23 @@
     right, left = taken[0:slots], taken[slots:]
     sub, lane = iota((128, 128), 0), iota((128, 128), 1)
     tiled = mm(right, one_hot((sub & 31) == (lane & 31)))
-    forward = jnp.zeros((slots, 128), F32)
+    forward = jnp.zeros((2 * slots, 128), F32)
     backward = jnp.zeros(left.shape, F32)
     for k in range(8):
         parts = [b[0:slots, k * 128 : k * 128 + 128] for b in bundles]
         part = jnp.concatenate(parts, axis=0).astype(F32)
         backward = backward + part * mm(left, take_ref[k])
-        for piece in halves(part[0:slots] * tiled):
-            forward = forward + mm(piece, give_ref[k])
+        split = jnp.concatenate(halves(part[0:slots] * tiled), axis=0)
+        forward = forward + mm(split, give_ref[k])
     backward = backward + pltpu.roll(backward, 64, 1)
     backward = backward + pltpu.roll(backward, 32, 1)
+    forward = forward[0:slots] + forward[slots:]
     sums = jnp.concatenate([forward, backward], axis=0) * keep_ref[...]
-    total = jnp.zeros((DEVS, 128), F32)
+    split = jnp.concatenate(halves(sums), axis=1)
+    total = jnp.zeros((DEVS, 256), F32)
     for k in range(4):
-        for part in halves(sums[k * slots : k * slots + slots]):
-            total = total + mm(owner_ref[k], part)
+        total = total + mm(owner_ref[k], split[k * slots : k * slots + slots])
+    total = total[:, 0:128] + total[:, 128:256]
     row = iota((8, 128), 0)
     far_high = total.astype(BF16).astype(F32)
     far_low = total - far_high

time: 73.9 us -> 73.8 us (level)
  no operation moved by 1% of the time
where the time goes in v13:
time: 73.8 us; the launch traced here: 73.5 us
  blocking collectives  39.8 us (54%)
  starting transfers between devices  19.1 us (26%)
  waiting for transfers between devices  7.45 us (10%)
  Pallas kernels  6.36 us (9%)
    all_to_all x3, blocking collectives, to_all(): return lax.all_to_all(value, axis, split_axis=0, concat_axis=0, tiled=True)  39.8 us
    all_to_all x1, starting transfers between devices, to_all(): return lax.all_to_all(value, axis, split_axis=0, concat_axis=0, tiled=True)  13.7 us
    pallas_call x8, Pallas kernels, run(): kernel(*(pltpu.with_memory_space_constraint(arg, pltpu.HBM) if spec is HB...  6.36 us
    all_to_all x1, waiting for transfers between devices, to_all(): return lax.all_to_all(value, axis, split_axis=0, concat_axis=0, tiled=True)  5.55 us
    ppermute x4, starting transfers between devices, group_shift(): lax.ppermute(value, 'group', [(g, (g + step) % GROUPS) for g in range(GRO...  5.41 us
    ppermute x4, waiting for transfers between devices, group_shift(): lax.ppermute(value, 'group', [(g, (g + step) % GROUPS) for g in range(GRO...  1.9 us
  transfers between devices with their start and end apart: 5, of which 2 were waited for; matrix products, arithmetic and copies ran while one was open for 0% of the time, Pallas kernels for 4%

profile of v13, /device:TPU:1, one launch (start us, length us, event | category | flops | bytes accessed | tf_op | source)
XLA Modules:
  0.0 73.5 jit_solution(404560467137144043)
XLA Ops:
  0.6 1.7 %shard_map.104 = bf16[32,16,128]{2,1,0:T(8,128)(2,1)} custom-call(f32[8,128]{1,0:T(8,128)} %bitcast.13, bf16[128,256]{1,0:T(8,128)(2,1)} %bitcast.11), custom_call_target="tpu_custom_call" | custom-call | tf_op jit(solution)/shard_map/pallas_call | solution.py:29
  2.3 13.7 %all-to-all-start = ((bf16[32,16,128]{2,1,0:T(8,128)(2,1)}), bf16[32,16,128]{2,1,0:T(8,128)(2,1)S(1)}, u32[]{:S(2)}, u32[]{:S(2)}) async-start(bf16[32,16,128]{2,1,0:T(8,128)(2,1)} %shard_map.104), calls=%async_computation | async-start | bytes 262144 | tf_op jit(solution)/shard_map/all_to_all | solution.py:77
  16.1 1.6 %shard_map.105 = (bf16[80,1024]{1,0:T(8,128)(2,1)S(1)}, bf16[12,256,256]{2,1,0:T(8,128)(2,1)S(1)}, bf16[64,512]{1,0:T(8,128)(2,1)S(1)}, bf16[256,128]{1,0:T(8,128)(2,1)S(1)}, f32[1,128]{1,0:T(1,128)S(1)}) custom-call(bf16[12,256,256]{2,1,0:T(8,128)(2,1)} %tiles_hbm.1, bf16[64,1024]{1,0:T(8,128)(2,1)} %blocks_hbm.1, s32[2,64]{1,0:T(2,128)} %bitcast.14, ...), custom_call_target="tpu_custom_call" | custom-call | tf_op jit(solution)/shard_map/pallas_call | solution.py:29
  17.7 2.1 %collective-permute-start = (bf16[80,1024]{1,0:T(8,128)(2,1)S(1)}, bf16[80,1024]{1,0:T(8,128)(2,1)S(1)}, u32[]{:S(2)}, u32[]{:S(2)}) collective-permute-start(bf16[80,1024]{1,0:T(8,128)(2,1)S(1)} %get-tuple-element.21.own_ref), channel_id=1, source_target_pairs={{0,32},{32,64},{64,96},{96,128},{128,160},{160,192},{192,224},{224... | collective-permute-start | bytes 491528 | tf_op jit(solution)/shard_map/ppermute | solution.py:81
  19.8 0.0 collective-permute-start.1
  19.9 5.5 %all-to-all-done = bf16[32,16,128]{2,1,0:T(8,128)(2,1)S(1)} async-done(((bf16[32,16,128]{2,1,0:T(8,128)(2,1)}), bf16[32,16,128]{2,1,0:T(8,128)(2,1)S(1)}, u32[]{:S(2)}, u32[]{:S(2)}) %all-to-all-start) | async-done | bytes 131104 | tf_op jit(solution)/shard_map/all_to_all | solution.py:77
  25.4 3.3 %collective-permute-start.2 = (bf16[32,128]{1,0:T(8,128)(2,1)S(1)}, bf16[32,128]{1,0:T(8,128)(2,1)S(1)}, u32[]{:S(2)}, u32[]{:S(2)}) collective-permute-start(bf16[32,128]{1,0:T(8,128)(2,1)S(1)} %shard_map.107.own_coef_ref), channel_id=1, source_target_pairs={{0,32},{32,64},{64,96},{96,128},{128,160},{160,192},{192,224},{224... | collective-permute-start | bytes 24584 | tf_op jit(solution)/shard_map/ppermute | solution.py:81
  28.7 0.0 collective-permute-start.3
  28.7 0.0 collective-permute-done.before_ref
  28.7 0.0 collective-permute-done.1.after_ref
  28.7 0.0 copy-start
  28.7 0.0 copy-start.1
  28.7 1.1 %shard_map.106 = (f32[256,128]{1,0:T(8,128)S(1)}, bf16[256,96]{1,0:T(8,128)(2,1)S(1)}, f32[256,128]{1,0:T(8,128)S(1)}, f32[256,128]{1,0:T(8,128)S(1)}, bf16[4,32...) custom-call(bf16[512,128]{1,0:T(8,128)(2,1)S(1)} %bitcast.10, ...), custom_call_target="tpu_custom_call" | custom-call | tf_op jit(solution)/shard_map/pallas_call | solution.py:29
  29.8 0.0 collective-permute-done.2.before_coef_ref
  29.9 1.9 %collective-permute-done.3.after_coef_ref = bf16[32,128]{1,0:T(8,128)(2,1)S(1)} collective-permute-done((bf16[32,128]{1,0:T(8,128)(2,1)S(1)}, bf16[32,128]{1,0:T(8,128)(2,1)S(1)}, u32[]{:S(2)}, u32[]{:S(2)}) %collective-permute-start.3) | collective-permute-done | bytes 8224 | tf_op jit(solution)/shard_map/ppermute | solution.py:81
  31.8 0.8 %shard_map.108 = bf16[32,16,128]{2,1,0:T(8,128)(2,1)S(1)} custom-call(f32[256,128]{1,0:T(8,128)S(1)} %get-tuple-element.22.near_ref, bf16[80,1024]{1,0:T(8,128)(2,1)S(1)} %get-tuple-element.21.own_ref, bf16[80,1024]{1,0:T(8,128)(2,1)S(1)} %collective-permute-done.before_ref, bf16[80,1024]{1,0:T(8,128)(2,1)S(1)} %collective-permute-done.1.after_ref, ...), custom_call_target="tpu_custom_call" | custom-call | tf_op jit(solution)/shard_map/pallas_call | solution.py:29
  32.6 12.7 %all_to_all.20.pieces_ref = bf16[32,16,128]{2,1,0:T(8,128)(2,1)S(1)} all-to-all(bf16[32,16,128]{2,1,0:T(8,128)(2,1)S(1)} %shard_map.108), channel_id=1, replica_groups=mesh['group'=16,'dev'=32] {'dev'}, dimensions={0} | all-to-all | bytes 262144 | tf_op jit(solution)/shard_map/all_to_all | solution.py:77
  45.3 0.0 copy-done
  45.3 0.0 copy-done.1
  45.3 0.3 shard_map.109
  45.6 15.5 %all_to_all.21.pieces_ref = f32[16,1,128]{2,1,0:T(1,128)S(1)} all-to-all(f32[16,1,128]{2,1,0:T(1,128)S(1)} %get-tuple-element.30), channel_id=1, replica_groups=mesh['group'=16,'dev'=32] {'group'}, dimensions={0} | all-to-all | bytes 16384 | tf_op jit(solution)/shard_map/all_to_all | solution.py:77
  61.1 11.5 %all_to_all.22.refs_0_ = f32[32,1,128]{2,1,0:T(1,128)S(1)} all-to-all(f32[32,1,128]{2,1,0:T(1,128)S(1)} %shard_map.110), channel_id=1, replica_groups=mesh['group'=16,'dev'=32] {'dev'}, dimensions={0} | all-to-all | bytes 32768 | tf_op jit(solution)/shard_map/all_to_all | solution.py:77
  72.7 0.8 %shard_map.111 = (f32[8,128]{1,0:T(8,128)}, f32[1,8]{1,0:T(1,128)}) custom-call(f32[32,1,128]{2,1,0:T(1,128)S(1)} %all_to_all.22.refs_0_, f32[8,128]{1,0:T(8,128)S(1)} %get-tuple-element.31.refs_1_, f32[8,1024]{1,0:T(8,128)S(1)} %copy-done), custom_call_target="tpu_custom_call" | custom-call | tf_op jit(solution)/shard_map/pallas_call | solution.py:29
  (2 shorter events, 0.0 us)
Async XLA Ops:
  2.3 23.1 %all-to-all-start = ((bf16[32,16,128]{2,1,0:T(8,128)(2,1)}), bf16[32,16,128]{2,1,0:T(8,128)(2,1)S(1)}, u32[]{:S(2)}, u32[]{:S(2)}) async-start(bf16[32,16,128]{2,1,0:T(8,128)(2,1)} %shard_map.104), calls=%async_computation | async-start | bytes 262144 | tf_op jit(solution)/shard_map/all_to_all | solution.py:77
  17.7 11.0 %collective-permute-start = (bf16[80,1024]{1,0:T(8,128)(2,1)S(1)}, bf16[80,1024]{1,0:T(8,128)(2,1)S(1)}, u32[]{:S(2)}, u32[]{:S(2)}) collective-permute-start(bf16[80,1024]{1,0:T(8,128)(2,1)S(1)} %get-tuple-element.21.own_ref), channel_id=1, source_target_pairs={{0,32},{32,64},{64,96},{96,128},{128,160},{160,192},{192,224},{224... | collective-permute-start | bytes 491528 | tf_op jit(solution)/shard_map/ppermute | solution.py:81
  19.8 8.8 %collective-permute-start.1 = (bf16[80,1024]{1,0:T(8,128)(2,1)S(1)}, bf16[80,1024]{1,0:T(8,128)(2,1)S(1)}, u32[]{:S(2)}, u32[]{:S(2)}) collective-permute-start(bf16[80,1024]{1,0:T(8,128)(2,1)S(1)} %get-tuple-element.21.own_ref), channel_id=1, source_target_pairs={{0,480},{32,0},{64,32},{96,64},{128,96},{160,128},{192,160},{224,1... | collective-permute-start | bytes 491528 | tf_op jit(solution)/shard_map/ppermute | solution.py:81
  25.4 4.4 %collective-permute-start.2 = (bf16[32,128]{1,0:T(8,128)(2,1)S(1)}, bf16[32,128]{1,0:T(8,128)(2,1)S(1)}, u32[]{:S(2)}, u32[]{:S(2)}) collective-permute-start(bf16[32,128]{1,0:T(8,128)(2,1)S(1)} %shard_map.107.own_coef_ref), channel_id=1, source_target_pairs={{0,32},{32,64},{64,96},{96,128},{128,160},{160,192},{192,224},{224... | collective-permute-start | bytes 24584 | tf_op jit(solution)/shard_map/ppermute | solution.py:81
  28.7 3.1 %collective-permute-start.3 = (bf16[32,128]{1,0:T(8,128)(2,1)S(1)}, bf16[32,128]{1,0:T(8,128)(2,1)S(1)}, u32[]{:S(2)}, u32[]{:S(2)}) collective-permute-start(bf16[32,128]{1,0:T(8,128)(2,1)S(1)} %shard_map.107.own_coef_ref), channel_id=1, source_target_pairs={{0,480},{32,0},{64,32},{96,64},{128,96},{160,128},{192,160},{224,1... | collective-permute-start | bytes 24584 | tf_op jit(solution)/shard_map/ppermute | solution.py:81
  28.7 16.6 %copy-start = (f32[8,1024]{1,0:T(8,128)S(1)}, f32[8,1024]{1,0:T(8,128)}, u32[]{:S(2)}) copy-start(f32[8,1024]{1,0:T(8,128)} %refs_2_.1) | copy-start | bytes 98308
  28.7 16.6 %copy-start.1 = (bf16[4,32,256]{2,1,0:T(8,128)(2,1)S(1)}, bf16[4,32,256]{2,1,0:T(8,128)(2,1)}, u32[]{:S(2)}) copy-start(bf16[4,32,256]{2,1,0:T(8,128)(2,1)} %param.11) | copy-start | bytes 196612
